TPU v7x, 1024 devices: a whole 8x8x8 slice. The times are simulated.
1024 devices in a mesh: row: 16 (over z_lo, y), col: 64 (over x, z_hi, core).
Axes of the slice: x: 8, y: 8, z: 8 (z_hi: 4, z_lo: 2; z = z_hi * 2 + z_lo), core: 2. Of those that a mesh axis runs over, the one named last changes fastest.
Arguments:
- t_pair: float32 [4, 64, 512, 512], P(None, 'row', 'col'), may hold values from -16 to 16
- w_ovov: float32 [512, 512, 1024], P('col', 'row'), may hold values from -0.03125 to 0.03125
Outputs:
- cycle_residual: float32 [512, 4, 16, 512], P('col', None, None, 'row')
All inputs are finite; a program needn't handle non-finite values.
Results may differ from a plain program's by a relative error of at most 0.00007.
Values sent between devices are 32-bit elements; how exact they have to be, the bound alone decides.
No kernel may reach another device: no remote copies, remote signals or barrier semaphores. Data moves between devices by JAX's collectives and lax.ppermute only.
A program may use at most 64 MiB of HBM per device.

v0:
```python
import jax
import jax.numpy as jnp
from jax import lax
from jax.sharding import PartitionSpec as P


def contract(amplitudes, integrals):
    return jnp.einsum(
        "ikca,cbkj->aijb",
        amplitudes,
        integrals,
        preferred_element_type=jnp.float32,
        precision=lax.Precision.HIGHEST,
    )


def shards(t_pair, w_ovov):
    occupied = t_pair.shape[1] * lax.axis_size("row")
    pair_count = w_ovov.shape[2] // occupied
    shaped_w = w_ovov.reshape(w_ovov.shape[0], w_ovov.shape[1], occupied, pair_count)
    gathered = lax.all_gather(t_pair, "row", axis=1, tiled=True)
    partial_terms = contract(gathered, shaped_w)
    return lax.psum_scatter(partial_terms, "col", scatter_dimension=0, tiled=True)


def solution(mesh):
    return jax.shard_map(
        shards,
        mesh=mesh,
        in_specs=(P(None, "row", "col", None), P("col", "row", None)),
        out_specs=P("col", None, None, "row"),
        check_vma=False,
    )
```

profile of v0, /device:TPU:1, one launch (start us, length us, event | category | flops | bytes accessed | tf_op | source)
XLA Modules:
  0.0 371.4 jit_solution(6580045915925362478)
XLA Ops:
  6.5 0.0 all-gather.2.cloned.1.call-start
  6.5 1.7 copy.11
  8.2 0.0 all-gather.2.cloned.1.call-update
  8.2 0.0 reduce-scatter.2.cloned.1.call-start
  8.3 3.6 copy.10
  11.9 9.0 %copy.15 = f32[8,32,64,16,1]{3,0,2,4,1:T(8,128)} copy(f32[8,32,64,16,1]{1,3,2,0,4:T(8,128)} %bitcast.13) | data formatting | bytes 2097152 | tf_op jit(solution)/shard_map/reshape | solution.py:20
  20.8 74.6 %all-gather.2.cloned.1.call-done = f32[4,64,8,512]{3,2,0,1:T(8,128)} async-done(((f32[4,4,8,512]{3,2,0,1:T(8,128)}), f32[4,64,8,512]{3,2,0,1:T(8,128)}) %all-gather.2.cloned.1.call-update) | async-done | bytes 4194320 | tf_op jit(solution)/shard_map/all_gather | solution.py:21
  95.4 19.4 %fusion.2 = f32[512,4,16,32]{0,2,1,3:T(8,128)} fusion(f32[8,32,64,16,1]{3,0,2,4,1:T(8,128)} %copy.15, f32[4,64,8,512]{3,2,0,1:T(8,128)} %all-gather.2.cloned.1.call-done), kind=kOutput, calls=%fused_computation.2 | convolution fusion | flops 6442450944 | bytes 9437184 | tf_op jit(solution)/shard_map/ikca,cbkj->aijb/dot_general | solution.py:8
  114.9 14.5 %copy.14 = f32[512,4,16,32]{3,2,1,0:T(8,128)} copy(f32[512,4,16,32]{0,2,1,3:T(8,128)} %fusion.2) | data formatting | bytes 8388608 | tf_op jit(solution)/shard_map/ikca,cbkj->aijb/transpose | solution.py:8
  129.4 0.0 reduce-scatter.2.cloned.1.call-update
  129.4 235.2 %reduce-scatter.2.cloned.1.call-done = f32[8,4,16,32]{3,2,1,0:T(8,128)} async-done(((f32[512,4,16,32]{3,2,1,0:T(8,128)}), f32[8,4,16,32]{3,2,1,0:T(8,128)}) %reduce-scatter.2.cloned.1.call-update) | async-done | bytes 65552 | tf_op jit(solution)/shard_map/reduce_scatter | solution.py:23
Async XLA Ops:
  6.5 88.9 %all-gather.2.cloned.1.call-start = ((), (), s32[]{:S(2)}) async-start(), calls=%async_computation.1 | async-start | bytes 4456448 | tf_op jit(solution)/shard_map/all_gather | solution.py:21
  8.2 356.3 %reduce-scatter.2.cloned.1.call-start = ((), (), s32[]{:S(2)}) async-start(), calls=%async_computation.2 | async-start | bytes 17039360 | tf_op jit(solution)/shard_map/reduce_scatter | solution.py:23
Sparse Core Ops, SparseCore 0:
  10.0 85.3 all-gather.1
  129.5 235.0 reduce-scatter.1
where the time goes:
time: 375 us; the launch traced here: 371 us
  waiting for transfers between devices  310 us (83%)
  local copies, waits for them, and re-layouts  28.7 us (8%)
  matrix products  19.4 us (5%)
  between operations  13.4 us (4%)
    reduce_scatter x1, waiting for transfers between devices, shards(): lax.psum_scatter(partial_terms, 'col', scatter_dimension=0, tiled=True)  235 us
    all_gather x1, waiting for transfers between devices, shards(): gathered = lax.all_gather(t_pair, 'row', axis=1, tiled=True)  74.6 us
    dot_general x1, matrix products, contract(): jnp.einsum('ikca,cbkj->aijb', amplitudes, integrals, preferred_element_ty...  19.4 us
    transpose x1, local copies, waits for them, and re-layouts, contract(): jnp.einsum('ikca,cbkj->aijb', amplitudes, integrals, preferred_element_ty...  14.5 us
    reshape x1, local copies, waits for them, and re-layouts, shards(): w_ovov.reshape(w_ovov.shape[0], w_ovov.shape[1], occupied, pair_count)  8.95 us
  transfers between devices with their start and end apart: 2, of which 2 were waited for; matrix products, arithmetic and copies ran while one was open for 3% of the time, Pallas kernels for 0%

commit v1 on v0

v1 whole, which is shorter than its diff:
```python
import functools

import jax
import jax.numpy as jnp
import numpy as np
from jax import lax
from jax.experimental import pallas as pl
from jax.experimental.pallas import tpu as pltpu
from jax.sharding import PartitionSpec as P

X, ZH, CORES = 8, 4, 2
ZL, Y = 2, 8
GX = 4
XH = X // GX
MEMBERS = GX * CORES
PEERS = XH * ZH
F32 = jnp.float32
BF16 = jnp.bfloat16


def col_of(x, zh, core):
    return (x * ZH + zh) * CORES + core


def col_perm(move):
    pairs = []
    for x in range(X):
        for zh in range(ZH):
            for core in range(CORES):
                pairs.append((col_of(x, zh, core), col_of(*move(x, zh, core))))
    return pairs


def row_perm(move):
    pairs = []
    for zl in range(ZL):
        for y in range(Y):
            z2, y2 = move(zl, y)
            pairs.append((zl * Y + y, z2 * Y + y2 % Y))
    return pairs


MEMBER_GROUPS = [
    [col_of(xh * GX + xl, zh, core) for xl in range(GX) for core in range(CORES)]
    for xh in range(XH)
    for zh in range(ZH)
]
PEER_GROUPS = [
    [col_of(xh * GX + xl, zh, core) for xh in range(XH) for zh in range(ZH)]
    for xl in range(GX)
    for core in range(CORES)
]


BLOCKS = [((0, 1), 0)]
for _step in range(1, Y // 2):
    BLOCKS += [((0, 1), -_step), ((0, 1), _step)]
BLOCKS += [((0,), Y // 2), ((1,), Y // 2)]


def row_table():
    table = np.zeros((ZL * Y, len(BLOCKS) * ZL), np.int32)
    for zl in range(ZL):
        for y in range(Y):
            for n, (which, shift) in enumerate(BLOCKS):
                for at in range(ZL):
                    z = zl ^ which[min(at, len(which) - 1)]
                    table[zl * Y + y, n * ZL + at] = z * Y + (y + shift) % Y
    return table


def col_table():
    table = np.zeros((X * ZH * CORES, MEMBERS), np.int32)
    for col in range(table.shape[0]):
        x, core = col // (ZH * CORES), col % CORES
        for n in range(MEMBERS):
            source = (x - n % GX) % GX
            table[col, n] = source * CORES + (core if n < GX else 1 - core)
    return table


def split2(v):
    hi = v.astype(BF16)
    return hi, (v - hi.astype(F32)).astype(BF16)


def regroup_kernel(t_ref, out_ref):
    blocks, rows, virt = t_ref.shape[0], t_ref.shape[1], t_ref.shape[2]
    run = virt // (X * ZH * CORES)
    src = lax.broadcasted_iota(jnp.int32, (virt, virt), 0)
    dst = lax.broadcasted_iota(jnp.int32, (virt, virt), 1)
    r = dst % run
    zh = (dst // run) % ZH
    xh = (dst // (run * ZH)) % XH
    core = (dst // (run * ZH * XH)) % CORES
    xl = dst // (run * ZH * XH * CORES)
    want = ((((xh * GX + xl) * ZH + zh) * CORES) + core) * run + r
    onehot = jnp.where(src == want, 1.0, 0.0).astype(BF16)
    width = virt // MEMBERS
    for i in range(blocks):
        v = t_ref[i]
        hi = v.astype(BF16)
        rest = v - hi.astype(F32)
        mid = rest.astype(BF16)
        low = (rest - mid.astype(F32)).astype(BF16)
        parts = jnp.dot(
            jnp.concatenate([hi, mid, low], axis=0), onehot, preferred_element_type=F32
        )
        moved = (parts[:rows] + parts[rows : 2 * rows]) + parts[2 * rows :]
        for m in range(MEMBERS):
            out_ref[m, :, i * width : (i + 1) * width] = moved[:, m * width : (m + 1) * width]


def regroup(t):
    blocks, ks, cs, virt = t.shape
    rows = ks * cs
    return pl.pallas_call(
        regroup_kernel,
        out_shape=jax.ShapeDtypeStruct((MEMBERS, rows, blocks * virt // MEMBERS), F32),
        cost_estimate=pl.CostEstimate(flops=6 * blocks * rows * virt * virt, bytes_accessed=t.size * 8, transcendentals=0),
    )(t.reshape(blocks, rows, virt))


def multiply_kernel(has_acc, blocks, *refs):
    s_ref, t_ref = refs[0], refs[1]
    w_refs = refs[2 : 2 + MEMBERS]
    out_ref = refs[-1]

    @pl.when(pl.program_id(0) == 0)
    def _():
        if has_acc:
            out_ref[...] = refs[2 + MEMBERS][...]
        else:
            out_ref[...] = jnp.zeros_like(out_ref)

    left = jnp.concatenate([t_ref[0, s_ref[len(BLOCKS) * ZL + n]] for n in range(MEMBERS)], axis=0)
    right = jnp.concatenate([w[0] for w in w_refs], axis=0)
    lh, ll = split2(left)
    rh, rl = split2(right)
    dims = (((0,), (0,)), ((), ()))
    total = lax.dot_general(
        jnp.concatenate([lh, lh, ll], axis=0),
        jnp.concatenate([rh, rl, rh], axis=0),
        dims,
        preferred_element_type=F32,
    )
    run = total.shape[0] // (blocks * PEERS)
    total = total.reshape(blocks, PEERS, run, total.shape[1])
    for i in range(blocks):
        out_ref[:, i * run : (i + 1) * run, :] += total[i]


def multiply(scalars, at, t, ws, acc, blocks):
    rows, width = t.shape[2], t.shape[3]
    wide = ws[0].shape[2]
    out_shape = (PEERS, width // PEERS, wide)
    in_specs = [pl.BlockSpec((1, MEMBERS, rows, width), lambda z, s: (z, 0, 0, 0))]
    in_specs += [pl.BlockSpec((1, rows, wide), lambda z, s: (s[at * ZL + z], 0, 0))] * MEMBERS
    args = [scalars, t, *ws]
    whole = pl.BlockSpec(out_shape, lambda z, s: (0, 0, 0))
    aliases = {}
    if acc is not None:
        in_specs.append(whole)
        args.append(acc)
        aliases = {len(args) - 1: 0}
    return pl.pallas_call(
        functools.partial(multiply_kernel, acc is not None, blocks),
        grid_spec=pltpu.PrefetchScalarGridSpec(
            num_scalar_prefetch=1, grid=(t.shape[0],), in_specs=in_specs, out_specs=whole
        ),
        out_shape=jax.ShapeDtypeStruct(out_shape, F32),
        input_output_aliases=aliases,
        cost_estimate=pl.CostEstimate(
            flops=6 * t.shape[0] * MEMBERS * rows * width * wide, bytes_accessed=t.size * 4 + 2 * len(ws) * rows * wide * 4, transcendentals=0
        ),
    )(*args)


def shards(t_pair, w_ovov):
    blocks, ks, cs, virt = t_pair.shape
    rows = ks * cs
    row, col = lax.axis_index("row"), lax.axis_index("col")
    scalars = jnp.concatenate(
        [
            lax.dynamic_index_in_dim(jnp.asarray(row_table()), row, keepdims=False),
            lax.dynamic_index_in_dim(jnp.asarray(col_table()), col, keepdims=False),
        ]
    )

    sent = regroup(t_pair)
    mine = lax.all_to_all(sent, "col", 0, 0, tiled=True, axis_index_groups=MEMBER_GROUPS)

    depth, wb, kj = w_ovov.shape
    occupied = ks * ZL * Y
    pairs = kj // occupied
    own_w = w_ovov.reshape(cs, wb, occupied, pairs).transpose(2, 0, 3, 1).reshape(ZL * Y, rows, pairs * wb)
    swap_core = col_perm(lambda x, zh, c: (x, zh, 1 - c))
    near = [own_w]
    for s in range(1, GX):
        near.append(
            lax.ppermute(own_w, "col", col_perm(lambda x, zh, c, s=s: ((x // GX) * GX + (x + s) % GX, zh, c)))
        )
    far = [lax.ppermute(w, "col", swap_core) for w in near]
    ws = near + far
    other = lax.ppermute(mine, "row", row_perm(lambda z, q: (1 - z, q)))
    own = jnp.stack([mine, other])
    up_perm = row_perm(lambda z, q: (z, q + 1))
    down_perm = row_perm(lambda z, q: (z, q - 1))
    got = [own]
    up = down = own
    for _ in range(1, Y // 2):
        up = lax.ppermute(up, "row", up_perm)
        down = lax.ppermute(down, "row", down_perm)
        got += [up, down]
    got.append(lax.ppermute(up[:1], "row", up_perm))
    got.append(lax.ppermute(down[1:], "row", down_perm))

    acc = None
    for at, block in enumerate(got):
        acc = multiply(scalars, at, block, ws, acc, blocks)

    arrived = lax.all_to_all(acc, "col", 0, 0, tiled=True, axis_index_groups=PEER_GROUPS)
    total = jnp.sum(arrived, axis=0)
    run = virt // (X * ZH * CORES)
    return total.reshape(blocks, run, pairs, wb).transpose(1, 0, 2, 3)


def solution(mesh):
    return jax.shard_map(
        shards,
        mesh=mesh,
        in_specs=(P(None, "row", "col", None), P("col", "row", None)),
        out_specs=P("col", None, None, "row"),
        check_vma=False,
    )
```

time: 375 us -> 239 us (0.64)
  the two profiles are of different devices: /device:TPU:1 before, /device:TPU:58 now
where the time goes in v1:
time: 239 us; the launch traced here: 237 us
  waiting for transfers between devices  82.5 us (35%)
  starting transfers between devices  50 us (21%)
  blocking collectives  48.6 us (20%)
  Pallas kernels  36 us (15%)
  local copies, waits for them, and re-layouts  18.3 us (8%)
    ppermute x3, waiting for transfers between devices, shards(): lax.ppermute(own_w, 'col', col_perm(lambda x, zh, c, s=s: (x // GX * GX +...  59.6 us
    all_to_all x1, blocking collectives, shards(): lax.all_to_all(acc, 'col', 0, 0, tiled=True, axis_index_groups=PEER_GROUPS)  36 us
    pallas_call x9, Pallas kernels, multiply(): pl.pallas_call(functools.partial(multiply_kernel, acc is not None, blocks...  33.8 us
    ppermute x3, waiting for transfers between devices, shards(): down = lax.ppermute(down, 'row', down_perm)  20.6 us
    ppermute x3, starting transfers between devices, shards(): up = lax.ppermute(up, 'row', up_perm)  15.1 us
    all_to_all x1, blocking collectives, shards(): lax.all_to_all(sent, 'col', 0, 0, tiled=True, axis_index_groups=MEMBER_GR...  12.6 us
    ppermute x3, starting transfers between devices, shards(): lax.ppermute(own_w, 'col', col_perm(lambda x, zh, c, s=s: (x // GX * GX +...  9.99 us
    ppermute x4, starting transfers between devices, shards(): far = [lax.ppermute(w, 'col', swap_core) for w in near]  8.15 us
  transfers between devices with their start and end apart: 16, of which 5 were waited for; matrix products, arithmetic and copies ran while one was open for 7% of the time, Pallas kernels for 13%

profile of v1, /device:TPU:58, one launch (start us, length us, event | category | flops | bytes accessed | tf_op | source)
XLA Modules:
  0.0 237.2 jit_solution(18259381449922570884)
XLA Ops:
  0.0 2.2 shard_map.46
  2.2 12.6 %all_to_all.10 = f32[8,32,256]{2,1,0:T(8,128)S(1)} all-to-all(f32[8,32,256]{2,1,0:T(8,128)} %shard_map.46), channel_id=1, replica_groups={{0,1,8,9,16,17,24,25},{2,3,10,11,18,19,26,27},{4,5,12,13,20,21,28,29},{..., dimensions={0} | all-to-all | bytes 524288 | tf_op jit(solution)/shard_map/all_to_all | solution.py:191
  14.8 5.2 %collective-permute-start = (f32[8,32,256]{2,1,0:T(8,128)S(1)}, f32[8,32,256]{2,1,0:T(8,128)S(1)}, u32[]{:S(2)}, u32[]{:S(2)}) collective-permute-start(f32[8,32,256]{2,1,0:T(8,128)S(1)} %all_to_all.10), channel_id=1, source_target_pairs={{0,512},{64,576},{128,640},{192,704},{256,768},{320,832},{384,896}... | collective-permute-start | bytes 786440 | tf_op jit(solution)/shard_map/ppermute | solution.py:205
  20.0 3.6 %copy.14 = f32[8,32,1024]{1,2,0:T(8,128)} copy(f32[8,32,1024]{2,1,0:T(8,128)} %param.5) | data formatting | bytes 2097152 | tf_op args[1]
  23.6 2.3 collective-permute-done
  25.9 0.9 pad_maximum_fusion.refs_1_
  26.8 4.8 %collective-permute-start.12 = (f32[2,8,32,256]{3,2,1,0:T(8,128)}, f32[2,8,32,256]{3,2,1,0:T(8,128)}, u32[]{:S(2)}, u32[]{:S(2)}) collective-permute-start(f32[2,8,32,256]{3,2,1,0:T(8,128)} %pad_maximum_fusion.refs_1_), channel_id=1, source_target_pairs={{0,64},{64,128},{128,192},{192,256},{256,320},{320,384},{384,448},... | collective-permute-start | bytes 1572872 | tf_op jit(solution)/shard_map/ppermute | solution.py:212
  31.6 4.8 %copy.15 = f32[64,8,16,32]{3,2,1,0:T(8,128)} copy(f32[64,8,16,32]{3,2,0,1:T(8,128)} %bitcast.13) | data formatting | bytes 2097152 | tf_op jit(solution)/shard_map/transpose | solution.py:196
  36.4 3.5 %reshape.14.refs_2_ = f32[16,32,512]{2,1,0:T(8,128)S(1)} reshape(f32[64,8,16,32]{3,2,1,0:T(8,128)} %copy.15) | data formatting | bytes 2097152 | tf_op jit(solution)/shard_map/reshape | solution.py:196
  40.0 4.2 %collective-permute-start.6 = (f32[16,32,512]{2,1,0:T(8,128)S(1)}, f32[16,32,512]{2,1,0:T(8,128)S(1)}, u32[]{:S(2)}, u32[]{:S(2)}) collective-permute-start(f32[16,32,512]{2,1,0:T(8,128)S(1)} %reshape.14.refs_2_), channel_id=1, source_target_pairs={{0,16},{1,17},{2,18},{3,19},{4,20},{5,21},{6,22},{7,23},{8,24},{9,... | collective-permute-start | bytes 3145736 | tf_op jit(solution)/shard_map/ppermute | solution.py:201
  44.1 1.9 collective-permute-start.7
  46.0 3.9 %collective-permute-start.5 = (f32[16,32,512]{2,1,0:T(8,128)S(1)}, f32[16,32,512]{2,1,0:T(8,128)}, u32[]{:S(2)}, u32[]{:S(2)}) collective-permute-start(f32[16,32,512]{2,1,0:T(8,128)S(1)} %reshape.14.refs_2_), channel_id=1, source_target_pairs={{0,8},{1,9},{2,10},{3,11},{4,12},{5,13},{6,14},{7,15},{8,16},{9,17... | collective-permute-start | bytes 3145736 | tf_op jit(solution)/shard_map/ppermute | solution.py:201
  50.0 1.9 collective-permute-start.1
  51.9 0.0 collective-permute-done.12.refs_1_
  51.9 5.1 %collective-permute-start.13 = (f32[2,8,32,256]{3,2,1,0:T(8,128)}, f32[2,8,32,256]{3,2,1,0:T(8,128)S(1)}, u32[]{:S(2)}, u32[]{:S(2)}) collective-permute-start(f32[2,8,32,256]{3,2,1,0:T(8,128)} %collective-permute-done.12.refs_1_), channel_id=1, source_target_pairs={{0,64},{64,128},{128,192},{192,256},{256,320},{320,384},{384,448},... | collective-permute-start | bytes 1572872 | tf_op jit(solution)/shard_map/ppermute | solution.py:212
  57.1 8.5 %collective-permute-done.1.refs_1_ = f32[2,8,32,256]{3,2,1,0:T(8,128)S(1)} collective-permute-done((f32[2,8,32,256]{3,2,1,0:T(8,128)}, f32[2,8,32,256]{3,2,1,0:T(8,128)S(1)}, u32[]{:S(2)}, u32[]{:S(2)}) %collective-permute-start.1) | collective-permute-done | bytes 524320 | tf_op jit(solution)/shard_map/ppermute | solution.py:213
  65.5 1.9 collective-permute-start.2
  67.5 0.0 collective-permute-done.13.refs_1_
  67.5 5.1 %collective-permute-start.14 = (f32[2,8,32,256]{3,2,1,0:T(8,128)S(1)}, f32[2,8,32,256]{3,2,1,0:T(8,128)}, u32[]{:S(2)}, u32[]{:S(2)}) collective-permute-start(f32[2,8,32,256]{3,2,1,0:T(8,128)S(1)} %collective-permute-done.13.refs_1_), channel_id=1, source_target_pairs={{0,64},{64,128},{128,192},{192,256},{256,320},{320,384},{384,448},... | collective-permute-start | bytes 1572872 | tf_op jit(solution)/shard_map/ppermute | solution.py:212
  72.6 37.1 %collective-permute-done.6.refs_4_ = f32[16,32,512]{2,1,0:T(8,128)S(1)} collective-permute-done((f32[16,32,512]{2,1,0:T(8,128)S(1)}, f32[16,32,512]{2,1,0:T(8,128)S(1)}, u32[]{:S(2)}, u32[]{:S(2)}) %collective-permute-start.6) | collective-permute-done | bytes 1048608 | tf_op jit(solution)/shard_map/ppermute | solution.py:201
  109.7 1.9 collective-permute-start.8
  111.6 22.5 %collective-permute-done.7.refs_5_ = f32[16,32,512]{2,1,0:T(8,128)S(1)} collective-permute-done((f32[16,32,512]{2,1,0:T(8,128)S(1)}, f32[16,32,512]{2,1,0:T(8,128)S(1)}, u32[]{:S(2)}, u32[]{:S(2)}) %collective-permute-start.7) | collective-permute-done | bytes 1048608 | tf_op jit(solution)/shard_map/ppermute | solution.py:201
  134.1 1.9 collective-permute-start.10
  136.1 0.0 collective-permute-done.5.refs_3_
  136.1 2.4 %collective-permute-start.11 = (f32[16,32,512]{2,1,0:T(8,128)S(1)}, f32[16,32,512]{2,1,0:T(8,128)}, u32[]{:S(2)}, u32[]{:S(2)}) collective-permute-start(f32[16,32,512]{2,1,0:T(8,128)S(1)} %collective-permute-done.7.refs_5_), channel_id=1, source_target_pairs={{0,1},{1,0},{2,3},{3,2},{4,5},{5,4},{6,7},{7,6},{8,9},{9,8},{10,11... | collective-permute-start | bytes 3145736 | tf_op jit(solution)/shard_map/ppermute | solution.py:203
  138.5 1.9 collective-permute-start.9
  140.5 1.9 collective-permute-start.3
  142.4 0.7 dynamic-slice_bitcast_fusion.1
  143.1 0.7 dynamic-slice_bitcast_fusion
  143.8 0.6 pad_add_fusion.refs_0_
  144.4 1.7 slice.9
  146.1 12.1 %collective-permute-done.3.refs_1_ = f32[2,8,32,256]{3,2,1,0:T(8,128)} collective-permute-done((f32[2,8,32,256]{3,2,1,0:T(8,128)}, f32[2,8,32,256]{3,2,1,0:T(8,128)}, u32[]{:S(2)}, u32[]{:S(2)}) %collective-permute-start.3) | collective-permute-done | bytes 524320 | tf_op jit(solution)/shard_map/ppermute | solution.py:213
  158.2 1.9 collective-permute-start.15
  160.1 1.7 slice.8
  161.8 3.9 %collective-permute-start.4 = (f32[1,8,32,256]{3,2,1,0:T(8,128)}, f32[1,8,32,256]{3,2,1,0:T(8,128)S(1)}, u32[]{:S(2)}, u32[]{:S(2)}) collective-permute-start(f32[1,8,32,256]{3,2,1,0:T(8,128)} %slice.8), channel_id=1, source_target_pairs={{0,448},{64,0},{128,64},{192,128},{256,192},{320,256},{384,320},{4... | collective-permute-start | bytes 786440 | tf_op jit(solution)/shard_map/ppermute | solution.py:216
  165.8 3.6 %shard_map.47.refs_10_ = f32[8,32,512]{2,1,0:T(8,128)} custom-call(s32[26]{0:T(128)} %pad_add_fusion.refs_0_, f32[2,8,32,256]{3,2,1,0:T(8,128)} %pad_maximum_fusion.refs_1_, f32[16,32,512]{2,1,0:T(8,128)} %copy-done, f32[16,32,512]{2,1,0:T(8,128)} %collective-permute-done.5.refs_3_, f32[16,32,512]{2,1,0:T(8,128)} %copy-done.1, f32[16,32,512]{2,1,0:T(8,128)} %copy-done.2, ...), custom_call_target="tpu_custom_call" | custom-call | flops 402653184 | bytes 1572864 | tf_op jit(solution)/shard_map/pallas_call | solution.py:166
  169.4 4.0 %shard_map.48.refs_10_ = f32[8,32,512]{2,1,0:T(8,128)} custom-call(s32[26]{0:T(128)} %pad_add_fusion.refs_0_, f32[2,8,32,256]{3,2,1,0:T(8,128)} %collective-permute-done.12.refs_1_, f32[16,32,512]{2,1,0:T(8,128)} %copy-done, f32[16,32,512]{2,1,0:T(8,128)} %collective-permute-done.5.refs_3_, ...), custom_call_target="tpu_custom_call", output_to_operand_aliasing={{}: (10, {})} | custom-call | flops 402653184 | bytes 1572864 | tf_op jit(solution)/shard_map/pallas_call | solution.py:166
  173.4 4.0 %shard_map.49.refs_10_ = f32[8,32,512]{2,1,0:T(8,128)} custom-call(s32[26]{0:T(128)} %pad_add_fusion.refs_0_, f32[2,8,32,256]{3,2,1,0:T(8,128)} %copy-done.3, f32[16,32,512]{2,1,0:T(8,128)} %copy-done, f32[16,32,512]{2,1,0:T(8,128)} %collective-permute-done.5.refs_3_, f32[16,32,512]{2,1,0:T(8,128)} %copy-done.1, ...), custom_call_target="tpu_custom_call", output_to_operand_aliasing={{}: (10, {})} | custom-call | flops 402653184 | bytes 1572864 | tf_op jit(solution)/shard_map/pallas_call | solution.py:166
  177.3 4.0 %shard_map.50.refs_10_ = f32[8,32,512]{2,1,0:T(8,128)} custom-call(s32[26]{0:T(128)} %pad_add_fusion.refs_0_, f32[2,8,32,256]{3,2,1,0:T(8,128)} %copy-done.4, f32[16,32,512]{2,1,0:T(8,128)} %copy-done, f32[16,32,512]{2,1,0:T(8,128)} %collective-permute-done.5.refs_3_, f32[16,32,512]{2,1,0:T(8,128)} %copy-done.1, ...), custom_call_target="tpu_custom_call", output_to_operand_aliasing={{}: (10, {})} | custom-call | flops 402653184 | bytes 1572864 | tf_op jit(solution)/shard_map/pallas_call | solution.py:166
  181.3 4.0 %shard_map.51.refs_10_ = f32[8,32,512]{2,1,0:T(8,128)} custom-call(s32[26]{0:T(128)} %pad_add_fusion.refs_0_, f32[2,8,32,256]{3,2,1,0:T(8,128)} %collective-permute-done.2.refs_1_, f32[16,32,512]{2,1,0:T(8,128)} %copy-done, f32[16,32,512]{2,1,0:T(8,128)} %collective-permute-done.5.refs_3_, ...), custom_call_target="tpu_custom_call", output_to_operand_aliasing={{}: (10, {})} | custom-call | flops 402653184 | bytes 1572864 | tf_op jit(solution)/shard_map/pallas_call | solution.py:166
  185.2 4.0 %shard_map.52.refs_10_ = f32[8,32,512]{2,1,0:T(8,128)} custom-call(s32[26]{0:T(128)} %pad_add_fusion.refs_0_, f32[2,8,32,256]{3,2,1,0:T(8,128)} %collective-permute-done.14.refs_1_, f32[16,32,512]{2,1,0:T(8,128)} %copy-done, f32[16,32,512]{2,1,0:T(8,128)} %collective-permute-done.5.refs_3_, ...), custom_call_target="tpu_custom_call", output_to_operand_aliasing={{}: (10, {})} | custom-call | flops 402653184 | bytes 1572864 | tf_op jit(solution)/shard_map/pallas_call | solution.py:166
  189.2 4.0 %shard_map.53.refs_10_ = f32[8,32,512]{2,1,0:T(8,128)} custom-call(s32[26]{0:T(128)} %pad_add_fusion.refs_0_, f32[2,8,32,256]{3,2,1,0:T(8,128)} %collective-permute-done.3.refs_1_, f32[16,32,512]{2,1,0:T(8,128)} %copy-done, f32[16,32,512]{2,1,0:T(8,128)} %collective-permute-done.5.refs_3_, ...), custom_call_target="tpu_custom_call", output_to_operand_aliasing={{}: (10, {})} | custom-call | flops 402653184 | bytes 1572864 | tf_op jit(solution)/shard_map/pallas_call | solution.py:166
  193.2 3.2 %shard_map.54.refs_10_ = f32[8,32,512]{2,1,0:T(8,128)} custom-call(s32[26]{0:T(128)} %pad_add_fusion.refs_0_, f32[1,8,32,256]{3,2,1,0:T(8,128)} %collective-permute-done.15.refs_1_, f32[16,32,512]{2,1,0:T(8,128)} %copy-done, f32[16,32,512]{2,1,0:T(8,128)} %collective-permute-done.5.refs_3_, ...), custom_call_target="tpu_custom_call", output_to_operand_aliasing={{}: (10, {})} | custom-call | flops 201326592 | bytes 1310720 | tf_op jit(solution)/shard_map/pallas_call | solution.py:166
  196.4 0.7 copy-done.5
  197.1 3.2 %shard_map.55 = f32[8,32,512]{2,1,0:T(8,128)} custom-call(s32[26]{0:T(128)} %pad_add_fusion.refs_0_, f32[1,8,32,256]{3,2,1,0:T(8,128)} %copy-done.5, f32[16,32,512]{2,1,0:T(8,128)} %copy-done, f32[16,32,512]{2,1,0:T(8,128)} %collective-permute-done.5.refs_3_, f32[16,32,512]{2,1,0:T(8,128)} %copy-done.1, ...), custom_call_target="tpu_custom_call", output_to_operand_aliasing={{}: (10, {})} | custom-call | flops 201326592 | bytes 1310720 | tf_op jit(solution)/shard_map/pallas_call | solution.py:166
  200.3 36.0 %all_to_all.11 = f32[8,32,512]{2,1,0:T(8,128)S(1)} all-to-all(f32[8,32,512]{2,1,0:T(8,128)} %shard_map.55), channel_id=1, replica_groups={{0,2,4,6,32,34,36,38},{1,3,5,7,33,35,37,39},{8,10,12,14,40,42,44,46},{9..., dimensions={0} | all-to-all | bytes 1048576 | tf_op jit(solution)/shard_map/all_to_all | solution.py:222
  236.3 0.1 reshape.15
  236.5 0.7 copy.16
  (20 shorter events, 0.1 us)
Async XLA Ops:
  14.8 11.1 %collective-permute-start = (f32[8,32,256]{2,1,0:T(8,128)S(1)}, f32[8,32,256]{2,1,0:T(8,128)S(1)}, u32[]{:S(2)}, u32[]{:S(2)}) collective-permute-start(f32[8,32,256]{2,1,0:T(8,128)S(1)} %all_to_all.10), channel_id=1, source_target_pairs={{0,512},{64,576},{128,640},{192,704},{256,768},{320,832},{384,896}... | collective-permute-start | bytes 786440 | tf_op jit(solution)/shard_map/ppermute | solution.py:205
  26.8 25.1 %collective-permute-start.12 = (f32[2,8,32,256]{3,2,1,0:T(8,128)}, f32[2,8,32,256]{3,2,1,0:T(8,128)}, u32[]{:S(2)}, u32[]{:S(2)}) collective-permute-start(f32[2,8,32,256]{3,2,1,0:T(8,128)} %pad_maximum_fusion.refs_1_), channel_id=1, source_target_pairs={{0,64},{64,128},{128,192},{192,256},{256,320},{320,384},{384,448},... | collective-permute-start | bytes 1572872 | tf_op jit(solution)/shard_map/ppermute | solution.py:212
  39.9 125.8 %copy-start = (f32[16,32,512]{2,1,0:T(8,128)}, f32[16,32,512]{2,1,0:T(8,128)S(1)}, u32[]{:S(2)}) copy-start(f32[16,32,512]{2,1,0:T(8,128)S(1)} %reshape.14.refs_2_) | copy-start | bytes 3145732
  40.0 69.7 %collective-permute-start.6 = (f32[16,32,512]{2,1,0:T(8,128)S(1)}, f32[16,32,512]{2,1,0:T(8,128)S(1)}, u32[]{:S(2)}, u32[]{:S(2)}) collective-permute-start(f32[16,32,512]{2,1,0:T(8,128)S(1)} %reshape.14.refs_2_), channel_id=1, source_target_pairs={{0,16},{1,17},{2,18},{3,19},{4,20},{5,21},{6,22},{7,23},{8,24},{9,... | collective-permute-start | bytes 3145736 | tf_op jit(solution)/shard_map/ppermute | solution.py:201
  44.1 90.0 %collective-permute-start.7 = (f32[16,32,512]{2,1,0:T(8,128)S(1)}, f32[16,32,512]{2,1,0:T(8,128)S(1)}, u32[]{:S(2)}, u32[]{:S(2)}) collective-permute-start(f32[16,32,512]{2,1,0:T(8,128)S(1)} %reshape.14.refs_2_), channel_id=1, source_target_pairs={{0,24},{1,25},{2,26},{3,27},{4,28},{5,29},{6,30},{7,31},{8,0},{9,1... | collective-permute-start | bytes 3145736 | tf_op jit(solution)/shard_map/ppermute | solution.py:201
  46.0 90.0 %collective-permute-start.5 = (f32[16,32,512]{2,1,0:T(8,128)S(1)}, f32[16,32,512]{2,1,0:T(8,128)}, u32[]{:S(2)}, u32[]{:S(2)}) collective-permute-start(f32[16,32,512]{2,1,0:T(8,128)S(1)} %reshape.14.refs_2_), channel_id=1, source_target_pairs={{0,8},{1,9},{2,10},{3,11},{4,12},{5,13},{6,14},{7,15},{8,16},{9,17... | collective-permute-start | bytes 3145736 | tf_op jit(solution)/shard_map/ppermute | solution.py:201
  50.0 15.6 %collective-permute-start.1 = (f32[2,8,32,256]{3,2,1,0:T(8,128)}, f32[2,8,32,256]{3,2,1,0:T(8,128)S(1)}, u32[]{:S(2)}, u32[]{:S(2)}) collective-permute-start(f32[2,8,32,256]{3,2,1,0:T(8,128)} %pad_maximum_fusion.refs_1_), channel_id=1, source_target_pairs={{0,448},{64,0},{128,64},{192,128},{256,192},{320,256},{384,320},{4... | collective-permute-start | bytes 1572872 | tf_op jit(solution)/shard_map/ppermute | solution.py:213
  51.9 15.6 %collective-permute-start.13 = (f32[2,8,32,256]{3,2,1,0:T(8,128)}, f32[2,8,32,256]{3,2,1,0:T(8,128)S(1)}, u32[]{:S(2)}, u32[]{:S(2)}) collective-permute-start(f32[2,8,32,256]{3,2,1,0:T(8,128)} %collective-permute-done.12.refs_1_), channel_id=1, source_target_pairs={{0,64},{64,128},{128,192},{192,256},{256,320},{320,384},{384,448},... | collective-permute-start | bytes 1572872 | tf_op jit(solution)/shard_map/ppermute | solution.py:212
  65.5 70.5 %copy-start.3 = (f32[2,8,32,256]{3,2,1,0:T(8,128)}, f32[2,8,32,256]{3,2,1,0:T(8,128)S(1)}, u32[]{:S(2)}) copy-start(f32[2,8,32,256]{3,2,1,0:T(8,128)S(1)} %collective-permute-done.1.refs_1_) | copy-start | bytes 1572868
  65.5 73.0 %collective-permute-start.2 = (f32[2,8,32,256]{3,2,1,0:T(8,128)S(1)}, f32[2,8,32,256]{3,2,1,0:T(8,128)}, u32[]{:S(2)}, u32[]{:S(2)}) collective-permute-start(f32[2,8,32,256]{3,2,1,0:T(8,128)S(1)} %collective-permute-done.1.refs_1_), channel_id=1, source_target_pairs={{0,448},{64,0},{128,64},{192,128},{256,192},{320,256},{384,320},{4... | collective-permute-start | bytes 1572872 | tf_op jit(solution)/shard_map/ppermute | solution.py:213
  67.5 71.0 %copy-start.4 = (f32[2,8,32,256]{3,2,1,0:T(8,128)}, f32[2,8,32,256]{3,2,1,0:T(8,128)S(1)}, u32[]{:S(2)}) copy-start(f32[2,8,32,256]{3,2,1,0:T(8,128)S(1)} %collective-permute-done.13.refs_1_) | copy-start | bytes 1572868
  67.5 73.0 %collective-permute-start.14 = (f32[2,8,32,256]{3,2,1,0:T(8,128)S(1)}, f32[2,8,32,256]{3,2,1,0:T(8,128)}, u32[]{:S(2)}, u32[]{:S(2)}) collective-permute-start(f32[2,8,32,256]{3,2,1,0:T(8,128)S(1)} %collective-permute-done.13.refs_1_), channel_id=1, source_target_pairs={{0,64},{64,128},{128,192},{192,256},{256,320},{320,384},{384,448},... | collective-permute-start | bytes 1572872 | tf_op jit(solution)/shard_map/ppermute | solution.py:212
  109.7 56.1 %copy-start.1 = (f32[16,32,512]{2,1,0:T(8,128)}, f32[16,32,512]{2,1,0:T(8,128)S(1)}, u32[]{:S(2)}) copy-start(f32[16,32,512]{2,1,0:T(8,128)S(1)} %collective-permute-done.6.refs_4_) | copy-start | bytes 3145732
  109.7 52.1 %collective-permute-start.8 = (f32[16,32,512]{2,1,0:T(8,128)S(1)}, f32[16,32,512]{2,1,0:T(8,128)}, u32[]{:S(2)}, u32[]{:S(2)}) collective-permute-start(f32[16,32,512]{2,1,0:T(8,128)S(1)} %reshape.14.refs_2_), channel_id=1, source_target_pairs={{0,1},{1,0},{2,3},{3,2},{4,5},{5,4},{6,7},{7,6},{8,9},{9,8},{10,11... | collective-permute-start | bytes 3145736 | tf_op jit(solution)/shard_map/ppermute | solution.py:203
  134.1 31.6 %copy-start.2 = (f32[16,32,512]{2,1,0:T(8,128)}, f32[16,32,512]{2,1,0:T(8,128)S(1)}, u32[]{:S(2)}) copy-start(f32[16,32,512]{2,1,0:T(8,128)S(1)} %collective-permute-done.7.refs_5_) | copy-start | bytes 3145732
  134.1 31.6 %collective-permute-start.10 = (f32[16,32,512]{2,1,0:T(8,128)S(1)}, f32[16,32,512]{2,1,0:T(8,128)}, u32[]{:S(2)}, u32[]{:S(2)}) collective-permute-start(f32[16,32,512]{2,1,0:T(8,128)S(1)} %collective-permute-done.6.refs_4_), channel_id=1, source_target_pairs={{0,1},{1,0},{2,3},{3,2},{4,5},{5,4},{6,7},{7,6},{8,9},{9,8},{10,11... | collective-permute-start | bytes 3145736 | tf_op jit(solution)/shard_map/ppermute | solution.py:203
  136.1 29.6 %collective-permute-start.11 = (f32[16,32,512]{2,1,0:T(8,128)S(1)}, f32[16,32,512]{2,1,0:T(8,128)}, u32[]{:S(2)}, u32[]{:S(2)}) collective-permute-start(f32[16,32,512]{2,1,0:T(8,128)S(1)} %collective-permute-done.7.refs_5_), channel_id=1, source_target_pairs={{0,1},{1,0},{2,3},{3,2},{4,5},{5,4},{6,7},{7,6},{8,9},{9,8},{10,11... | collective-permute-start | bytes 3145736 | tf_op jit(solution)/shard_map/ppermute | solution.py:203
  138.5 27.2 %collective-permute-start.9 = (f32[16,32,512]{2,1,0:T(8,128)}, f32[16,32,512]{2,1,0:T(8,128)}, u32[]{:S(2)}, u32[]{:S(2)}) collective-permute-start(f32[16,32,512]{2,1,0:T(8,128)} %collective-permute-done.5.refs_3_), channel_id=1, source_target_pairs={{0,1},{1,0},{2,3},{3,2},{4,5},{5,4},{6,7},{7,6},{8,9},{9,8},{10,11... | collective-permute-start | bytes 3145736 | tf_op jit(solution)/shard_map/ppermute | solution.py:203
  140.5 17.7 %collective-permute-start.3 = (f32[2,8,32,256]{3,2,1,0:T(8,128)}, f32[2,8,32,256]{3,2,1,0:T(8,128)}, u32[]{:S(2)}, u32[]{:S(2)}) collective-permute-start(f32[2,8,32,256]{3,2,1,0:T(8,128)} %collective-permute-done.2.refs_1_), channel_id=1, source_target_pairs={{0,448},{64,0},{128,64},{192,128},{256,192},{320,256},{384,320},{4... | collective-permute-start | bytes 1572872 | tf_op jit(solution)/shard_map/ppermute | solution.py:213
  158.2 34.9 %collective-permute-start.15 = (f32[1,8,32,256]{3,2,1,0:T(8,128)}, f32[1,8,32,256]{3,2,1,0:T(8,128)}, u32[]{:S(2)}, u32[]{:S(2)}) collective-permute-start(f32[1,8,32,256]{3,2,1,0:T(8,128)} %slice.9), channel_id=1, source_target_pairs={{0,64},{64,128},{128,192},{192,256},{256,320},{320,384},{384,448},... | collective-permute-start | bytes 786440 | tf_op jit(solution)/shard_map/ppermute | solution.py:215
  161.8 34.6 %collective-permute-start.4 = (f32[1,8,32,256]{3,2,1,0:T(8,128)}, f32[1,8,32,256]{3,2,1,0:T(8,128)S(1)}, u32[]{:S(2)}, u32[]{:S(2)}) collective-permute-start(f32[1,8,32,256]{3,2,1,0:T(8,128)} %slice.8), channel_id=1, source_target_pairs={{0,448},{64,0},{128,64},{192,128},{256,192},{320,256},{384,320},{4... | collective-permute-start | bytes 786440 | tf_op jit(solution)/shard_map/ppermute | solution.py:216
  196.4 0.7 copy-start.5

commit v2 on v1

--- a/solution.py
+++ b/solution.py
@@ -10,7 +10,7 @@
 
 X, ZH, CORES = 8, 4, 2
 ZL, Y = 2, 8
-GX = 4
+GX = 2
 XH = X // GX
 MEMBERS = GX * CORES
 PEERS = XH * ZH
@@ -41,7 +41,13 @@
 
 
 MEMBER_GROUPS = [
-    [col_of(xh * GX + xl, zh, core) for xl in range(GX) for core in range(CORES)]
+    [
+        (zl * Y + y) * (X * ZH * CORES) + col_of(xh * GX + xl, zh, core)
+        for zl in range(ZL)
+        for xl in range(GX)
+        for core in range(CORES)
+    ]
+    for y in range(Y)
     for xh in range(XH)
     for zh in range(ZH)
 ]
@@ -52,20 +58,18 @@
 ]
 
 
-BLOCKS = [((0, 1), 0)]
+CALLS = [[((0, 1), 0)]]
 for _step in range(1, Y // 2):
-    BLOCKS += [((0, 1), -_step), ((0, 1), _step)]
-BLOCKS += [((0,), Y // 2), ((1,), Y // 2)]
+    CALLS.append([((0, 1), -_step), ((0, 1), _step)])
+CALLS.append([((0,), Y // 2), ((1,), Y // 2)])
+PLACES = [[(zl, shift) for which, shift in call for zl in which] for call in CALLS]
+SLOTS = sum(len(places) for places in PLACES)
 
 
 def row_table():
-    table = np.zeros((ZL * Y, len(BLOCKS) * ZL), np.int32)
-    for zl in range(ZL):
-        for y in range(Y):
-            for n, (which, shift) in enumerate(BLOCKS):
-                for at in range(ZL):
-                    z = zl ^ which[min(at, len(which) - 1)]
-                    table[zl * Y + y, n * ZL + at] = z * Y + (y + shift) % Y
+    table = np.zeros((ZL * Y, SLOTS), np.int32)
+    for row in range(ZL * Y):
+        table[row] = [zl * Y + (row + shift) % Y for places in PLACES for zl, shift in places]
     return table
 
 
@@ -121,57 +125,56 @@
     )(t.reshape(blocks, rows, virt))
 
 
-def multiply_kernel(has_acc, blocks, *refs):
-    s_ref, t_ref = refs[0], refs[1]
-    w_refs = refs[2 : 2 + MEMBERS]
+def multiply_kernel(has_acc, blocks, order_at, n_t, n_w, *refs):
+    s_ref = refs[0]
+    t_refs = refs[1 : 1 + n_t]
+    w_refs = refs[1 + n_t : 1 + n_t + n_w]
     out_ref = refs[-1]
-
-    @pl.when(pl.program_id(0) == 0)
-    def _():
-        if has_acc:
-            out_ref[...] = refs[2 + MEMBERS][...]
-        else:
-            out_ref[...] = jnp.zeros_like(out_ref)
-
-    left = jnp.concatenate([t_ref[0, s_ref[len(BLOCKS) * ZL + n]] for n in range(MEMBERS)], axis=0)
+    left = jnp.concatenate(
+        [t[z, s_ref[order_at + n]] for t in t_refs for z in range(t.shape[0]) for n in range(MEMBERS)], axis=0
+    )
     right = jnp.concatenate([w[0] for w in w_refs], axis=0)
     lh, ll = split2(left)
     rh, rl = split2(right)
-    dims = (((0,), (0,)), ((), ()))
     total = lax.dot_general(
         jnp.concatenate([lh, lh, ll], axis=0),
         jnp.concatenate([rh, rl, rh], axis=0),
-        dims,
+        (((0,), (0,)), ((), ())),
         preferred_element_type=F32,
     )
     run = total.shape[0] // (blocks * PEERS)
     total = total.reshape(blocks, PEERS, run, total.shape[1])
     for i in range(blocks):
-        out_ref[:, i * run : (i + 1) * run, :] += total[i]
-
-
-def multiply(scalars, at, t, ws, acc, blocks):
-    rows, width = t.shape[2], t.shape[3]
+        rows = slice(i * run, (i + 1) * run)
+        if has_acc:
+            out_ref[:, rows, :] = refs[1 + n_t + n_w][:, rows, :] + total[i]
+        else:
+            out_ref[:, rows, :] = total[i]
+
+
+def multiply(scalars, at, ts, ws, acc, blocks):
+    rows, width = ts[0].shape[2], ts[0].shape[3]
     wide = ws[0].shape[2]
     out_shape = (PEERS, width // PEERS, wide)
-    in_specs = [pl.BlockSpec((1, MEMBERS, rows, width), lambda z, s: (z, 0, 0, 0))]
-    in_specs += [pl.BlockSpec((1, rows, wide), lambda z, s: (s[at * ZL + z], 0, 0))] * MEMBERS
-    args = [scalars, t, *ws]
+    first = sum(len(places) for places in PLACES[:at])
+    slots = range(first, first + len(PLACES[at]))
+    in_specs = [pl.BlockSpec(t.shape, lambda z, s: (0, 0, 0, 0)) for t in ts]
+    in_specs += [
+        pl.BlockSpec((1, rows, wide), lambda z, s, slot=slot: (s[slot], 0, 0)) for slot in slots for _ in ws
+    ]
+    args = [scalars, *ts, *(list(ws) * len(slots))]
     whole = pl.BlockSpec(out_shape, lambda z, s: (0, 0, 0))
-    aliases = {}
     if acc is not None:
         in_specs.append(whole)
         args.append(acc)
-        aliases = {len(args) - 1: 0}
+    depth = len(slots) * len(ws) * rows
     return pl.pallas_call(
-        functools.partial(multiply_kernel, acc is not None, blocks),
-        grid_spec=pltpu.PrefetchScalarGridSpec(
-            num_scalar_prefetch=1, grid=(t.shape[0],), in_specs=in_specs, out_specs=whole
-        ),
+        functools.partial(multiply_kernel, acc is not None, blocks, SLOTS, len(ts), len(slots) * len(ws)),
+        grid_spec=pltpu.PrefetchScalarGridSpec(num_scalar_prefetch=1, grid=(1,), in_specs=in_specs, out_specs=whole),
         out_shape=jax.ShapeDtypeStruct(out_shape, F32),
-        input_output_aliases=aliases,
+        compiler_params=pltpu.CompilerParams(vmem_limit_bytes=32 * 2**20),
         cost_estimate=pl.CostEstimate(
-            flops=6 * t.shape[0] * MEMBERS * rows * width * wide, bytes_accessed=t.size * 4 + 2 * len(ws) * rows * wide * 4, transcendentals=0
+            flops=6 * depth * width * wide, bytes_accessed=4 * depth * (width + wide), transcendentals=0
         ),
     )(*args)
 
@@ -188,36 +191,36 @@
     )
 
     sent = regroup(t_pair)
-    mine = lax.all_to_all(sent, "col", 0, 0, tiled=True, axis_index_groups=MEMBER_GROUPS)
+    own = lax.all_to_all(
+        jnp.concatenate([sent] * ZL), ("row", "col"), 0, 0, tiled=True, axis_index_groups=MEMBER_GROUPS
+    ).reshape(ZL, MEMBERS, rows, -1)
 
     depth, wb, kj = w_ovov.shape
     occupied = ks * ZL * Y
     pairs = kj // occupied
     own_w = w_ovov.reshape(cs, wb, occupied, pairs).transpose(2, 0, 3, 1).reshape(ZL * Y, rows, pairs * wb)
     swap_core = col_perm(lambda x, zh, c: (x, zh, 1 - c))
-    near = [own_w]
-    for s in range(1, GX):
-        near.append(
-            lax.ppermute(own_w, "col", col_perm(lambda x, zh, c, s=s: ((x // GX) * GX + (x + s) % GX, zh, c)))
-        )
-    far = [lax.ppermute(w, "col", swap_core) for w in near]
-    ws = near + far
-    other = lax.ppermute(mine, "row", row_perm(lambda z, q: (1 - z, q)))
-    own = jnp.stack([mine, other])
+    swap_x = col_perm(lambda x, zh, c: (x ^ 1, zh, c))
+    w_x = lax.ppermute(own_w, "col", swap_x)
+    w_c = lax.ppermute(own_w, "col", swap_core)
+
     up_perm = row_perm(lambda z, q: (z, q + 1))
     down_perm = row_perm(lambda z, q: (z, q - 1))
-    got = [own]
+    got = [(own,)]
     up = down = own
-    for _ in range(1, Y // 2):
+    for step in range(1, Y // 2):
         up = lax.ppermute(up, "row", up_perm)
         down = lax.ppermute(down, "row", down_perm)
-        got += [up, down]
-    got.append(lax.ppermute(up[:1], "row", up_perm))
-    got.append(lax.ppermute(down[1:], "row", down_perm))
+        got.append((up, down))
+        if step == 2:
+            up, down, w_x, w_c = lax.optimization_barrier((up, down, w_x, w_c))
+    w_xc = lax.ppermute(w_x, "col", swap_core)
+    got.append((lax.ppermute(up[:1], "row", up_perm), lax.ppermute(down[1:], "row", down_perm)))
+    ws = [own_w, w_x, w_c, w_xc]
 
     acc = None
-    for at, block in enumerate(got):
-        acc = multiply(scalars, at, block, ws, acc, blocks)
+    for at, ts in enumerate(got):
+        acc = multiply(scalars, at, ts, ws, acc, blocks)
 
     arrived = lax.all_to_all(acc, "col", 0, 0, tiled=True, axis_index_groups=PEER_GROUPS)
     total = jnp.sum(arrived, axis=0)

time: 239 us -> 162 us (0.68)
  the two profiles are of different devices: /device:TPU:58 before, /device:TPU:1 now
where the time goes in v2:
time: 162 us; the launch traced here: 161 us
  starting transfers between devices  55.5 us (34%)
  blocking collectives  43.2 us (27%)
  waiting for transfers between devices  27.7 us (17%)
  local copies, waits for them, and re-layouts  17.7 us (11%)
  Pallas kernels  14.6 us (9%)
  other arithmetic  2.04 us (1%)
    all_to_all x1, blocking collectives, shards(): lax.all_to_all(acc, 'col', 0, 0, tiled=True, axis_index_groups=PEER_GROUPS)  43.2 us
    ppermute x3, waiting for transfers between devices, shards(): up = lax.ppermute(up, 'row', up_perm)  20.2 us
    all_to_all x1, starting transfers between devices, shards(): lax.all_to_all(jnp.concatenate([sent] * ZL), ('row', 'col'), 0, 0, tiled=...  18.2 us
    ppermute x3, starting transfers between devices, shards(): down = lax.ppermute(down, 'row', down_perm)  15.5 us
    pallas_call x5, Pallas kernels, multiply(): pl.pallas_call(functools.partial(multiply_kernel, acc is not None, blocks...  12.5 us
    ppermute x3, waiting for transfers between devices, shards(): down = lax.ppermute(down, 'row', down_perm)  7.49 us
    ppermute x3, starting transfers between devices, shards(): up = lax.ppermute(up, 'row', up_perm)  5.75 us
    unnamed x9, local copies, waits for them, and re-layouts  5.19 us
  transfers between devices with their start and end apart: 12, of which 5 were waited for; matrix products, arithmetic and copies ran while one was open for 10% of the time, Pallas kernels for 6%

profile of v2, /device:TPU:1, one launch (start us, length us, event | category | flops | bytes accessed | tf_op | source)
XLA Modules:
  0.0 161.0 jit_solution(11599878247615899395)
XLA Ops:
  0.0 2.1 %shard_map.46 = f32[4,32,512]{2,1,0:T(8,128)} custom-call(f32[4,32,512]{2,1,0:T(8,128)} %bitcast.14), custom_call_target="tpu_custom_call" | custom-call | flops 201326592 | bytes 524288 | tf_op jit(solution)/shard_map/pallas_call | solution.py:121
  2.1 1.9 %pad_maximum_fusion = f32[8,32,512]{2,1,0:T(8,128)} fusion(f32[4,32,512]{2,1,0:T(8,128)} %shard_map.46), kind=kLoop, calls=%fused_computation | loop fusion | flops 131072 | bytes 786432 | tf_op jit(solution)/shard_map/concatenate | solution.py:195
  4.0 18.2 %all-to-all-start = ((f32[8,32,512]{2,1,0:T(8,128)}), f32[8,32,512]{2,1,0:T(8,128)}, u32[]{:S(2)}, u32[]{:S(2)}) async-start(f32[8,32,512]{2,1,0:T(8,128)} %pad_maximum_fusion), calls=%async_computation | async-start | bytes 1048576 | tf_op jit(solution)/shard_map/all_to_all | solution.py:194
  22.2 3.6 %copy.6 = f32[8,32,1024]{1,2,0:T(8,128)} copy(f32[8,32,1024]{2,1,0:T(8,128)} %param.5) | data formatting | bytes 2097152 | tf_op args[1]
  25.8 4.8 %copy.7 = f32[64,8,16,32]{3,2,1,0:T(8,128)} copy(f32[64,8,16,32]{3,2,0,1:T(8,128)} %bitcast.12) | data formatting | bytes 2097152 | tf_op jit(solution)/shard_map/transpose | solution.py:201
  30.6 3.5 %reshape.18.refs_2_.refs_6_.refs_3_.refs_7_.refs_11_.refs_15_ = f32[16,32,512]{2,1,0:T(8,128)S(1)} reshape(f32[64,8,16,32]{3,2,1,0:T(8,128)} %copy.7) | data formatting | bytes 2097152 | tf_op jit(solution)/shard_map/reshape | solution.py:201
  34.1 3.3 %collective-permute-start.4 = (f32[16,32,512]{2,1,0:T(8,128)S(1)}, f32[16,32,512]{2,1,0:T(8,128)S(1)}, u32[]{:S(2)}, u32[]{:S(2)}) collective-permute-start(f32[16,32,512]{2,1,0:T(8,128)S(1)} %reshape.18.refs_2_.refs_6_.refs_3_.refs_7_.refs_11_.refs_15_), channel_id=1, source_target_pairs={{0,8},{1,9},{2,10},{3,11},{4,12},{5,13},{6,14},{7,15},{8,0},{9,1},... | collective-permute-start | bytes 3145736 | tf_op jit(solution)/shard_map/ppermute | solution.py:204
  37.4 0.0 all-to-all-done
  37.4 1.9 %collective-permute-start = (f32[2,4,32,512]{3,2,1,0:T(8,128)}, f32[2,4,32,512]{3,2,1,0:T(8,128)S(1)}, u32[]{:S(2)}, u32[]{:S(2)}) collective-permute-start(f32[2,4,32,512]{3,2,1,0:T(8,128)} %bitcast.3.refs_1_), channel_id=1, source_target_pairs={{0,64},{64,128},{128,192},{192,256},{256,320},{320,384},{384,448},... | collective-permute-start | bytes 1572872 | tf_op jit(solution)/shard_map/ppermute | solution.py:212
  39.4 2.5 %collective-permute-start.5 = (f32[16,32,512]{2,1,0:T(8,128)S(1)}, f32[16,32,512]{2,1,0:T(8,128)S(1)}, u32[]{:S(2)}, u32[]{:S(2)}) collective-permute-start(f32[16,32,512]{2,1,0:T(8,128)S(1)} %reshape.18.refs_2_.refs_6_.refs_3_.refs_7_.refs_11_.refs_15_), channel_id=1, source_target_pairs={{0,1},{1,0},{2,3},{3,2},{4,5},{5,4},{6,7},{7,6},{8,9},{9,8},{10,11... | collective-permute-start | bytes 3145736 | tf_op jit(solution)/shard_map/ppermute | solution.py:205
  41.9 4.9 %collective-permute-start.2 = (f32[2,4,32,512]{3,2,1,0:T(8,128)}, f32[2,4,32,512]{3,2,1,0:T(8,128)S(1)}, u32[]{:S(2)}, u32[]{:S(2)}) collective-permute-start(f32[2,4,32,512]{3,2,1,0:T(8,128)} %bitcast.3.refs_1_), channel_id=1, source_target_pairs={{0,448},{64,0},{128,64},{192,128},{256,192},{320,256},{384,320},{4... | collective-permute-start | bytes 1572872 | tf_op jit(solution)/shard_map/ppermute | solution.py:213
  46.8 6.8 %collective-permute-done.refs_1_ = f32[2,4,32,512]{3,2,1,0:T(8,128)S(1)} collective-permute-done((f32[2,4,32,512]{3,2,1,0:T(8,128)}, f32[2,4,32,512]{3,2,1,0:T(8,128)S(1)}, u32[]{:S(2)}, u32[]{:S(2)}) %collective-permute-start) | collective-permute-done | bytes 524320 | tf_op jit(solution)/shard_map/ppermute | solution.py:212
  53.6 1.9 %collective-permute-start.1 = (f32[2,4,32,512]{3,2,1,0:T(8,128)S(1)}, f32[2,4,32,512]{3,2,1,0:T(8,128)}, u32[]{:S(2)}, u32[]{:S(2)}) collective-permute-start(f32[2,4,32,512]{3,2,1,0:T(8,128)S(1)} %collective-permute-done.refs_1_), channel_id=1, source_target_pairs={{0,64},{64,128},{128,192},{192,256},{256,320},{320,384},{384,448},... | collective-permute-start | bytes 1572872 | tf_op jit(solution)/shard_map/ppermute | solution.py:212
  55.5 0.0 copy-start
  55.5 0.8 copy-done
  56.3 2.1 %collective-permute-done.2.refs_2_ = f32[2,4,32,512]{3,2,1,0:T(8,128)S(1)} collective-permute-done((f32[2,4,32,512]{3,2,1,0:T(8,128)}, f32[2,4,32,512]{3,2,1,0:T(8,128)S(1)}, u32[]{:S(2)}, u32[]{:S(2)}) %collective-permute-start.2) | collective-permute-done | bytes 524320 | tf_op jit(solution)/shard_map/ppermute | solution.py:213
  58.4 5.2 %collective-permute-start.3 = (f32[2,4,32,512]{3,2,1,0:T(8,128)S(1)}, f32[2,4,32,512]{3,2,1,0:T(8,128)}, u32[]{:S(2)}, u32[]{:S(2)}) collective-permute-start(f32[2,4,32,512]{3,2,1,0:T(8,128)S(1)} %collective-permute-done.2.refs_2_), channel_id=1, source_target_pairs={{0,448},{64,0},{128,64},{192,128},{256,192},{320,256},{384,320},{4... | collective-permute-start | bytes 1572872 | tf_op jit(solution)/shard_map/ppermute | solution.py:213
  63.6 0.0 copy-start.2
  63.6 0.8 copy-done.2
  64.4 0.0 collective-permute-done.4.refs_3_.refs_7_.refs_4_.refs_8_.refs_12_.refs_16_
  64.4 0.0 collective-permute-done.5.refs_4_.refs_8_.refs_5_.refs_9_.refs_13_.refs_17_
  64.4 4.3 %collective-permute-done.1.refs_1_ = f32[2,4,32,512]{3,2,1,0:T(8,128)} collective-permute-done((f32[2,4,32,512]{3,2,1,0:T(8,128)S(1)}, f32[2,4,32,512]{3,2,1,0:T(8,128)}, u32[]{:S(2)}, u32[]{:S(2)}) %collective-permute-start.1) | collective-permute-done | bytes 524320 | tf_op jit(solution)/shard_map/ppermute | solution.py:212
  68.7 5.4 %collective-permute-done.3.refs_2_ = f32[2,4,32,512]{3,2,1,0:T(8,128)} collective-permute-done((f32[2,4,32,512]{3,2,1,0:T(8,128)S(1)}, f32[2,4,32,512]{3,2,1,0:T(8,128)}, u32[]{:S(2)}, u32[]{:S(2)}) %collective-permute-start.3) | collective-permute-done | bytes 524320 | tf_op jit(solution)/shard_map/ppermute | solution.py:213
  74.1 3.6 %collective-permute-start.10 = (f32[16,32,512]{2,1,0:T(8,128)S(1)}, f32[16,32,512]{2,1,0:T(8,128)}, u32[]{:S(2)}, u32[]{:S(2)}) collective-permute-start(f32[16,32,512]{2,1,0:T(8,128)S(1)} %collective-permute-done.4.refs_3_.refs_7_.refs_4_.refs_8_.refs_12_.refs_16_), channel_id=1, source_target_pairs={{0,1},{1,0},{2,3},{3,2},{4,5},{5,4},{6,7},{7,6},{8,9},{9,8},{10,11... | collective-permute-start | bytes 3145736 | tf_op jit(solution)/shard_map/ppermute | solution.py:217
  77.7 1.9 %collective-permute-start.6 = (f32[2,4,32,512]{3,2,1,0:T(8,128)}, f32[2,4,32,512]{3,2,1,0:T(8,128)}, u32[]{:S(2)}, u32[]{:S(2)}) collective-permute-start(f32[2,4,32,512]{3,2,1,0:T(8,128)} %collective-permute-done.1.refs_1_), channel_id=1, source_target_pairs={{0,64},{64,128},{128,192},{192,256},{256,320},{320,384},{384,448},... | collective-permute-start | bytes 1572872 | tf_op jit(solution)/shard_map/ppermute | solution.py:212
  79.6 5.4 %collective-permute-start.8 = (f32[2,4,32,512]{3,2,1,0:T(8,128)}, f32[2,4,32,512]{3,2,1,0:T(8,128)}, u32[]{:S(2)}, u32[]{:S(2)}) collective-permute-start(f32[2,4,32,512]{3,2,1,0:T(8,128)} %collective-permute-done.3.refs_2_), channel_id=1, source_target_pairs={{0,448},{64,0},{128,64},{192,128},{256,192},{320,256},{384,320},{4... | collective-permute-start | bytes 1572872 | tf_op jit(solution)/shard_map/ppermute | solution.py:213
  85.0 0.7 dynamic-slice_bitcast_fusion.1
  85.7 0.7 dynamic-slice_bitcast_fusion
  86.4 0.1 pad_add_fusion.refs_0_
  86.5 9.2 %collective-permute-done.6.refs_1_ = f32[2,4,32,512]{3,2,1,0:T(8,128)} collective-permute-done((f32[2,4,32,512]{3,2,1,0:T(8,128)}, f32[2,4,32,512]{3,2,1,0:T(8,128)}, u32[]{:S(2)}, u32[]{:S(2)}) %collective-permute-start.6) | collective-permute-done | bytes 524320 | tf_op jit(solution)/shard_map/ppermute | solution.py:212
  95.7 1.0 slice.8
  96.6 1.9 %collective-permute-start.7 = (f32[1,4,32,512]{3,2,1,0:T(8,128)S(1)}, f32[1,4,32,512]{3,2,1,0:T(8,128)S(1)}, u32[]{:S(2)}, u32[]{:S(2)}) collective-permute-start(f32[1,4,32,512]{3,2,1,0:T(8,128)S(1)} %slice.8), channel_id=1, source_target_pairs={{0,64},{64,128},{128,192},{192,256},{256,320},{320,384},{384,448},... | collective-permute-start | bytes 786440 | tf_op jit(solution)/shard_map/ppermute | solution.py:218
  98.6 0.0 collective-permute-done.8.refs_2_
  98.6 1.0 slice.9
  99.6 0.0 copy-start.1
  99.6 4.7 %collective-permute-start.9 = (f32[1,4,32,512]{3,2,1,0:T(8,128)S(1)}, f32[1,4,32,512]{3,2,1,0:T(8,128)S(1)}, u32[]{:S(2)}, u32[]{:S(2)}) collective-permute-start(f32[1,4,32,512]{3,2,1,0:T(8,128)S(1)} %slice.9), channel_id=1, source_target_pairs={{0,448},{64,0},{128,64},{192,128},{256,192},{320,256},{384,320},{4... | collective-permute-start | bytes 786440 | tf_op jit(solution)/shard_map/ppermute | solution.py:218
  104.3 0.0 collective-permute-done.10.refs_5_.refs_9_.refs_6_.refs_10_.refs_14_.refs_18_
  104.3 2.2 %shard_map.47.refs_19_ = f32[16,32,512]{2,1,0:T(8,128)S(1)} custom-call(s32[20]{0:T(128)S(1)} %pad_add_fusion.refs_0_, f32[2,4,32,512]{3,2,1,0:T(8,128)} %bitcast.3.refs_1_, f32[16,32,512]{2,1,0:T(8,128)S(1)} %reshape.18.refs_2_.refs_6_.refs_3_.refs_7_.refs_11_.refs_15_, ...), custom_call_target="tpu_custom_call" | custom-call | flops 402653184 | bytes 1048576 | tf_op jit(solution)/shard_map/pallas_call | solution.py:171
  106.5 2.5 %shard_map.48.refs_19_ = f32[16,32,512]{2,1,0:T(8,128)S(1)} custom-call(s32[20]{0:T(128)S(1)} %pad_add_fusion.refs_0_, f32[2,4,32,512]{3,2,1,0:T(8,128)S(1)} %copy-done.1, f32[2,4,32,512]{3,2,1,0:T(8,128)S(1)} %copy-done.3, f32[16,32,512]{2,1,0:T(8,128)S(1)} %reshape.18.refs_2_.refs_6_.refs_3_.refs_7_.refs_11_.refs_15_, ...), custom_call_target="tpu_custom_call" | custom-call | flops 805306368 | bytes 2097152 | tf_op jit(solution)/shard_map/pallas_call | solution.py:171
  109.1 2.8 %shard_map.49.refs_19_ = f32[16,32,512]{2,1,0:T(8,128)S(1)} custom-call(s32[20]{0:T(128)S(1)} %pad_add_fusion.refs_0_, f32[2,4,32,512]{3,2,1,0:T(8,128)} %collective-permute-done.1.refs_1_, f32[2,4,32,512]{3,2,1,0:T(8,128)} %collective-permute-done.3.refs_2_, f32[16,32,512]{2,1,0:T(8,128)S(1)} %reshape.18.refs_2_.refs_6_.refs_3_.refs_7_.refs_11_.refs_15_, ...), custom_call_target="tpu_custom_call" | custom-call | flops 805306368 | bytes 2097152 | tf_op jit(solution)/shard_map/pallas_call | solution.py:171
  111.9 2.8 %shard_map.50.refs_11_ = f32[16,32,512]{2,1,0:T(8,128)S(1)} custom-call(s32[20]{0:T(128)S(1)} %pad_add_fusion.refs_0_, f32[2,4,32,512]{3,2,1,0:T(8,128)} %collective-permute-done.6.refs_1_, f32[2,4,32,512]{3,2,1,0:T(8,128)} %collective-permute-done.8.refs_2_, f32[16,32,512]{2,1,0:T(8,128)S(1)} %reshape.18.refs_2_.refs_6_.refs_3_.refs_7_.refs_11_.refs_15_, ...), custom_call_target="tpu_custom_call" | custom-call | flops 805306368 | bytes 2097152 | tf_op jit(solution)/shard_map/pallas_call | solution.py:171
  114.8 0.0 collective-permute-done.7.refs_1_
  114.8 0.0 collective-permute-done.9.refs_2_
  114.8 2.1 %shard_map.51 = f32[16,32,512]{2,1,0:T(8,128)S(1)} custom-call(s32[20]{0:T(128)S(1)} %pad_add_fusion.refs_0_, f32[1,4,32,512]{3,2,1,0:T(8,128)S(1)} %collective-permute-done.7.refs_1_, f32[1,4,32,512]{3,2,1,0:T(8,128)S(1)} %collective-permute-done.9.refs_2_, f32[16,32,512]{2,1,0:T(8,128)S(1)} %reshape.18.refs_2_.refs_6_.refs_3_.refs_7_.refs_11_.refs_15_, ...), custom_call_target="tpu_custom_call" | custom-call | flops 402653184 | bytes 1048576 | tf_op jit(solution)/shard_map/pallas_call | solution.py:171
  116.8 43.2 %all_to_all.10 = f32[16,32,512]{2,1,0:T(8,128)S(1)} all-to-all(f32[16,32,512]{2,1,0:T(8,128)S(1)} %shard_map.51), channel_id=1, replica_groups={{0,2,4,6,16,18,20,22,32,34,36,38,48,50,52,54},{1,3,5,7,17,19,21,23,33,3..., dimensions={0} | all-to-all | bytes 2097152 | tf_op jit(solution)/shard_map/all_to_all | solution.py:225
  160.0 0.1 reduce_sum.9
  160.1 0.1 reshape.19
  160.2 0.7 copy.8
  (3 shorter events, 0.0 us)
Async XLA Ops:
  4.0 33.4 %all-to-all-start = ((f32[8,32,512]{2,1,0:T(8,128)}), f32[8,32,512]{2,1,0:T(8,128)}, u32[]{:S(2)}, u32[]{:S(2)}) async-start(f32[8,32,512]{2,1,0:T(8,128)} %pad_maximum_fusion), calls=%async_computation | async-start | bytes 1048576 | tf_op jit(solution)/shard_map/all_to_all | solution.py:194
  34.1 30.3 %collective-permute-start.4 = (f32[16,32,512]{2,1,0:T(8,128)S(1)}, f32[16,32,512]{2,1,0:T(8,128)S(1)}, u32[]{:S(2)}, u32[]{:S(2)}) collective-permute-start(f32[16,32,512]{2,1,0:T(8,128)S(1)} %reshape.18.refs_2_.refs_6_.refs_3_.refs_7_.refs_11_.refs_15_), channel_id=1, source_target_pairs={{0,8},{1,9},{2,10},{3,11},{4,12},{5,13},{6,14},{7,15},{8,0},{9,1},... | collective-permute-start | bytes 3145736 | tf_op jit(solution)/shard_map/ppermute | solution.py:204
  37.4 16.1 %collective-permute-start = (f32[2,4,32,512]{3,2,1,0:T(8,128)}, f32[2,4,32,512]{3,2,1,0:T(8,128)S(1)}, u32[]{:S(2)}, u32[]{:S(2)}) collective-permute-start(f32[2,4,32,512]{3,2,1,0:T(8,128)} %bitcast.3.refs_1_), channel_id=1, source_target_pairs={{0,64},{64,128},{128,192},{192,256},{256,320},{320,384},{384,448},... | collective-permute-start | bytes 1572872 | tf_op jit(solution)/shard_map/ppermute | solution.py:212
  39.4 25.1 %collective-permute-start.5 = (f32[16,32,512]{2,1,0:T(8,128)S(1)}, f32[16,32,512]{2,1,0:T(8,128)S(1)}, u32[]{:S(2)}, u32[]{:S(2)}) collective-permute-start(f32[16,32,512]{2,1,0:T(8,128)S(1)} %reshape.18.refs_2_.refs_6_.refs_3_.refs_7_.refs_11_.refs_15_), channel_id=1, source_target_pairs={{0,1},{1,0},{2,3},{3,2},{4,5},{5,4},{6,7},{7,6},{8,9},{9,8},{10,11... | collective-permute-start | bytes 3145736 | tf_op jit(solution)/shard_map/ppermute | solution.py:205
  41.9 16.5 %collective-permute-start.2 = (f32[2,4,32,512]{3,2,1,0:T(8,128)}, f32[2,4,32,512]{3,2,1,0:T(8,128)S(1)}, u32[]{:S(2)}, u32[]{:S(2)}) collective-permute-start(f32[2,4,32,512]{3,2,1,0:T(8,128)} %bitcast.3.refs_1_), channel_id=1, source_target_pairs={{0,448},{64,0},{128,64},{192,128},{256,192},{320,256},{384,320},{4... | collective-permute-start | bytes 1572872 | tf_op jit(solution)/shard_map/ppermute | solution.py:213
  53.6 15.1 %collective-permute-start.1 = (f32[2,4,32,512]{3,2,1,0:T(8,128)S(1)}, f32[2,4,32,512]{3,2,1,0:T(8,128)}, u32[]{:S(2)}, u32[]{:S(2)}) collective-permute-start(f32[2,4,32,512]{3,2,1,0:T(8,128)S(1)} %collective-permute-done.refs_1_), channel_id=1, source_target_pairs={{0,64},{64,128},{128,192},{192,256},{256,320},{320,384},{384,448},... | collective-permute-start | bytes 1572872 | tf_op jit(solution)/shard_map/ppermute | solution.py:212
  55.5 0.8 copy-start
  58.4 15.6 %collective-permute-start.3 = (f32[2,4,32,512]{3,2,1,0:T(8,128)S(1)}, f32[2,4,32,512]{3,2,1,0:T(8,128)}, u32[]{:S(2)}, u32[]{:S(2)}) collective-permute-start(f32[2,4,32,512]{3,2,1,0:T(8,128)S(1)} %collective-permute-done.2.refs_2_), channel_id=1, source_target_pairs={{0,448},{64,0},{128,64},{192,128},{256,192},{320,256},{384,320},{4... | collective-permute-start | bytes 1572872 | tf_op jit(solution)/shard_map/ppermute | solution.py:213
  63.6 0.8 copy-start.2
  74.1 30.2 %collective-permute-start.10 = (f32[16,32,512]{2,1,0:T(8,128)S(1)}, f32[16,32,512]{2,1,0:T(8,128)}, u32[]{:S(2)}, u32[]{:S(2)}) collective-permute-start(f32[16,32,512]{2,1,0:T(8,128)S(1)} %collective-permute-done.4.refs_3_.refs_7_.refs_4_.refs_8_.refs_12_.refs_16_), channel_id=1, source_target_pairs={{0,1},{1,0},{2,3},{3,2},{4,5},{5,4},{6,7},{7,6},{8,9},{9,8},{10,11... | collective-permute-start | bytes 3145736 | tf_op jit(solution)/shard_map/ppermute | solution.py:217
  77.7 18.0 %collective-permute-start.6 = (f32[2,4,32,512]{3,2,1,0:T(8,128)}, f32[2,4,32,512]{3,2,1,0:T(8,128)}, u32[]{:S(2)}, u32[]{:S(2)}) collective-permute-start(f32[2,4,32,512]{3,2,1,0:T(8,128)} %collective-permute-done.1.refs_1_), channel_id=1, source_target_pairs={{0,64},{64,128},{128,192},{192,256},{256,320},{320,384},{384,448},... | collective-permute-start | bytes 1572872 | tf_op jit(solution)/shard_map/ppermute | solution.py:212
  79.6 19.0 %collective-permute-start.8 = (f32[2,4,32,512]{3,2,1,0:T(8,128)}, f32[2,4,32,512]{3,2,1,0:T(8,128)}, u32[]{:S(2)}, u32[]{:S(2)}) collective-permute-start(f32[2,4,32,512]{3,2,1,0:T(8,128)} %collective-permute-done.3.refs_2_), channel_id=1, source_target_pairs={{0,448},{64,0},{128,64},{192,128},{256,192},{320,256},{384,320},{4... | collective-permute-start | bytes 1572872 | tf_op jit(solution)/shard_map/ppermute | solution.py:213
  96.6 18.1 %collective-permute-start.7 = (f32[1,4,32,512]{3,2,1,0:T(8,128)S(1)}, f32[1,4,32,512]{3,2,1,0:T(8,128)S(1)}, u32[]{:S(2)}, u32[]{:S(2)}) collective-permute-start(f32[1,4,32,512]{3,2,1,0:T(8,128)S(1)} %slice.8), channel_id=1, source_target_pairs={{0,64},{64,128},{128,192},{192,256},{256,320},{320,384},{384,448},... | collective-permute-start | bytes 786440 | tf_op jit(solution)/shard_map/ppermute | solution.py:218
  99.6 7.0 %copy-start.1 = (f32[2,4,32,512]{3,2,1,0:T(8,128)S(1)}, f32[2,4,32,512]{3,2,1,0:T(8,128)}, u32[]{:S(2)}) copy-start(f32[2,4,32,512]{3,2,1,0:T(8,128)} %copy-done) | copy-start | bytes 1572868
  99.6 7.0 %copy-start.3 = (f32[2,4,32,512]{3,2,1,0:T(8,128)S(1)}, f32[2,4,32,512]{3,2,1,0:T(8,128)}, u32[]{:S(2)}) copy-start(f32[2,4,32,512]{3,2,1,0:T(8,128)} %copy-done.2) | copy-start | bytes 1572868
  99.6 15.2 %collective-permute-start.9 = (f32[1,4,32,512]{3,2,1,0:T(8,128)S(1)}, f32[1,4,32,512]{3,2,1,0:T(8,128)S(1)}, u32[]{:S(2)}, u32[]{:S(2)}) collective-permute-start(f32[1,4,32,512]{3,2,1,0:T(8,128)S(1)} %slice.9), channel_id=1, source_target_pairs={{0,448},{64,0},{128,64},{192,128},{256,192},{320,256},{384,320},{4... | collective-permute-start | bytes 786440 | tf_op jit(solution)/shard_map/ppermute | solution.py:218

commit v3 on v2

--- a/solution.py
+++ b/solution.py
@@ -58,18 +58,42 @@
 ]
 
 
-CALLS = [[((0, 1), 0)]]
-for _step in range(1, Y // 2):
-    CALLS.append([((0, 1), -_step), ((0, 1), _step)])
-CALLS.append([((0,), Y // 2), ((1,), Y // 2)])
-PLACES = [[(zl, shift) for which, shift in call for zl in which] for call in CALLS]
-SLOTS = sum(len(places) for places in PLACES)
+def low_pair(y):
+    return y ^ 1
+
+
+def high_pair(y):
+    return (y + 1 if y % 2 else y - 1) % Y
+
+
+MEETS = [(low_pair, high_pair), (high_pair, low_pair)]
+
+
+def sources(y):
+    per_half = []
+    for first, second in MEETS:
+        steps = [[lambda q: q], [first]]
+        held = steps[0] + steps[1]
+        for n in range(2, Y // 2 + 1):
+            meet = second if n % 2 == 0 else first
+            held = [lambda q, f=f, meet=meet: f(meet(q)) for f in held]
+            steps.append(held)
+        per_half.append([[f(y) for f in step] for step in steps])
+    zero, one = per_half
+    calls = [[(0, y), (1, y)] + [(0, q) for q in zero[1]] + [(1, q) for q in one[1]]]
+    for n in range(2, Y // 2 + 1):
+        calls.append([(0, q) for q in zero[n]] + [(1, q) for q in one[n]])
+    return calls
+
+
+COUNTS = [len(call) for call in sources(0)]
+SLOTS = sum(COUNTS)
 
 
 def row_table():
     table = np.zeros((ZL * Y, SLOTS), np.int32)
     for row in range(ZL * Y):
-        table[row] = [zl * Y + (row + shift) % Y for places in PLACES for zl, shift in places]
+        table[row] = [zl * Y + q for call in sources(row % Y) for zl, q in call]
     return table
 
 
@@ -112,7 +136,9 @@
         )
         moved = (parts[:rows] + parts[rows : 2 * rows]) + parts[2 * rows :]
         for m in range(MEMBERS):
-            out_ref[m, :, i * width : (i + 1) * width] = moved[:, m * width : (m + 1) * width]
+            piece = moved[:, m * width : (m + 1) * width]
+            for z in range(ZL):
+                out_ref[z * MEMBERS + m, :, i * width : (i + 1) * width] = piece
 
 
 def regroup(t):
@@ -120,7 +146,7 @@
     rows = ks * cs
     return pl.pallas_call(
         regroup_kernel,
-        out_shape=jax.ShapeDtypeStruct((MEMBERS, rows, blocks * virt // MEMBERS), F32),
+        out_shape=jax.ShapeDtypeStruct((ZL * MEMBERS, rows, blocks * virt // MEMBERS), F32),
         cost_estimate=pl.CostEstimate(flops=6 * blocks * rows * virt * virt, bytes_accessed=t.size * 8, transcendentals=0),
     )(t.reshape(blocks, rows, virt))
 
@@ -156,8 +182,8 @@
     rows, width = ts[0].shape[2], ts[0].shape[3]
     wide = ws[0].shape[2]
     out_shape = (PEERS, width // PEERS, wide)
-    first = sum(len(places) for places in PLACES[:at])
-    slots = range(first, first + len(PLACES[at]))
+    first = sum(COUNTS[:at])
+    slots = range(first, first + COUNTS[at])
     in_specs = [pl.BlockSpec(t.shape, lambda z, s: (0, 0, 0, 0)) for t in ts]
     in_specs += [
         pl.BlockSpec((1, rows, wide), lambda z, s, slot=slot: (s[slot], 0, 0)) for slot in slots for _ in ws
@@ -192,7 +218,7 @@
 
     sent = regroup(t_pair)
     own = lax.all_to_all(
-        jnp.concatenate([sent] * ZL), ("row", "col"), 0, 0, tiled=True, axis_index_groups=MEMBER_GROUPS
+        sent, ("row", "col"), 0, 0, tiled=True, axis_index_groups=MEMBER_GROUPS
     ).reshape(ZL, MEMBERS, rows, -1)
 
     depth, wb, kj = w_ovov.shape
@@ -204,18 +230,21 @@
     w_x = lax.ppermute(own_w, "col", swap_x)
     w_c = lax.ppermute(own_w, "col", swap_core)
 
-    up_perm = row_perm(lambda z, q: (z, q + 1))
-    down_perm = row_perm(lambda z, q: (z, q - 1))
+    meets = [[row_perm(lambda z, q, f=f: (z, f(q))) for f in pair] for pair in MEETS]
+    halves = [own[:1], own[1:]]
     got = [(own,)]
-    up = down = own
-    for step in range(1, Y // 2):
-        up = lax.ppermute(up, "row", up_perm)
-        down = lax.ppermute(down, "row", down_perm)
-        got.append((up, down))
+    for step in range(1, Y // 2 + 1):
+        moved = [lax.ppermute(h, "row", meets[n][(step + 1) % 2]) for n, h in enumerate(halves)]
+        if step == 1:
+            got[0] += tuple(moved)
+            halves = [jnp.concatenate([h, m]) for h, m in zip(halves, moved)]
+        else:
+            got.append(tuple(moved))
+            halves = moved
         if step == 2:
-            up, down, w_x, w_c = lax.optimization_barrier((up, down, w_x, w_c))
+            *halves, w_x, w_c = lax.optimization_barrier((*halves, w_x, w_c))
+            got[-1] = tuple(halves)
     w_xc = lax.ppermute(w_x, "col", swap_core)
-    got.append((lax.ppermute(up[:1], "row", up_perm), lax.ppermute(down[1:], "row", down_perm)))
     ws = [own_w, w_x, w_c, w_xc]
 
     acc = None

time: 162 us -> 153 us (0.944)
  starting transfers between devices: 55.5 us -> 46.1 us
  waiting for transfers between devices: 27.7 us -> 32.6 us
  other arithmetic: 2.04 us -> 0.22 us
    ppermute x8, starting transfers between devices: 27.9 us -> 18.5 us  [shards(): lax.ppermute(h, 'row', meets[n][(step + 1) % 2])]
    ppermute x1, waiting for transfers between devices: 0.01 us -> 3.61 us  [shards(): w_x = lax.ppermute(own_w, 'col', swap_x)]
    concatenate x1 -> x2, other arithmetic: 1.89 us -> 0.07 us  [shards(): halves = [jnp.concatenate([h, m]) for h, m in zip(halves, moved)]]
    pallas_call x5 -> x4, Pallas kernels: 12.5 us -> 10.9 us  [multiply(): pl.pallas_call(functools.partial(multiply_kernel, acc is not None, blocks...]
    unnamed x9 -> x5, local copies, waits for them, and re-layouts: 5.19 us -> 4.56 us
  transfers between devices with their start and end apart: 12 -> 12, of which waited for: 5 -> 8; matrix products, arithmetic and copies ran while one was open for 10% -> 10% of each run, Pallas kernels for 6% -> 6%
where the time goes in v3:
time: 153 us; the launch traced here: 152 us
  starting transfers between devices  46.1 us (30%)
  blocking collectives  43.6 us (28%)
  waiting for transfers between devices  32.6 us (21%)
  local copies, waits for them, and re-layouts  16.2 us (11%)
  Pallas kernels  13.1 us (9%)
    all_to_all x1, blocking collectives, shards(): lax.all_to_all(acc, 'col', 0, 0, tiled=True, axis_index_groups=PEER_GROUPS)  43.6 us
    ppermute x8, waiting for transfers between devices, shards(): lax.ppermute(h, 'row', meets[n][(step + 1) % 2])  29 us
    ppermute x8, starting transfers between devices, shards(): lax.ppermute(h, 'row', meets[n][(step + 1) % 2])  18.5 us
    all_to_all x1, starting transfers between devices, shards(): lax.all_to_all(sent, ('row', 'col'), 0, 0, tiled=True, axis_index_groups=...  18.2 us
    pallas_call x4, Pallas kernels, multiply(): pl.pallas_call(functools.partial(multiply_kernel, acc is not None, blocks...  10.9 us
    transpose x1, local copies, waits for them, and re-layouts, shards(): w_ovov.reshape(cs, wb, occupied, pairs).transpose(2, 0, 3, 1)  4.78 us
    unnamed x5, local copies, waits for them, and re-layouts  4.56 us
    ppermute x1, waiting for transfers between devices, shards(): w_x = lax.ppermute(own_w, 'col', swap_x)  3.61 us
  transfers between devices with their start and end apart: 12, of which 8 were waited for; matrix products, arithmetic and copies ran while one was open for 10% of the time, Pallas kernels for 6%

profile of v3, /device:TPU:1, one launch (start us, length us, event | category | flops | bytes accessed | tf_op | source)
XLA Modules:
  0.0 152.1 jit_solution(16289831679644756202)
XLA Ops:
  0.0 2.3 %shard_map.46 = f32[8,32,512]{2,1,0:T(8,128)} custom-call(f32[4,32,512]{2,1,0:T(8,128)} %bitcast.18), custom_call_target="tpu_custom_call" | custom-call | flops 201326592 | bytes 524288 | tf_op jit(solution)/shard_map/pallas_call | solution.py:147
  2.3 18.2 %all-to-all-start = ((f32[8,32,512]{2,1,0:T(8,128)}), f32[8,32,512]{2,1,0:T(8,128)}, u32[]{:S(2)}, u32[]{:S(2)}) async-start(f32[8,32,512]{2,1,0:T(8,128)} %shard_map.46), calls=%async_computation | async-start | bytes 1048576 | tf_op jit(solution)/shard_map/all_to_all | solution.py:220
  20.4 3.6 %copy.6 = f32[8,32,1024]{1,2,0:T(8,128)} copy(f32[8,32,1024]{2,1,0:T(8,128)} %param.5) | data formatting | bytes 2097152 | tf_op args[1]
  24.0 4.8 %copy.7 = f32[64,8,16,32]{3,2,1,0:T(8,128)} copy(f32[64,8,16,32]{3,2,0,1:T(8,128)} %bitcast.16) | data formatting | bytes 2097152 | tf_op jit(solution)/shard_map/transpose | solution.py:227
  28.8 3.5 %reshape.19.refs_4_.refs_8_.refs_12_.refs_16_.refs_3_.refs_7_.refs_11_.refs_15_ = f32[16,32,512]{2,1,0:T(8,128)S(1)} reshape(f32[64,8,16,32]{3,2,1,0:T(8,128)} %copy.7) | data formatting | bytes 2097152 | tf_op jit(solution)/shard_map/reshape | solution.py:227
  32.4 3.3 %collective-permute-start.4 = (f32[16,32,512]{2,1,0:T(8,128)S(1)}, f32[16,32,512]{2,1,0:T(8,128)S(1)}, u32[]{:S(2)}, u32[]{:S(2)}) collective-permute-start(f32[16,32,512]{2,1,0:T(8,128)S(1)} %reshape.19.refs_4_.refs_8_.refs_12_.refs_16_.refs_3_.refs_7_.refs_11_.refs_15_), channel_id=1, source_target_pairs={{0,8},{1,9},{2,10},{3,11},{4,12},{5,13},{6,14},{7,15},{8,0},{9,1},... | collective-permute-start | bytes 3145736 | tf_op jit(solution)/shard_map/ppermute | solution.py:230
  35.7 2.5 %collective-permute-start.5 = (f32[16,32,512]{2,1,0:T(8,128)S(1)}, f32[16,32,512]{2,1,0:T(8,128)S(1)}, u32[]{:S(2)}, u32[]{:S(2)}) collective-permute-start(f32[16,32,512]{2,1,0:T(8,128)S(1)} %reshape.19.refs_4_.refs_8_.refs_12_.refs_16_.refs_3_.refs_7_.refs_11_.refs_15_), channel_id=1, source_target_pairs={{0,1},{1,0},{2,3},{3,2},{4,5},{5,4},{6,7},{7,6},{8,9},{9,8},{10,11... | collective-permute-start | bytes 3145736 | tf_op jit(solution)/shard_map/ppermute | solution.py:231
  38.2 0.0 all-to-all-done
  38.2 1.1 slice_bitcast_fusion
  39.3 1.9 %collective-permute-start.2 = (f32[1,4,32,512]{3,2,1,0:T(8,128)S(1)}, f32[1,4,32,512]{3,2,1,0:T(8,128)S(1)}, u32[]{:S(2)}, u32[]{:S(2)}) collective-permute-start(f32[1,4,32,512]{3,2,1,0:T(8,128)S(1)} %get-tuple-element.13), channel_id=1, source_target_pairs={{0,448},{64,128},{128,64},{192,256},{256,192},{320,384},{384,320},... | collective-permute-start | bytes 786440 | tf_op jit(solution)/shard_map/ppermute | solution.py:237
  41.3 1.9 %collective-permute-start = (f32[1,4,32,512]{3,2,1,0:T(8,128)S(1)}, f32[1,4,32,512]{3,2,1,0:T(8,128)S(1)}, u32[]{:S(2)}, u32[]{:S(2)}) collective-permute-start(f32[1,4,32,512]{3,2,1,0:T(8,128)S(1)} %get-tuple-element.14), channel_id=1, source_target_pairs={{0,64},{64,0},{128,192},{192,128},{256,320},{320,256},{384,448},{4... | collective-permute-start | bytes 786440 | tf_op jit(solution)/shard_map/ppermute | solution.py:237
  43.2 7.2 %collective-permute-done.2.refs_3_ = f32[1,4,32,512]{3,2,1,0:T(8,128)S(1)} collective-permute-done((f32[1,4,32,512]{3,2,1,0:T(8,128)S(1)}, f32[1,4,32,512]{3,2,1,0:T(8,128)S(1)}, u32[]{:S(2)}, u32[]{:S(2)}) %collective-permute-start.2) | collective-permute-done | bytes 262176 | tf_op jit(solution)/shard_map/ppermute | solution.py:237
  50.4 1.9 %collective-permute-start.3 = (f32[2,4,32,512]{3,2,1,0:T(8,128)S(1)}, f32[2,4,32,512]{3,2,1,0:T(8,128)}, u32[]{:S(2)}, u32[]{:S(2)}) collective-permute-start(f32[2,4,32,512]{3,2,1,0:T(8,128)S(1)} %pad_maximum_fusion.1), channel_id=1, source_target_pairs={{0,64},{64,0},{128,192},{192,128},{256,320},{320,256},{384,448},{4... | collective-permute-start | bytes 1572872 | tf_op jit(solution)/shard_map/ppermute | solution.py:237
  52.3 0.0 collective-permute-done.refs_2_
  52.3 0.0 copy-start
  52.4 3.0 %collective-permute-start.1 = (f32[2,4,32,512]{3,2,1,0:T(8,128)S(1)}, f32[2,4,32,512]{3,2,1,0:T(8,128)}, u32[]{:S(2)}, u32[]{:S(2)}) collective-permute-start(f32[2,4,32,512]{3,2,1,0:T(8,128)S(1)} %pad_maximum_fusion), channel_id=1, source_target_pairs={{0,448},{64,128},{128,64},{192,256},{256,192},{320,384},{384,320},... | collective-permute-start | bytes 1572872 | tf_op jit(solution)/shard_map/ppermute | solution.py:237
  55.4 3.6 %collective-permute-done.4.refs_5_.refs_9_.refs_13_.refs_17_.refs_4_.refs_8_.refs_12_.refs_16_ = f32[16,32,512]{2,1,0:T(8,128)S(1)} collective-permute-done((f32[16,32,512]{2,1,0:T(8,128)S(1)}, f32[16,32,512]{2,1,0:T(8,128)S(1)}, u32[]{:S(2)}, u32[]{:S(2)}) %collective-permute-start.4) | collective-permute-done | bytes 1048608 | tf_op jit(solution)/shard_map/ppermute | solution.py:230
  59.0 0.0 collective-permute-done.5.refs_6_.refs_10_.refs_14_.refs_18_.refs_5_.refs_9_.refs_13_.refs_17_
  59.0 6.1 %collective-permute-done.3.refs_2_ = f32[2,4,32,512]{3,2,1,0:T(8,128)} collective-permute-done((f32[2,4,32,512]{3,2,1,0:T(8,128)S(1)}, f32[2,4,32,512]{3,2,1,0:T(8,128)}, u32[]{:S(2)}, u32[]{:S(2)}) %collective-permute-start.3) | collective-permute-done | bytes 524320 | tf_op jit(solution)/shard_map/ppermute | solution.py:237
  65.1 0.0 copy-done
  65.1 3.2 %collective-permute-done.1.refs_1_ = f32[2,4,32,512]{3,2,1,0:T(8,128)} collective-permute-done((f32[2,4,32,512]{3,2,1,0:T(8,128)S(1)}, f32[2,4,32,512]{3,2,1,0:T(8,128)}, u32[]{:S(2)}, u32[]{:S(2)}) %collective-permute-start.1) | collective-permute-done | bytes 524320 | tf_op jit(solution)/shard_map/ppermute | solution.py:237
  68.3 3.6 %collective-permute-start.10 = (f32[16,32,512]{2,1,0:T(8,128)S(1)}, f32[16,32,512]{2,1,0:T(8,128)}, u32[]{:S(2)}, u32[]{:S(2)}) collective-permute-start(f32[16,32,512]{2,1,0:T(8,128)S(1)} %collective-permute-done.4.refs_5_.refs_9_.refs_13_.refs_17_.refs_4_.refs_8_.refs_12_.refs_16_), channel_id=1, source_target_pairs={{0,1},{1,0},{2,3},{3,2},{4,5},{5,4},{6,7},{7,6},{8,9},{9,8},{10,11... | collective-permute-start | bytes 3145736 | tf_op jit(solution)/shard_map/ppermute | solution.py:247
  71.8 2.2 %collective-permute-start.6 = (f32[2,4,32,512]{3,2,1,0:T(8,128)}, f32[2,4,32,512]{3,2,1,0:T(8,128)}, u32[]{:S(2)}, u32[]{:S(2)}) collective-permute-start(f32[2,4,32,512]{3,2,1,0:T(8,128)} %collective-permute-done.1.refs_1_), channel_id=1, source_target_pairs={{0,64},{64,0},{128,192},{192,128},{256,320},{320,256},{384,448},{4... | collective-permute-start | bytes 1572872 | tf_op jit(solution)/shard_map/ppermute | solution.py:237
  74.0 2.7 %collective-permute-start.8 = (f32[2,4,32,512]{3,2,1,0:T(8,128)}, f32[2,4,32,512]{3,2,1,0:T(8,128)}, u32[]{:S(2)}, u32[]{:S(2)}) collective-permute-start(f32[2,4,32,512]{3,2,1,0:T(8,128)} %collective-permute-done.3.refs_2_), channel_id=1, source_target_pairs={{0,448},{64,128},{128,64},{192,256},{256,192},{320,384},{384,320},... | collective-permute-start | bytes 1572872 | tf_op jit(solution)/shard_map/ppermute | solution.py:237
  76.8 10.8 %collective-permute-done.6.refs_1_ = f32[2,4,32,512]{3,2,1,0:T(8,128)} collective-permute-done((f32[2,4,32,512]{3,2,1,0:T(8,128)}, f32[2,4,32,512]{3,2,1,0:T(8,128)}, u32[]{:S(2)}, u32[]{:S(2)}) %collective-permute-start.6) | collective-permute-done | bytes 524320 | tf_op jit(solution)/shard_map/ppermute | solution.py:237
  87.6 3.0 %collective-permute-start.7 = (f32[2,4,32,512]{3,2,1,0:T(8,128)}, f32[2,4,32,512]{3,2,1,0:T(8,128)S(1)}, u32[]{:S(2)}, u32[]{:S(2)}) collective-permute-start(f32[2,4,32,512]{3,2,1,0:T(8,128)} %collective-permute-done.6.refs_1_), channel_id=1, source_target_pairs={{0,448},{64,128},{128,64},{192,256},{256,192},{320,384},{384,320},... | collective-permute-start | bytes 1572872 | tf_op jit(solution)/shard_map/ppermute | solution.py:237
  90.6 0.1 collective-permute-done.8.refs_2_
  90.7 1.9 %collective-permute-start.9 = (f32[2,4,32,512]{3,2,1,0:T(8,128)}, f32[2,4,32,512]{3,2,1,0:T(8,128)S(1)}, u32[]{:S(2)}, u32[]{:S(2)}) collective-permute-start(f32[2,4,32,512]{3,2,1,0:T(8,128)} %collective-permute-done.8.refs_2_), channel_id=1, source_target_pairs={{0,64},{64,0},{128,192},{192,128},{256,320},{320,256},{384,448},{4... | collective-permute-start | bytes 1572872 | tf_op jit(solution)/shard_map/ppermute | solution.py:237
  92.6 0.7 dynamic-slice_bitcast_fusion.1
  93.3 0.7 dynamic-slice_bitcast_fusion
  94.0 0.1 pad_add_fusion.refs_0_
  94.0 0.0 collective-permute-done.10.refs_7_.refs_11_.refs_15_.refs_19_.refs_6_.refs_10_.refs_14_.refs_18_
  94.0 0.0 copy-start.1
  94.0 0.9 copy-done.1
  95.0 2.7 %shard_map.47.refs_19_ = f32[16,32,512]{2,1,0:T(8,128)S(1)} custom-call(s32[20]{0:T(128)S(1)} %pad_add_fusion.refs_0_, f32[2,4,32,512]{3,2,1,0:T(8,128)} %bitcast.7.refs_1_, f32[1,4,32,512]{3,2,1,0:T(8,128)S(1)} %copy-done.1, f32[1,4,32,512]{3,2,1,0:T(8,128)S(1)} %collective-permute-done.2.refs_3_, ...), custom_call_target="tpu_custom_call" | custom-call | flops 805306368 | bytes 2097152 | tf_op jit(solution)/shard_map/pallas_call | solution.py:197
  97.7 2.8 %shard_map.48.refs_19_ = f32[16,32,512]{2,1,0:T(8,128)S(1)} custom-call(s32[20]{0:T(128)S(1)} %pad_add_fusion.refs_0_, f32[2,4,32,512]{3,2,1,0:T(8,128)} %collective-permute-done.1.refs_1_, f32[2,4,32,512]{3,2,1,0:T(8,128)} %collective-permute-done.3.refs_2_, f32[16,32,512]{2,1,0:T(8,128)S(1)} %reshape.19.refs_4_.refs_8_.refs_12_.refs_16_.refs_3_.refs_7_.refs_11_.refs_15_, ...), custom_call_target="tpu_custom_call" | custom-call | flops 805306368 | bytes 2097152 | tf_op jit(solution)/shard_map/pallas_call | solution.py:197
  100.6 2.8 %shard_map.49.refs_19_ = f32[16,32,512]{2,1,0:T(8,128)S(1)} custom-call(s32[20]{0:T(128)S(1)} %pad_add_fusion.refs_0_, f32[2,4,32,512]{3,2,1,0:T(8,128)} %collective-permute-done.6.refs_1_, f32[2,4,32,512]{3,2,1,0:T(8,128)} %collective-permute-done.8.refs_2_, f32[16,32,512]{2,1,0:T(8,128)S(1)} %reshape.19.refs_4_.refs_8_.refs_12_.refs_16_.refs_3_.refs_7_.refs_11_.refs_15_, ...), custom_call_target="tpu_custom_call" | custom-call | flops 805306368 | bytes 2097152 | tf_op jit(solution)/shard_map/pallas_call | solution.py:197
  103.4 0.2 collective-permute-done.7.refs_1_
  103.6 1.5 collective-permute-done.9.refs_2_
  105.1 2.5 %shard_map.50 = f32[16,32,512]{2,1,0:T(8,128)S(1)} custom-call(s32[20]{0:T(128)S(1)} %pad_add_fusion.refs_0_, f32[2,4,32,512]{3,2,1,0:T(8,128)S(1)} %collective-permute-done.7.refs_1_, f32[2,4,32,512]{3,2,1,0:T(8,128)S(1)} %collective-permute-done.9.refs_2_, f32[16,32,512]{2,1,0:T(8,128)S(1)} %reshape.19.refs_4_.refs_8_.refs_12_.refs_16_.refs_3_.refs_7_.refs_11_.refs_15_, ...), custom_call_target="tpu_custom_call" | custom-call | flops 805306368 | bytes 2097152 | tf_op jit(solution)/shard_map/pallas_call | solution.py:197
  107.5 43.6 %all_to_all.10 = f32[16,32,512]{2,1,0:T(8,128)S(1)} all-to-all(f32[16,32,512]{2,1,0:T(8,128)S(1)} %shard_map.50), channel_id=1, replica_groups={{0,2,4,6,16,18,20,22,32,34,36,38,48,50,52,54},{1,3,5,7,17,19,21,23,33,3..., dimensions={0} | all-to-all | bytes 2097152 | tf_op jit(solution)/shard_map/all_to_all | solution.py:254
  151.1 0.1 reduce_sum.9
  151.2 0.1 reshape.21
  151.3 0.7 copy.8
  (2 shorter events, 0.1 us)
Async XLA Ops:
  2.3 36.0 %all-to-all-start = ((f32[8,32,512]{2,1,0:T(8,128)}), f32[8,32,512]{2,1,0:T(8,128)}, u32[]{:S(2)}, u32[]{:S(2)}) async-start(f32[8,32,512]{2,1,0:T(8,128)} %shard_map.46), calls=%async_computation | async-start | bytes 1048576 | tf_op jit(solution)/shard_map/all_to_all | solution.py:220
  32.4 26.6 %collective-permute-start.4 = (f32[16,32,512]{2,1,0:T(8,128)S(1)}, f32[16,32,512]{2,1,0:T(8,128)S(1)}, u32[]{:S(2)}, u32[]{:S(2)}) collective-permute-start(f32[16,32,512]{2,1,0:T(8,128)S(1)} %reshape.19.refs_4_.refs_8_.refs_12_.refs_16_.refs_3_.refs_7_.refs_11_.refs_15_), channel_id=1, source_target_pairs={{0,8},{1,9},{2,10},{3,11},{4,12},{5,13},{6,14},{7,15},{8,0},{9,1},... | collective-permute-start | bytes 3145736 | tf_op jit(solution)/shard_map/ppermute | solution.py:230
  35.7 23.3 %collective-permute-start.5 = (f32[16,32,512]{2,1,0:T(8,128)S(1)}, f32[16,32,512]{2,1,0:T(8,128)S(1)}, u32[]{:S(2)}, u32[]{:S(2)}) collective-permute-start(f32[16,32,512]{2,1,0:T(8,128)S(1)} %reshape.19.refs_4_.refs_8_.refs_12_.refs_16_.refs_3_.refs_7_.refs_11_.refs_15_), channel_id=1, source_target_pairs={{0,1},{1,0},{2,3},{3,2},{4,5},{5,4},{6,7},{7,6},{8,9},{9,8},{10,11... | collective-permute-start | bytes 3145736 | tf_op jit(solution)/shard_map/ppermute | solution.py:231
  39.3 11.0 %collective-permute-start.2 = (f32[1,4,32,512]{3,2,1,0:T(8,128)S(1)}, f32[1,4,32,512]{3,2,1,0:T(8,128)S(1)}, u32[]{:S(2)}, u32[]{:S(2)}) collective-permute-start(f32[1,4,32,512]{3,2,1,0:T(8,128)S(1)} %get-tuple-element.13), channel_id=1, source_target_pairs={{0,448},{64,128},{128,64},{192,256},{256,192},{320,384},{384,320},... | collective-permute-start | bytes 786440 | tf_op jit(solution)/shard_map/ppermute | solution.py:237
  41.3 11.1 %collective-permute-start = (f32[1,4,32,512]{3,2,1,0:T(8,128)S(1)}, f32[1,4,32,512]{3,2,1,0:T(8,128)S(1)}, u32[]{:S(2)}, u32[]{:S(2)}) collective-permute-start(f32[1,4,32,512]{3,2,1,0:T(8,128)S(1)} %get-tuple-element.14), channel_id=1, source_target_pairs={{0,64},{64,0},{128,192},{192,128},{256,320},{320,256},{384,448},{4... | collective-permute-start | bytes 786440 | tf_op jit(solution)/shard_map/ppermute | solution.py:237
  50.4 14.7 %collective-permute-start.3 = (f32[2,4,32,512]{3,2,1,0:T(8,128)S(1)}, f32[2,4,32,512]{3,2,1,0:T(8,128)}, u32[]{:S(2)}, u32[]{:S(2)}) collective-permute-start(f32[2,4,32,512]{3,2,1,0:T(8,128)S(1)} %pad_maximum_fusion.1), channel_id=1, source_target_pairs={{0,64},{64,0},{128,192},{192,128},{256,320},{320,256},{384,448},{4... | collective-permute-start | bytes 1572872 | tf_op jit(solution)/shard_map/ppermute | solution.py:237
  52.3 12.7 %copy-start = (f32[1,4,32,512]{3,2,1,0:T(8,128)}, f32[1,4,32,512]{3,2,1,0:T(8,128)S(1)}, u32[]{:S(2)}) copy-start(f32[1,4,32,512]{3,2,1,0:T(8,128)S(1)} %collective-permute-done.refs_2_) | copy-start | bytes 786436
  52.4 15.9 %collective-permute-start.1 = (f32[2,4,32,512]{3,2,1,0:T(8,128)S(1)}, f32[2,4,32,512]{3,2,1,0:T(8,128)}, u32[]{:S(2)}, u32[]{:S(2)}) collective-permute-start(f32[2,4,32,512]{3,2,1,0:T(8,128)S(1)} %pad_maximum_fusion), channel_id=1, source_target_pairs={{0,448},{64,128},{128,64},{192,256},{256,192},{320,384},{384,320},... | collective-permute-start | bytes 1572872 | tf_op jit(solution)/shard_map/ppermute | solution.py:237
  68.3 25.8 %collective-permute-start.10 = (f32[16,32,512]{2,1,0:T(8,128)S(1)}, f32[16,32,512]{2,1,0:T(8,128)}, u32[]{:S(2)}, u32[]{:S(2)}) collective-permute-start(f32[16,32,512]{2,1,0:T(8,128)S(1)} %collective-permute-done.4.refs_5_.refs_9_.refs_13_.refs_17_.refs_4_.refs_8_.refs_12_.refs_16_), channel_id=1, source_target_pairs={{0,1},{1,0},{2,3},{3,2},{4,5},{5,4},{6,7},{7,6},{8,9},{9,8},{10,11... | collective-permute-start | bytes 3145736 | tf_op jit(solution)/shard_map/ppermute | solution.py:247
  71.8 15.8 %collective-permute-start.6 = (f32[2,4,32,512]{3,2,1,0:T(8,128)}, f32[2,4,32,512]{3,2,1,0:T(8,128)}, u32[]{:S(2)}, u32[]{:S(2)}) collective-permute-start(f32[2,4,32,512]{3,2,1,0:T(8,128)} %collective-permute-done.1.refs_1_), channel_id=1, source_target_pairs={{0,64},{64,0},{128,192},{192,128},{256,320},{320,256},{384,448},{4... | collective-permute-start | bytes 1572872 | tf_op jit(solution)/shard_map/ppermute | solution.py:237
  74.0 16.6 %collective-permute-start.8 = (f32[2,4,32,512]{3,2,1,0:T(8,128)}, f32[2,4,32,512]{3,2,1,0:T(8,128)}, u32[]{:S(2)}, u32[]{:S(2)}) collective-permute-start(f32[2,4,32,512]{3,2,1,0:T(8,128)} %collective-permute-done.3.refs_2_), channel_id=1, source_target_pairs={{0,448},{64,128},{128,64},{192,256},{256,192},{320,384},{384,320},... | collective-permute-start | bytes 1572872 | tf_op jit(solution)/shard_map/ppermute | solution.py:237
  87.6 16.0 %collective-permute-start.7 = (f32[2,4,32,512]{3,2,1,0:T(8,128)}, f32[2,4,32,512]{3,2,1,0:T(8,128)S(1)}, u32[]{:S(2)}, u32[]{:S(2)}) collective-permute-start(f32[2,4,32,512]{3,2,1,0:T(8,128)} %collective-permute-done.6.refs_1_), channel_id=1, source_target_pairs={{0,448},{64,128},{128,64},{192,256},{256,192},{320,384},{384,320},... | collective-permute-start | bytes 1572872 | tf_op jit(solution)/shard_map/ppermute | solution.py:237
  90.7 14.4 %collective-permute-start.9 = (f32[2,4,32,512]{3,2,1,0:T(8,128)}, f32[2,4,32,512]{3,2,1,0:T(8,128)S(1)}, u32[]{:S(2)}, u32[]{:S(2)}) collective-permute-start(f32[2,4,32,512]{3,2,1,0:T(8,128)} %collective-permute-done.8.refs_2_), channel_id=1, source_target_pairs={{0,64},{64,0},{128,192},{192,128},{256,320},{320,256},{384,448},{4... | collective-permute-start | bytes 1572872 | tf_op jit(solution)/shard_map/ppermute | solution.py:237
  94.0 1.0 copy-start.1

commit v4 on v3

--- a/solution.py
+++ b/solution.py
@@ -10,10 +10,10 @@
 
 X, ZH, CORES = 8, 4, 2
 ZL, Y = 2, 8
-GX = 2
-XH = X // GX
-MEMBERS = GX * CORES
-PEERS = XH * ZH
+GX, GZ = 1, 2
+XH, ZG = X // GX, ZH // GZ
+MEMBERS = GX * GZ * CORES
+PEERS = XH * ZG
 F32 = jnp.float32
 BF16 = jnp.bfloat16
 
@@ -40,22 +40,16 @@
     return pairs
 
 
+GROUP = [(xl, zm, core) for xl in range(GX) for zm in range(GZ) for core in range(CORES)]
+BASES = [(xh * GX, zg * GZ) for xh in range(XH) for zg in range(ZG)]
 MEMBER_GROUPS = [
-    [
-        (zl * Y + y) * (X * ZH * CORES) + col_of(xh * GX + xl, zh, core)
-        for zl in range(ZL)
-        for xl in range(GX)
-        for core in range(CORES)
-    ]
+    [(zl * Y + y) * (X * ZH * CORES) + col_of(x + xl, zh + zm, core) for zl in range(ZL) for xl, zm, core in GROUP]
     for y in range(Y)
-    for xh in range(XH)
-    for zh in range(ZH)
+    for x, zh in BASES
 ]
-PEER_GROUPS = [
-    [col_of(xh * GX + xl, zh, core) for xh in range(XH) for zh in range(ZH)]
-    for xl in range(GX)
-    for core in range(CORES)
-]
+PEER_GROUPS = [[col_of(x + xl, zh + zm, core) for x, zh in BASES] for xl, zm, core in GROUP]
+NEAR = [(dx, dz) for dx in range(GX) for dz in range(GZ)]
+FROM = [(dx, dz, dc) for dc in range(CORES) for dx, dz in NEAR]
 
 
 def low_pair(y):
@@ -90,6 +84,16 @@
 SLOTS = sum(COUNTS)
 
 
+HOLD = 3
+EVERY = list(range(MEMBERS))
+LATE = [n for n, (dx, dz, dc) in enumerate(FROM) if dx + dz == 2]
+EARLY = [n for n in EVERY if n not in LATE]
+if LATE:
+    PLAN = [((0,), EARLY), ((1,), EARLY), ((2,), EARLY), ((0, 1, 2), LATE), ((3,), EVERY)]
+else:
+    PLAN = [((n,), EVERY) for n in range(len(COUNTS))]
+
+
 def row_table():
     table = np.zeros((ZL * Y, SLOTS), np.int32)
     for row in range(ZL * Y):
@@ -100,10 +104,8 @@
 def col_table():
     table = np.zeros((X * ZH * CORES, MEMBERS), np.int32)
     for col in range(table.shape[0]):
-        x, core = col // (ZH * CORES), col % CORES
-        for n in range(MEMBERS):
-            source = (x - n % GX) % GX
-            table[col, n] = source * CORES + (core if n < GX else 1 - core)
+        x, zh, core = col // (ZH * CORES) % GX, col // CORES % GZ, col % CORES
+        table[col] = [((x ^ dx) * GZ + (zh ^ dz)) * CORES + (core ^ dc) for dx, dz, dc in FROM]
     return table
 
 
@@ -113,16 +115,17 @@
 
 
 def regroup_kernel(t_ref, out_ref):
-    blocks, rows, virt = t_ref.shape[0], t_ref.shape[1], t_ref.shape[2]
+    blocks, rows, virt = t_ref.shape
     run = virt // (X * ZH * CORES)
     src = lax.broadcasted_iota(jnp.int32, (virt, virt), 0)
     dst = lax.broadcasted_iota(jnp.int32, (virt, virt), 1)
     r = dst % run
-    zh = (dst // run) % ZH
-    xh = (dst // (run * ZH)) % XH
-    core = (dst // (run * ZH * XH)) % CORES
-    xl = dst // (run * ZH * XH * CORES)
-    want = ((((xh * GX + xl) * ZH + zh) * CORES) + core) * run + r
+    zg = (dst // run) % ZG
+    xh = (dst // (run * ZG)) % XH
+    core = (dst // (run * PEERS)) % CORES
+    zm = (dst // (run * PEERS * CORES)) % GZ
+    xl = dst // (run * PEERS * CORES * GZ)
+    want = (((((xh * GX + xl) * ZG + zg) * GZ + zm) * CORES) + core) * run + r
     onehot = jnp.where(src == want, 1.0, 0.0).astype(BF16)
     width = virt // MEMBERS
     for i in range(blocks):
@@ -151,13 +154,13 @@
     )(t.reshape(blocks, rows, virt))
 
 
-def multiply_kernel(has_acc, blocks, order_at, n_t, n_w, *refs):
+def multiply_kernel(has_acc, blocks, picks, n_t, n_w, *refs):
     s_ref = refs[0]
     t_refs = refs[1 : 1 + n_t]
     w_refs = refs[1 + n_t : 1 + n_t + n_w]
     out_ref = refs[-1]
     left = jnp.concatenate(
-        [t[z, s_ref[order_at + n]] for t in t_refs for z in range(t.shape[0]) for n in range(MEMBERS)], axis=0
+        [t[z, s_ref[SLOTS + n]] for t in t_refs for z in range(t.shape[0]) for n in picks], axis=0
     )
     right = jnp.concatenate([w[0] for w in w_refs], axis=0)
     lh, ll = split2(left)
@@ -178,12 +181,12 @@
             out_ref[:, rows, :] = total[i]
 
 
-def multiply(scalars, at, ts, ws, acc, blocks):
+def multiply(scalars, at, ts, ws, picks, acc, blocks):
+    ws = [ws[n] for n in picks]
     rows, width = ts[0].shape[2], ts[0].shape[3]
     wide = ws[0].shape[2]
     out_shape = (PEERS, width // PEERS, wide)
-    first = sum(COUNTS[:at])
-    slots = range(first, first + COUNTS[at])
+    slots = [sum(COUNTS[:n]) + m for n in at for m in range(COUNTS[n])]
     in_specs = [pl.BlockSpec(t.shape, lambda z, s: (0, 0, 0, 0)) for t in ts]
     in_specs += [
         pl.BlockSpec((1, rows, wide), lambda z, s, slot=slot: (s[slot], 0, 0)) for slot in slots for _ in ws
@@ -195,7 +198,7 @@
         args.append(acc)
     depth = len(slots) * len(ws) * rows
     return pl.pallas_call(
-        functools.partial(multiply_kernel, acc is not None, blocks, SLOTS, len(ts), len(slots) * len(ws)),
+        functools.partial(multiply_kernel, acc is not None, blocks, picks, len(ts), len(slots) * len(ws)),
         grid_spec=pltpu.PrefetchScalarGridSpec(num_scalar_prefetch=1, grid=(1,), in_specs=in_specs, out_specs=whole),
         out_shape=jax.ShapeDtypeStruct(out_shape, F32),
         compiler_params=pltpu.CompilerParams(vmem_limit_bytes=32 * 2**20),
@@ -224,32 +227,48 @@
     depth, wb, kj = w_ovov.shape
     occupied = ks * ZL * Y
     pairs = kj // occupied
-    own_w = w_ovov.reshape(cs, wb, occupied, pairs).transpose(2, 0, 3, 1).reshape(ZL * Y, rows, pairs * wb)
-    swap_core = col_perm(lambda x, zh, c: (x, zh, 1 - c))
+    w_t = w_ovov.reshape(cs, wb, occupied, pairs).transpose(2, 0, 3, 1)
+    own_w = w_t.reshape(ZL * Y, rows, pairs * wb)
+    swap_core = col_perm(lambda x, zh, c: (x, zh, c ^ 1))
     swap_x = col_perm(lambda x, zh, c: (x ^ 1, zh, c))
-    w_x = lax.ppermute(own_w, "col", swap_x)
-    w_c = lax.ppermute(own_w, "col", swap_core)
+    swap_z = col_perm(lambda x, zh, c: (x, zh ^ 1, c))
 
     meets = [[row_perm(lambda z, q, f=f: (z, f(q))) for f in pair] for pair in MEETS]
     halves = [own[:1], own[1:]]
     got = [(own,)]
+    near = {(0, 0): own_w}
+    far = {}
     for step in range(1, Y // 2 + 1):
         moved = [lax.ppermute(h, "row", meets[n][(step + 1) % 2]) for n, h in enumerate(halves)]
         if step == 1:
+            if GZ == 2:
+                near[0, 1] = lax.ppermute(own_w, "col", swap_z)
+            if GX == 2:
+                near[1, 0] = lax.ppermute(own_w, "col", swap_x)
+            *moved, held_w = lax.optimization_barrier((*moved, own_w))
+            far[0, 0] = lax.ppermute(held_w, "col", swap_core)
             got[0] += tuple(moved)
             halves = [jnp.concatenate([h, m]) for h, m in zip(halves, moved)]
         else:
             got.append(tuple(moved))
             halves = moved
-        if step == 2:
-            *halves, w_x, w_c = lax.optimization_barrier((*halves, w_x, w_c))
+        if step == HOLD:
+            keys = list(near)
+            *halves, kept, w_last = lax.optimization_barrier((*halves, near[keys[-1]], near[keys[1]]))
             got[-1] = tuple(halves)
-    w_xc = lax.ppermute(w_x, "col", swap_core)
-    ws = [own_w, w_x, w_c, w_xc]
+            near[keys[-1]], near[keys[1]] = kept, w_last
+            if GX * GZ == 4:
+                near[1, 1] = lax.ppermute(near[0, 1], "col", swap_x)
+            for key in keys[1:]:
+                far[key] = lax.ppermute(near[key], "col", swap_core)
+    if GX * GZ == 4:
+        far[1, 1] = lax.ppermute(near[1, 1], "col", swap_core)
+    ws = [(far if dc else near)[dx, dz] for dx, dz, dc in FROM]
 
     acc = None
-    for at, ts in enumerate(got):
-        acc = multiply(scalars, at, ts, ws, acc, blocks)
+    for at, picks in PLAN:
+        ts = [t for n in at for t in got[n]]
+        acc = multiply(scalars, at, ts, ws, picks, acc, blocks)
 
     arrived = lax.all_to_all(acc, "col", 0, 0, tiled=True, axis_index_groups=PEER_GROUPS)
     total = jnp.sum(arrived, axis=0)

time: 153 us -> 170 us (1.11)
  blocking collectives: 43.6 us -> 73.7 us
  starting transfers between devices: 46.1 us -> 34.3 us
  waiting for transfers between devices: 32.6 us -> 29.2 us
  local copies, waits for them, and re-layouts: 16.2 us -> 19.5 us
    all_to_all x0 -> x1, blocking collectives: none -> 30.9 us  [shards(): lax.all_to_all(sent, ('row', 'col'), 0, 0, tiled=True, axis_index_groups=...]
    ppermute x8, waiting for transfers between devices: 29 us -> 9.15 us  [shards(): lax.ppermute(h, 'row', meets[n][(step + 1) % 2])]
    all_to_all x1 -> x0, starting transfers between devices: 18.2 us -> none  [shards(): lax.all_to_all(sent, ('row', 'col'), 0, 0, tiled=True, axis_index_groups=...]
    ppermute x3, waiting for transfers between devices: 3.61 us -> 20 us  [the longest x1 20 us: shards(): near[0, 1] = lax.ppermute(own_w, 'col', swap_z)]
    ppermute x8, starting transfers between devices: 18.5 us -> 23.2 us  [shards(): lax.ppermute(h, 'row', meets[n][(step + 1) % 2])]
    unnamed x5 -> x25, local copies, waits for them, and re-layouts: 4.56 us -> 8.85 us
  transfers between devices with their start and end apart: 12 -> 11, of which waited for: 8 -> 3; matrix products, arithmetic and copies ran while one was open for 10% -> 8% of each run, Pallas kernels for 6% -> 4%
where the time goes in v4:
time: 170 us
  blocking collectives  73.7 us (43%)
  starting transfers between devices  34.3 us (20%)
  waiting for transfers between devices  29.2 us (17%)
  local copies, waits for them, and re-layouts  19.5 us (11%)
  Pallas kernels  12.3 us (7%)
    all_to_all x1, blocking collectives, shards(): lax.all_to_all(acc, 'col', 0, 0, tiled=True, axis_index_groups=PEER_GROUPS)  42.8 us
    all_to_all x1, blocking collectives, shards(): lax.all_to_all(sent, ('row', 'col'), 0, 0, tiled=True, axis_index_groups=...  30.9 us
    ppermute x8, starting transfers between devices, shards(): lax.ppermute(h, 'row', meets[n][(step + 1) % 2])  23.2 us
    ppermute x1, waiting for transfers between devices, shards(): near[0, 1] = lax.ppermute(own_w, 'col', swap_z)  20 us
    pallas_call x4, Pallas kernels, multiply(): pl.pallas_call(functools.partial(multiply_kernel, acc is not None, blocks...  10.1 us
    ppermute x8, waiting for transfers between devices, shards(): lax.ppermute(h, 'row', meets[n][(step + 1) % 2])  9.15 us
    unnamed x25, local copies, waits for them, and re-layouts  8.85 us
    ppermute x1, starting transfers between devices, shards(): far[0, 0] = lax.ppermute(held_w, 'col', swap_core)  5.5 us
  transfers between devices with their start and end apart: 11, of which 3 were waited for; matrix products, arithmetic and copies ran while one was open for 8% of the time, Pallas kernels for 4%

profile of v4, /device:TPU:1, one launch (start us, length us, event | category | flops | bytes accessed | tf_op | source)
XLA Modules:
  0.0 169.5 jit_solution(9327807215581720962)
XLA Ops:
  0.0 2.2 %shard_map.46 = f32[8,32,512]{2,1,0:T(8,128)} custom-call(f32[4,32,512]{2,1,0:T(8,128)} %bitcast.19), custom_call_target="tpu_custom_call" | custom-call | flops 201326592 | bytes 524288 | tf_op jit(solution)/shard_map/pallas_call | solution.py:150
  2.2 30.9 %all_to_all.10 = f32[8,32,512]{2,1,0:T(8,128)S(1)} all-to-all(f32[8,32,512]{2,1,0:T(8,128)} %shard_map.46), channel_id=1, replica_groups={{0,1,2,3,512,513,514,515},{4,5,6,7,516,517,518,519},{8,9,10,11,520,521,..., dimensions={0} | all-to-all | bytes 1048576 | tf_op jit(solution)/shard_map/all_to_all | solution.py:223
  33.2 0.0 copy-start
  33.2 0.8 copy-done
  34.0 1.9 %collective-permute-start = (f32[1,4,32,512]{3,2,1,0:T(8,128)S(1)}, f32[1,4,32,512]{3,2,1,0:T(8,128)S(1)}, u32[]{:S(2)}, u32[]{:S(2)}) collective-permute-start(f32[1,4,32,512]{3,2,1,0:T(8,128)S(1)} %get-tuple-element.18), channel_id=1, source_target_pairs={{0,64},{64,0},{128,192},{192,128},{256,320},{320,256},{384,448},{4... | collective-permute-start | bytes 786440 | tf_op jit(solution)/shard_map/ppermute | solution.py:242
  35.9 1.9 %collective-permute-start.1 = (f32[1,4,32,512]{3,2,1,0:T(8,128)S(1)}, f32[1,4,32,512]{3,2,1,0:T(8,128)S(1)}, u32[]{:S(2)}, u32[]{:S(2)}) collective-permute-start(f32[1,4,32,512]{3,2,1,0:T(8,128)S(1)} %get-tuple-element.17), channel_id=1, source_target_pairs={{0,448},{64,128},{128,64},{192,256},{256,192},{320,384},{384,320},... | collective-permute-start | bytes 786440 | tf_op jit(solution)/shard_map/ppermute | solution.py:242
  37.9 3.6 %copy.6 = f32[8,32,1024]{1,2,0:T(8,128)} copy(f32[8,32,1024]{2,1,0:T(8,128)} %param.5) | data formatting | bytes 2097152 | tf_op args[1]
  41.5 4.8 %copy.7 = f32[64,8,16,32]{3,2,1,0:T(8,128)} copy(f32[64,8,16,32]{3,2,0,1:T(8,128)} %bitcast.17) | data formatting | bytes 2097152 | tf_op jit(solution)/shard_map/transpose | solution.py:230
  46.3 3.5 %reshape.19.refs_4_.refs_8_.refs_12_.refs_16_.refs_3_.refs_7_.refs_11_.refs_15_ = f32[16,32,512]{2,1,0:T(8,128)S(1)} reshape(f32[64,8,16,32]{3,2,1,0:T(8,128)} %copy.7) | data formatting | bytes 2097152 | tf_op jit(solution)/shard_map/reshape | solution.py:231
  49.8 2.4 %collective-permute-start.6 = (f32[16,32,512]{2,1,0:T(8,128)S(1)}, f32[16,32,512]{2,1,0:T(8,128)S(1)}, u32[]{:S(2)}, u32[]{:S(2)}) collective-permute-start(f32[16,32,512]{2,1,0:T(8,128)S(1)} %reshape.19.refs_4_.refs_8_.refs_12_.refs_16_.refs_3_.refs_7_.refs_11_.refs_15_), channel_id=1, source_target_pairs={{0,2},{1,3},{2,0},{3,1},{4,6},{5,7},{6,4},{7,5},{8,10},{9,11},{10,... | collective-permute-start | bytes 3145736 | tf_op jit(solution)/shard_map/ppermute | solution.py:245
  52.3 0.0 collective-permute-done.refs_2_
  52.3 0.0 collective-permute-done.1.refs_3_
  52.3 0.0 copy-start.2
  52.3 3.4 %collective-permute-start.4 = (f32[2,4,32,512]{3,2,1,0:T(8,128)S(1)}, f32[2,4,32,512]{3,2,1,0:T(8,128)S(1)}, u32[]{:S(2)}, u32[]{:S(2)}) collective-permute-start(f32[2,4,32,512]{3,2,1,0:T(8,128)S(1)} %pad_maximum_fusion.1), channel_id=1, source_target_pairs={{0,64},{64,0},{128,192},{192,128},{256,320},{320,256},{384,448},{4... | collective-permute-start | bytes 1572872 | tf_op jit(solution)/shard_map/ppermute | solution.py:242
  55.7 3.1 %collective-permute-start.2 = (f32[2,4,32,512]{3,2,1,0:T(8,128)S(1)}, f32[2,4,32,512]{3,2,1,0:T(8,128)S(1)}, u32[]{:S(2)}, u32[]{:S(2)}) collective-permute-start(f32[2,4,32,512]{3,2,1,0:T(8,128)S(1)} %pad_maximum_fusion), channel_id=1, source_target_pairs={{0,448},{64,128},{128,64},{192,256},{256,192},{320,384},{384,320},... | collective-permute-start | bytes 1572872 | tf_op jit(solution)/shard_map/ppermute | solution.py:242
  58.9 7.2 %collective-permute-done.4.refs_2_ = f32[2,4,32,512]{3,2,1,0:T(8,128)S(1)} collective-permute-done((f32[2,4,32,512]{3,2,1,0:T(8,128)S(1)}, f32[2,4,32,512]{3,2,1,0:T(8,128)S(1)}, u32[]{:S(2)}, u32[]{:S(2)}) %collective-permute-start.4) | collective-permute-done | bytes 524320 | tf_op jit(solution)/shard_map/ppermute | solution.py:242
  66.0 4.3 %collective-permute-start.5 = (f32[2,4,32,512]{3,2,1,0:T(8,128)S(1)}, f32[2,4,32,512]{3,2,1,0:T(8,128)S(1)}, u32[]{:S(2)}, u32[]{:S(2)}) collective-permute-start(f32[2,4,32,512]{3,2,1,0:T(8,128)S(1)} %collective-permute-done.4.refs_2_), channel_id=1, source_target_pairs={{0,448},{64,128},{128,64},{192,256},{256,192},{320,384},{384,320},... | collective-permute-start | bytes 1572872 | tf_op jit(solution)/shard_map/ppermute | solution.py:242
  70.3 0.0 copy-start.4
  70.3 0.8 copy-done.4
  71.1 0.0 collective-permute-done.2.refs_1_
  71.1 0.0 copy-done.2
  71.1 1.9 %collective-permute-start.3 = (f32[2,4,32,512]{3,2,1,0:T(8,128)S(1)}, f32[2,4,32,512]{3,2,1,0:T(8,128)S(1)}, u32[]{:S(2)}, u32[]{:S(2)}) collective-permute-start(f32[2,4,32,512]{3,2,1,0:T(8,128)S(1)} %collective-permute-done.2.refs_1_), channel_id=1, source_target_pairs={{0,64},{64,0},{128,192},{192,128},{256,320},{320,256},{384,448},{4... | collective-permute-start | bytes 1572872 | tf_op jit(solution)/shard_map/ppermute | solution.py:242
  73.0 0.8 copy-done.6
  73.9 5.5 %collective-permute-start.9 = (f32[16,32,512]{2,1,0:T(8,128)S(1)}, f32[16,32,512]{2,1,0:T(8,128)S(1)}, u32[]{:S(2)}, u32[]{:S(2)}) collective-permute-start(f32[16,32,512]{2,1,0:T(8,128)S(1)} %reshape.19.refs_4_.refs_8_.refs_12_.refs_16_.refs_3_.refs_7_.refs_11_.refs_15_), channel_id=1, source_target_pairs={{0,1},{1,0},{2,3},{3,2},{4,5},{5,4},{6,7},{7,6},{8,9},{9,8},{10,11... | collective-permute-start | bytes 3145736 | tf_op jit(solution)/shard_map/ppermute | solution.py:249
  79.4 20.0 %collective-permute-done.6.refs_5_.refs_9_.refs_13_.refs_17_.refs_4_.refs_8_.refs_12_.refs_16_ = f32[16,32,512]{2,1,0:T(8,128)S(1)} collective-permute-done((f32[16,32,512]{2,1,0:T(8,128)S(1)}, f32[16,32,512]{2,1,0:T(8,128)S(1)}, u32[]{:S(2)}, u32[]{:S(2)}) %collective-permute-start.6) | collective-permute-done | bytes 1048608 | tf_op jit(solution)/shard_map/ppermute | solution.py:245
  99.4 0.0 collective-permute-done.5.refs_2_
  99.4 0.0 collective-permute-done.3.refs_1_
  99.4 0.8 copy-done.8
  100.2 3.2 %collective-permute-start.10 = (f32[16,32,512]{2,1,0:T(8,128)S(1)}, f32[16,32,512]{2,1,0:T(8,128)}, u32[]{:S(2)}, u32[]{:S(2)}) collective-permute-start(f32[16,32,512]{2,1,0:T(8,128)S(1)} %collective-permute-done.6.refs_5_.refs_9_.refs_13_.refs_17_.refs_4_.refs_8_.refs_12_.refs_16_), channel_id=1, source_target_pairs={{0,1},{1,0},{2,3},{3,2},{4,5},{5,4},{6,7},{7,6},{8,9},{9,8},{10,11... | collective-permute-start | bytes 3145736 | tf_op jit(solution)/shard_map/ppermute | solution.py:263
  103.4 4.6 %collective-permute-start.7 = (f32[2,4,32,512]{3,2,1,0:T(8,128)}, f32[2,4,32,512]{3,2,1,0:T(8,128)S(1)}, u32[]{:S(2)}, u32[]{:S(2)}) collective-permute-start(f32[2,4,32,512]{3,2,1,0:T(8,128)} %copy-done.10), channel_id=1, source_target_pairs={{0,448},{64,128},{128,64},{192,256},{256,192},{320,384},{384,320},... | collective-permute-start | bytes 1572872 | tf_op jit(solution)/shard_map/ppermute | solution.py:242
  108.0 2.2 %collective-permute-start.8 = (f32[2,4,32,512]{3,2,1,0:T(8,128)}, f32[2,4,32,512]{3,2,1,0:T(8,128)S(1)}, u32[]{:S(2)}, u32[]{:S(2)}) collective-permute-start(f32[2,4,32,512]{3,2,1,0:T(8,128)} %copy-done.8), channel_id=1, source_target_pairs={{0,64},{64,0},{128,192},{192,128},{256,320},{320,256},{384,448},{4... | collective-permute-start | bytes 1572872 | tf_op jit(solution)/shard_map/ppermute | solution.py:242
  110.1 0.7 dynamic-slice_bitcast_fusion.1
  110.8 0.7 dynamic-slice_bitcast_fusion
  111.5 0.1 pad_add_fusion.refs_0_
  111.6 0.0 collective-permute-done.9.refs_6_.refs_10_.refs_14_.refs_18_.refs_5_.refs_9_.refs_13_.refs_17_
  111.6 0.0 collective-permute-done.10.refs_7_.refs_11_.refs_15_.refs_19_.refs_6_.refs_10_.refs_14_.refs_18_
  111.6 1.0 copy-done.1
  112.6 0.9 copy-done.3
  113.6 2.5 %shard_map.47.refs_19_ = f32[16,32,512]{2,1,0:T(8,128)S(1)} custom-call(s32[20]{0:T(128)S(1)} %pad_add_fusion.refs_0_, f32[2,4,32,512]{3,2,1,0:T(8,128)S(1)} %bitcast.16, f32[1,4,32,512]{3,2,1,0:T(8,128)S(1)} %collective-permute-done.refs_2_, f32[1,4,32,512]{3,2,1,0:T(8,128)S(1)} %copy-done.3, ...), custom_call_target="tpu_custom_call" | custom-call | flops 805306368 | bytes 2097152 | tf_op jit(solution)/shard_map/pallas_call | solution.py:200
  116.2 2.5 %shard_map.48.refs_19_ = f32[16,32,512]{2,1,0:T(8,128)S(1)} custom-call(s32[20]{0:T(128)S(1)} %pad_add_fusion.refs_0_, f32[2,4,32,512]{3,2,1,0:T(8,128)S(1)} %copy-done.7, f32[2,4,32,512]{3,2,1,0:T(8,128)S(1)} %copy-done.5, f32[16,32,512]{2,1,0:T(8,128)S(1)} %reshape.19.refs_4_.refs_8_.refs_12_.refs_16_.refs_3_.refs_7_.refs_11_.refs_15_, ...), custom_call_target="tpu_custom_call" | custom-call | flops 805306368 | bytes 2097152 | tf_op jit(solution)/shard_map/pallas_call | solution.py:200
  118.7 2.5 %shard_map.49.refs_19_ = f32[16,32,512]{2,1,0:T(8,128)S(1)} custom-call(s32[20]{0:T(128)S(1)} %pad_add_fusion.refs_0_, f32[2,4,32,512]{3,2,1,0:T(8,128)S(1)} %copy-done.11, f32[2,4,32,512]{3,2,1,0:T(8,128)S(1)} %copy-done.9, f32[16,32,512]{2,1,0:T(8,128)S(1)} %reshape.19.refs_4_.refs_8_.refs_12_.refs_16_.refs_3_.refs_7_.refs_11_.refs_15_, ...), custom_call_target="tpu_custom_call" | custom-call | flops 805306368 | bytes 2097152 | tf_op jit(solution)/shard_map/pallas_call | solution.py:200
  121.3 0.0 collective-permute-done.7.refs_1_
  121.3 2.0 %collective-permute-done.8.refs_2_ = f32[2,4,32,512]{3,2,1,0:T(8,128)S(1)} collective-permute-done((f32[2,4,32,512]{3,2,1,0:T(8,128)}, f32[2,4,32,512]{3,2,1,0:T(8,128)S(1)}, u32[]{:S(2)}, u32[]{:S(2)}) %collective-permute-start.8) | collective-permute-done | bytes 524320 | tf_op jit(solution)/shard_map/ppermute | solution.py:242
  123.3 2.5 %shard_map.50 = f32[16,32,512]{2,1,0:T(8,128)S(1)} custom-call(s32[20]{0:T(128)S(1)} %pad_add_fusion.refs_0_, f32[2,4,32,512]{3,2,1,0:T(8,128)S(1)} %collective-permute-done.7.refs_1_, f32[2,4,32,512]{3,2,1,0:T(8,128)S(1)} %collective-permute-done.8.refs_2_, f32[16,32,512]{2,1,0:T(8,128)S(1)} %reshape.19.refs_4_.refs_8_.refs_12_.refs_16_.refs_3_.refs_7_.refs_11_.refs_15_, ...), custom_call_target="tpu_custom_call" | custom-call | flops 805306368 | bytes 2097152 | tf_op jit(solution)/shard_map/pallas_call | solution.py:200
  125.8 42.8 %all_to_all.11 = f32[16,32,512]{2,1,0:T(8,128)S(1)} all-to-all(f32[16,32,512]{2,1,0:T(8,128)S(1)} %shard_map.50), channel_id=1, replica_groups={{0,4,8,12,16,20,24,28,32,36,40,44,48,52,56,60},{1,5,9,13,17,21,25,29,33..., dimensions={0} | all-to-all | bytes 2097152 | tf_op jit(solution)/shard_map/all_to_all | solution.py:273
  168.6 0.1 reduce_sum.9
  168.7 0.1 reshape.21
  168.8 0.7 copy.8
  (17 shorter events, 0.1 us)
Async XLA Ops:
  33.2 0.9 copy-start
  34.0 18.2 %collective-permute-start = (f32[1,4,32,512]{3,2,1,0:T(8,128)S(1)}, f32[1,4,32,512]{3,2,1,0:T(8,128)S(1)}, u32[]{:S(2)}, u32[]{:S(2)}) collective-permute-start(f32[1,4,32,512]{3,2,1,0:T(8,128)S(1)} %get-tuple-element.18), channel_id=1, source_target_pairs={{0,64},{64,0},{128,192},{192,128},{256,320},{320,256},{384,448},{4... | collective-permute-start | bytes 786440 | tf_op jit(solution)/shard_map/ppermute | solution.py:242
  35.9 16.3 %collective-permute-start.1 = (f32[1,4,32,512]{3,2,1,0:T(8,128)S(1)}, f32[1,4,32,512]{3,2,1,0:T(8,128)S(1)}, u32[]{:S(2)}, u32[]{:S(2)}) collective-permute-start(f32[1,4,32,512]{3,2,1,0:T(8,128)S(1)} %get-tuple-element.17), channel_id=1, source_target_pairs={{0,448},{64,128},{128,64},{192,256},{256,192},{320,384},{384,320},... | collective-permute-start | bytes 786440 | tf_op jit(solution)/shard_map/ppermute | solution.py:242
  49.8 49.6 %collective-permute-start.6 = (f32[16,32,512]{2,1,0:T(8,128)S(1)}, f32[16,32,512]{2,1,0:T(8,128)S(1)}, u32[]{:S(2)}, u32[]{:S(2)}) collective-permute-start(f32[16,32,512]{2,1,0:T(8,128)S(1)} %reshape.19.refs_4_.refs_8_.refs_12_.refs_16_.refs_3_.refs_7_.refs_11_.refs_15_), channel_id=1, source_target_pairs={{0,2},{1,3},{2,0},{3,1},{4,6},{5,7},{6,4},{7,5},{8,10},{9,11},{10,... | collective-permute-start | bytes 3145736 | tf_op jit(solution)/shard_map/ppermute | solution.py:245
  52.3 18.8 %copy-start.2 = (f32[1,4,32,512]{3,2,1,0:T(8,128)}, f32[1,4,32,512]{3,2,1,0:T(8,128)S(1)}, u32[]{:S(2)}) copy-start(f32[1,4,32,512]{3,2,1,0:T(8,128)S(1)} %collective-permute-done.1.refs_3_) | copy-start | bytes 786436
  52.3 13.7 %collective-permute-start.4 = (f32[2,4,32,512]{3,2,1,0:T(8,128)S(1)}, f32[2,4,32,512]{3,2,1,0:T(8,128)S(1)}, u32[]{:S(2)}, u32[]{:S(2)}) collective-permute-start(f32[2,4,32,512]{3,2,1,0:T(8,128)S(1)} %pad_maximum_fusion.1), channel_id=1, source_target_pairs={{0,64},{64,0},{128,192},{192,128},{256,320},{320,256},{384,448},{4... | collective-permute-start | bytes 1572872 | tf_op jit(solution)/shard_map/ppermute | solution.py:242
  55.7 15.4 %collective-permute-start.2 = (f32[2,4,32,512]{3,2,1,0:T(8,128)S(1)}, f32[2,4,32,512]{3,2,1,0:T(8,128)S(1)}, u32[]{:S(2)}, u32[]{:S(2)}) collective-permute-start(f32[2,4,32,512]{3,2,1,0:T(8,128)S(1)} %pad_maximum_fusion), channel_id=1, source_target_pairs={{0,448},{64,128},{128,64},{192,256},{256,192},{320,384},{384,320},... | collective-permute-start | bytes 1572872 | tf_op jit(solution)/shard_map/ppermute | solution.py:242
  66.0 33.4 %collective-permute-start.5 = (f32[2,4,32,512]{3,2,1,0:T(8,128)S(1)}, f32[2,4,32,512]{3,2,1,0:T(8,128)S(1)}, u32[]{:S(2)}, u32[]{:S(2)}) collective-permute-start(f32[2,4,32,512]{3,2,1,0:T(8,128)S(1)} %collective-permute-done.4.refs_2_), channel_id=1, source_target_pairs={{0,448},{64,128},{128,64},{192,256},{256,192},{320,384},{384,320},... | collective-permute-start | bytes 1572872 | tf_op jit(solution)/shard_map/ppermute | solution.py:242
  70.3 0.8 copy-start.4
  71.1 28.3 %collective-permute-start.3 = (f32[2,4,32,512]{3,2,1,0:T(8,128)S(1)}, f32[2,4,32,512]{3,2,1,0:T(8,128)S(1)}, u32[]{:S(2)}, u32[]{:S(2)}) collective-permute-start(f32[2,4,32,512]{3,2,1,0:T(8,128)S(1)} %collective-permute-done.2.refs_1_), channel_id=1, source_target_pairs={{0,64},{64,0},{128,192},{192,128},{256,320},{320,256},{384,448},{4... | collective-permute-start | bytes 1572872 | tf_op jit(solution)/shard_map/ppermute | solution.py:242
  73.0 0.8 copy-start.6
  73.9 37.7 %collective-permute-start.9 = (f32[16,32,512]{2,1,0:T(8,128)S(1)}, f32[16,32,512]{2,1,0:T(8,128)S(1)}, u32[]{:S(2)}, u32[]{:S(2)}) collective-permute-start(f32[16,32,512]{2,1,0:T(8,128)S(1)} %reshape.19.refs_4_.refs_8_.refs_12_.refs_16_.refs_3_.refs_7_.refs_11_.refs_15_), channel_id=1, source_target_pairs={{0,1},{1,0},{2,3},{3,2},{4,5},{5,4},{6,7},{7,6},{8,9},{9,8},{10,11... | collective-permute-start | bytes 3145736 | tf_op jit(solution)/shard_map/ppermute | solution.py:249
  99.4 0.8 copy-start.8
  100.2 3.2 %copy-start.10 = (f32[2,4,32,512]{3,2,1,0:T(8,128)}, f32[2,4,32,512]{3,2,1,0:T(8,128)S(1)}, u32[]{:S(2)}) copy-start(f32[2,4,32,512]{3,2,1,0:T(8,128)S(1)} %collective-permute-done.3.refs_1_) | copy-start | bytes 1572868
  100.2 11.4 %collective-permute-start.10 = (f32[16,32,512]{2,1,0:T(8,128)S(1)}, f32[16,32,512]{2,1,0:T(8,128)}, u32[]{:S(2)}, u32[]{:S(2)}) collective-permute-start(f32[16,32,512]{2,1,0:T(8,128)S(1)} %collective-permute-done.6.refs_5_.refs_9_.refs_13_.refs_17_.refs_4_.refs_8_.refs_12_.refs_16_), channel_id=1, source_target_pairs={{0,1},{1,0},{2,3},{3,2},{4,5},{5,4},{6,7},{7,6},{8,9},{9,8},{10,11... | collective-permute-start | bytes 3145736 | tf_op jit(solution)/shard_map/ppermute | solution.py:263
  103.4 17.9 %collective-permute-start.7 = (f32[2,4,32,512]{3,2,1,0:T(8,128)}, f32[2,4,32,512]{3,2,1,0:T(8,128)S(1)}, u32[]{:S(2)}, u32[]{:S(2)}) collective-permute-start(f32[2,4,32,512]{3,2,1,0:T(8,128)} %copy-done.10), channel_id=1, source_target_pairs={{0,448},{64,128},{128,64},{192,256},{256,192},{320,384},{384,320},... | collective-permute-start | bytes 1572872 | tf_op jit(solution)/shard_map/ppermute | solution.py:242
  108.0 15.3 %collective-permute-start.8 = (f32[2,4,32,512]{3,2,1,0:T(8,128)}, f32[2,4,32,512]{3,2,1,0:T(8,128)S(1)}, u32[]{:S(2)}, u32[]{:S(2)}) collective-permute-start(f32[2,4,32,512]{3,2,1,0:T(8,128)} %copy-done.8), channel_id=1, source_target_pairs={{0,64},{64,0},{128,192},{192,128},{256,320},{320,256},{384,448},{4... | collective-permute-start | bytes 1572872 | tf_op jit(solution)/shard_map/ppermute | solution.py:242
  111.6 1.0 copy-start.1
  112.6 0.9 copy-start.3
  113.6 2.5 %copy-start.5 = (f32[2,4,32,512]{3,2,1,0:T(8,128)S(1)}, f32[2,4,32,512]{3,2,1,0:T(8,128)}, u32[]{:S(2)}) copy-start(f32[2,4,32,512]{3,2,1,0:T(8,128)} %copy-done.4) | copy-start | bytes 1572868
  113.6 2.5 %copy-start.7 = (f32[2,4,32,512]{3,2,1,0:T(8,128)S(1)}, f32[2,4,32,512]{3,2,1,0:T(8,128)}, u32[]{:S(2)}) copy-start(f32[2,4,32,512]{3,2,1,0:T(8,128)} %copy-done.6) | copy-start | bytes 1572868
  116.1 2.6 %copy-start.9 = (f32[2,4,32,512]{3,2,1,0:T(8,128)S(1)}, f32[2,4,32,512]{3,2,1,0:T(8,128)}, u32[]{:S(2)}) copy-start(f32[2,4,32,512]{3,2,1,0:T(8,128)} %copy-done.8) | copy-start | bytes 1572868
  116.2 2.6 %copy-start.11 = (f32[2,4,32,512]{3,2,1,0:T(8,128)S(1)}, f32[2,4,32,512]{3,2,1,0:T(8,128)}, u32[]{:S(2)}) copy-start(f32[2,4,32,512]{3,2,1,0:T(8,128)} %copy-done.10) | copy-start | bytes 1572868

commit v5 on v4

--- a/solution.py
+++ b/solution.py
@@ -10,7 +10,7 @@
 
 X, ZH, CORES = 8, 4, 2
 ZL, Y = 2, 8
-GX, GZ = 1, 2
+GX, GZ = 2, 1
 XH, ZG = X // GX, ZH // GZ
 MEMBERS = GX * GZ * CORES
 PEERS = XH * ZG
@@ -84,14 +84,8 @@
 SLOTS = sum(COUNTS)
 
 
-HOLD = 3
+PARTS = (2, 2)
 EVERY = list(range(MEMBERS))
-LATE = [n for n, (dx, dz, dc) in enumerate(FROM) if dx + dz == 2]
-EARLY = [n for n in EVERY if n not in LATE]
-if LATE:
-    PLAN = [((0,), EARLY), ((1,), EARLY), ((2,), EARLY), ((0, 1, 2), LATE), ((3,), EVERY)]
-else:
-    PLAN = [((n,), EVERY) for n in range(len(COUNTS))]
 
 
 def row_table():
@@ -231,49 +225,47 @@
     own_w = w_t.reshape(ZL * Y, rows, pairs * wb)
     swap_core = col_perm(lambda x, zh, c: (x, zh, c ^ 1))
     swap_x = col_perm(lambda x, zh, c: (x ^ 1, zh, c))
-    swap_z = col_perm(lambda x, zh, c: (x, zh ^ 1, c))
 
     meets = [[row_perm(lambda z, q, f=f: (z, f(q))) for f in pair] for pair in MEETS]
-    halves = [own[:1], own[1:]]
-    got = [(own,)]
+    width = own.shape[3] // blocks
     near = {(0, 0): own_w}
     far = {}
-    for step in range(1, Y // 2 + 1):
-        moved = [lax.ppermute(h, "row", meets[n][(step + 1) % 2]) for n, h in enumerate(halves)]
-        if step == 1:
-            if GZ == 2:
-                near[0, 1] = lax.ppermute(own_w, "col", swap_z)
-            if GX == 2:
+    totals = []
+    after = None
+    first = 0
+    for part, count in enumerate(PARTS):
+        mine = own[:, :, :, first * width : (first + count) * width]
+        first += count
+        halves = [mine[:1], mine[1:]]
+        if after is not None:
+            *halves, _ = lax.optimization_barrier((*halves, after))
+        got = [tuple(halves)]
+        for step in range(1, Y // 2 + 1):
+            moved = [lax.ppermute(h, "row", meets[n][(step + 1) % 2]) for n, h in enumerate(halves)]
+            if part == 0 and step == 1:
                 near[1, 0] = lax.ppermute(own_w, "col", swap_x)
-            *moved, held_w = lax.optimization_barrier((*moved, own_w))
-            far[0, 0] = lax.ppermute(held_w, "col", swap_core)
-            got[0] += tuple(moved)
-            halves = [jnp.concatenate([h, m]) for h, m in zip(halves, moved)]
-        else:
-            got.append(tuple(moved))
-            halves = moved
-        if step == HOLD:
-            keys = list(near)
-            *halves, kept, w_last = lax.optimization_barrier((*halves, near[keys[-1]], near[keys[1]]))
-            got[-1] = tuple(halves)
-            near[keys[-1]], near[keys[1]] = kept, w_last
-            if GX * GZ == 4:
-                near[1, 1] = lax.ppermute(near[0, 1], "col", swap_x)
-            for key in keys[1:]:
-                far[key] = lax.ppermute(near[key], "col", swap_core)
-    if GX * GZ == 4:
-        far[1, 1] = lax.ppermute(near[1, 1], "col", swap_core)
-    ws = [(far if dc else near)[dx, dz] for dx, dz, dc in FROM]
-
-    acc = None
-    for at, picks in PLAN:
-        ts = [t for n in at for t in got[n]]
-        acc = multiply(scalars, at, ts, ws, picks, acc, blocks)
-
-    arrived = lax.all_to_all(acc, "col", 0, 0, tiled=True, axis_index_groups=PEER_GROUPS)
-    total = jnp.sum(arrived, axis=0)
+                *moved, held_w = lax.optimization_barrier((*moved, own_w))
+                far[0, 0] = lax.ppermute(held_w, "col", swap_core)
+            if part == 0 and step == 2:
+                *moved, near[1, 0] = lax.optimization_barrier((*moved, near[1, 0]))
+                far[1, 0] = lax.ppermute(near[1, 0], "col", swap_core)
+            if step == 3:
+                *moved, after = lax.optimization_barrier((*moved, moved[0]))
+            if step == 1:
+                got[0] += tuple(moved)
+                halves = [jnp.concatenate([h, m]) for h, m in zip(halves, moved)]
+            else:
+                got.append(tuple(moved))
+                halves = moved
+        ws = [(far if dc else near)[dx, dz] for dx, dz, dc in FROM]
+        acc = None
+        for at, ts in enumerate(got):
+            acc = multiply(scalars, (at,), ts, ws, EVERY, acc, count)
+        arrived = lax.all_to_all(acc, "col", 0, 0, tiled=True, axis_index_groups=PEER_GROUPS)
+        totals.append(arrived)
     run = virt // (X * ZH * CORES)
-    return total.reshape(blocks, run, pairs, wb).transpose(1, 0, 2, 3)
+    totals = [jnp.sum(t, axis=0).reshape(n, run, pairs, wb) for t, n in zip(totals, PARTS)]
+    return jnp.concatenate(totals).transpose(1, 0, 2, 3)
 
 
 def solution(mesh):

time: 170 us -> 181 us (1.065)
  the two profiles are of different devices: /device:TPU:1 before, /device:TPU:2 now
where the time goes in v5:
time: 181 us; the launch traced here: 179 us
  starting transfers between devices  89.9 us (50%)
  waiting for transfers between devices  47.5 us (26%)
  Pallas kernels  19.4 us (11%)
  local copies, waits for them, and re-layouts  18.6 us (10%)
  other arithmetic  3.1 us (2%)
    ppermute x16, starting transfers between devices, shards(): lax.ppermute(h, 'row', meets[n][(step + 1) % 2])  44.7 us
    ppermute x16, waiting for transfers between devices, shards(): lax.ppermute(h, 'row', meets[n][(step + 1) % 2])  24.7 us
    all_to_all x2, starting transfers between devices, shards(): lax.all_to_all(acc, 'col', 0, 0, tiled=True, axis_index_groups=PEER_GROUPS)  22.8 us
    pallas_call x8, Pallas kernels, multiply(): pl.pallas_call(functools.partial(multiply_kernel, acc is not None, blocks...  17.1 us
    all_to_all x1, starting transfers between devices, shards(): lax.all_to_all(sent, ('row', 'col'), 0, 0, tiled=True, axis_index_groups=...  16.6 us
    all_to_all x2, waiting for transfers between devices, shards(): lax.all_to_all(acc, 'col', 0, 0, tiled=True, axis_index_groups=PEER_GROUPS)  15 us
    unnamed x17, local copies, waits for them, and re-layouts  7.9 us
    ppermute x1, waiting for transfers between devices, shards(): near[1, 0] = lax.ppermute(own_w, 'col', swap_x)  7.76 us
  transfers between devices with their start and end apart: 22, of which 10 were waited for; matrix products, arithmetic and copies ran while one was open for 9% of the time, Pallas kernels for 10%

profile of v5, /device:TPU:2, one launch (start us, length us, event | category | flops | bytes accessed | tf_op | source)
XLA Modules:
  0.0 179.1 jit_solution(4581872493573154307)
XLA Ops:
  0.0 2.3 %shard_map.46 = f32[8,32,512]{2,1,0:T(8,128)} custom-call(f32[4,32,512]{2,1,0:T(8,128)} %bitcast.15), custom_call_target="tpu_custom_call" | custom-call | flops 201326592 | bytes 524288 | tf_op jit(solution)/shard_map/pallas_call | solution.py:144
  2.3 16.6 %all-to-all-start = ((f32[8,32,512]{2,1,0:T(8,128)}), f32[8,32,512]{2,1,0:T(8,128)S(1)}, u32[]{:S(2)}, u32[]{:S(2)}) async-start(f32[8,32,512]{2,1,0:T(8,128)} %shard_map.46), calls=%async_computation | async-start | bytes 1048576 | tf_op jit(solution)/shard_map/all_to_all | solution.py:217
  18.9 3.6 %copy.6 = f32[8,32,1024]{1,2,0:T(8,128)} copy(f32[8,32,1024]{2,1,0:T(8,128)} %param.5) | data formatting | bytes 2097152 | tf_op args[1]
  22.5 4.8 %copy.7 = f32[64,8,16,32]{3,2,1,0:T(8,128)} copy(f32[64,8,16,32]{3,2,0,1:T(8,128)} %bitcast.13) | data formatting | bytes 2097152 | tf_op jit(solution)/shard_map/transpose | solution.py:224
  27.3 3.5 %reshape.21.refs_5_.refs_9_.refs_13_.refs_17_.refs_3_.refs_7_.refs_11_.refs_15_ = f32[16,32,512]{2,1,0:T(8,128)S(1)} reshape(f32[64,8,16,32]{3,2,1,0:T(8,128)} %copy.7) | data formatting | bytes 2097152 | tf_op jit(solution)/shard_map/reshape | solution.py:225
  30.9 2.0 %collective-permute-start.4 = (f32[16,32,512]{2,1,0:T(8,128)S(1)}, f32[16,32,512]{2,1,0:T(8,128)S(1)}, u32[]{:S(2)}, u32[]{:S(2)}) collective-permute-start(f32[16,32,512]{2,1,0:T(8,128)S(1)} %reshape.21.refs_5_.refs_9_.refs_13_.refs_17_.refs_3_.refs_7_.refs_11_.refs_15_), channel_id=1, source_target_pairs={{0,8},{1,9},{2,10},{3,11},{4,12},{5,13},{6,14},{7,15},{8,0},{9,1},... | collective-permute-start | bytes 3145736 | tf_op jit(solution)/shard_map/ppermute | solution.py:246
  33.0 1.9 %collective-permute-start = (f32[1,4,32,256]{3,2,1,0:T(8,128)S(1)}, f32[1,4,32,256]{3,2,1,0:T(8,128)S(1)}, u32[]{:S(2)}, u32[]{:S(2)}) collective-permute-start(f32[1,4,32,256]{3,2,1,0:T(8,128)S(1)} %get-tuple-element.32.refs_1_), channel_id=1, source_target_pairs={{0,64},{64,0},{128,192},{192,128},{256,320},{320,256},{384,448},{4... | collective-permute-start | bytes 393224 | tf_op jit(solution)/shard_map/ppermute | solution.py:244
  34.9 1.9 %collective-permute-start.1 = (f32[1,4,32,256]{3,2,1,0:T(8,128)S(1)}, f32[1,4,32,256]{3,2,1,0:T(8,128)S(1)}, u32[]{:S(2)}, u32[]{:S(2)}) collective-permute-start(f32[1,4,32,256]{3,2,1,0:T(8,128)S(1)} %get-tuple-element.29.refs_2_), channel_id=1, source_target_pairs={{0,448},{64,128},{128,64},{192,256},{256,192},{320,384},{384,320},... | collective-permute-start | bytes 393224 | tf_op jit(solution)/shard_map/ppermute | solution.py:244
  36.8 3.6 %collective-permute-done.refs_3_ = f32[1,4,32,256]{3,2,1,0:T(8,128)S(1)} collective-permute-done((f32[1,4,32,256]{3,2,1,0:T(8,128)S(1)}, f32[1,4,32,256]{3,2,1,0:T(8,128)S(1)}, u32[]{:S(2)}, u32[]{:S(2)}) %collective-permute-start) | collective-permute-done | bytes 131104 | tf_op jit(solution)/shard_map/ppermute | solution.py:244
  40.4 3.1 %collective-permute-done.1.refs_4_ = f32[1,4,32,256]{3,2,1,0:T(8,128)S(1)} collective-permute-done((f32[1,4,32,256]{3,2,1,0:T(8,128)S(1)}, f32[1,4,32,256]{3,2,1,0:T(8,128)S(1)}, u32[]{:S(2)}, u32[]{:S(2)}) %collective-permute-start.1) | collective-permute-done | bytes 131104 | tf_op jit(solution)/shard_map/ppermute | solution.py:244
  43.6 2.2 %collective-permute-start.2 = (f32[2,4,32,256]{3,2,1,0:T(8,128)S(1)}, f32[2,4,32,256]{3,2,1,0:T(8,128)}, u32[]{:S(2)}, u32[]{:S(2)}) collective-permute-start(f32[2,4,32,256]{3,2,1,0:T(8,128)S(1)} %pad_maximum_fusion), channel_id=1, source_target_pairs={{0,448},{64,128},{128,64},{192,256},{256,192},{320,384},{384,320},... | collective-permute-start | bytes 786440 | tf_op jit(solution)/shard_map/ppermute | solution.py:244
  45.8 2.4 %collective-permute-start.3 = (f32[2,4,32,256]{3,2,1,0:T(8,128)S(1)}, f32[2,4,32,256]{3,2,1,0:T(8,128)}, u32[]{:S(2)}, u32[]{:S(2)}) collective-permute-start(f32[2,4,32,256]{3,2,1,0:T(8,128)S(1)} %pad_maximum_fusion.1), channel_id=1, source_target_pairs={{0,64},{64,0},{128,192},{192,128},{256,320},{320,256},{384,448},{4... | collective-permute-start | bytes 786440 | tf_op jit(solution)/shard_map/ppermute | solution.py:244
  48.3 1.9 %collective-permute-start.9 = (f32[16,32,512]{2,1,0:T(8,128)S(1)}, f32[16,32,512]{2,1,0:T(8,128)S(1)}, u32[]{:S(2)}, u32[]{:S(2)}) collective-permute-start(f32[16,32,512]{2,1,0:T(8,128)S(1)} %reshape.21.refs_5_.refs_9_.refs_13_.refs_17_.refs_3_.refs_7_.refs_11_.refs_15_), channel_id=1, source_target_pairs={{0,1},{1,0},{2,3},{3,2},{4,5},{5,4},{6,7},{7,6},{8,9},{9,8},{10,11... | collective-permute-start | bytes 3145736 | tf_op jit(solution)/shard_map/ppermute | solution.py:248
  50.2 7.8 %collective-permute-done.4.refs_6_.refs_10_.refs_14_.refs_18_.refs_4_.refs_8_.refs_12_.refs_16_ = f32[16,32,512]{2,1,0:T(8,128)S(1)} collective-permute-done((f32[16,32,512]{2,1,0:T(8,128)S(1)}, f32[16,32,512]{2,1,0:T(8,128)S(1)}, u32[]{:S(2)}, u32[]{:S(2)}) %collective-permute-start.4) | collective-permute-done | bytes 1048608 | tf_op jit(solution)/shard_map/ppermute | solution.py:246
  58.0 1.9 %collective-permute-start.10 = (f32[16,32,512]{2,1,0:T(8,128)S(1)}, f32[16,32,512]{2,1,0:T(8,128)}, u32[]{:S(2)}, u32[]{:S(2)}) collective-permute-start(f32[16,32,512]{2,1,0:T(8,128)S(1)} %collective-permute-done.4.refs_6_.refs_10_.refs_14_.refs_18_.refs_4_.refs_8_.refs_12_.refs_16_), channel_id=1, source_target_pairs={{0,1},{1,0},{2,3},{3,2},{4,5},{5,4},{6,7},{7,6},{8,9},{9,8},{10,11... | collective-permute-start | bytes 3145736 | tf_op jit(solution)/shard_map/ppermute | solution.py:251
  59.9 1.9 %collective-permute-start.5 = (f32[2,4,32,256]{3,2,1,0:T(8,128)}, f32[2,4,32,256]{3,2,1,0:T(8,128)}, u32[]{:S(2)}, u32[]{:S(2)}) collective-permute-start(f32[2,4,32,256]{3,2,1,0:T(8,128)} %collective-permute-done.2.refs_1_), channel_id=1, source_target_pairs={{0,64},{64,0},{128,192},{192,128},{256,320},{320,256},{384,448},{4... | collective-permute-start | bytes 786440 | tf_op jit(solution)/shard_map/ppermute | solution.py:244
  61.8 2.2 %collective-permute-start.6 = (f32[2,4,32,256]{3,2,1,0:T(8,128)}, f32[2,4,32,256]{3,2,1,0:T(8,128)}, u32[]{:S(2)}, u32[]{:S(2)}) collective-permute-start(f32[2,4,32,256]{3,2,1,0:T(8,128)} %collective-permute-done.3.refs_2_), channel_id=1, source_target_pairs={{0,448},{64,128},{128,64},{192,256},{256,192},{320,384},{384,320},... | collective-permute-start | bytes 786440 | tf_op jit(solution)/shard_map/ppermute | solution.py:244
  64.8 6.0 %collective-permute-done.5.refs_1_ = f32[2,4,32,256]{3,2,1,0:T(8,128)} collective-permute-done((f32[2,4,32,256]{3,2,1,0:T(8,128)}, f32[2,4,32,256]{3,2,1,0:T(8,128)}, u32[]{:S(2)}, u32[]{:S(2)}) %collective-permute-start.5) | collective-permute-done | bytes 262176 | tf_op jit(solution)/shard_map/ppermute | solution.py:244
  70.8 3.1 %collective-permute-done.6.refs_2_ = f32[2,4,32,256]{3,2,1,0:T(8,128)} collective-permute-done((f32[2,4,32,256]{3,2,1,0:T(8,128)}, f32[2,4,32,256]{3,2,1,0:T(8,128)}, u32[]{:S(2)}, u32[]{:S(2)}) %collective-permute-start.6) | collective-permute-done | bytes 262176 | tf_op jit(solution)/shard_map/ppermute | solution.py:244
  74.0 2.2 %collective-permute-start.7 = (f32[2,4,32,256]{3,2,1,0:T(8,128)}, f32[2,4,32,256]{3,2,1,0:T(8,128)S(1)}, u32[]{:S(2)}, u32[]{:S(2)}) collective-permute-start(f32[2,4,32,256]{3,2,1,0:T(8,128)} %collective-permute-done.5.refs_1_), channel_id=1, source_target_pairs={{0,448},{64,128},{128,64},{192,256},{256,192},{320,384},{384,320},... | collective-permute-start | bytes 786440 | tf_op jit(solution)/shard_map/ppermute | solution.py:244
  76.2 2.4 %collective-permute-start.8 = (f32[2,4,32,256]{3,2,1,0:T(8,128)}, f32[2,4,32,256]{3,2,1,0:T(8,128)S(1)}, u32[]{:S(2)}, u32[]{:S(2)}) collective-permute-start(f32[2,4,32,256]{3,2,1,0:T(8,128)} %collective-permute-done.6.refs_2_), channel_id=1, source_target_pairs={{0,64},{64,0},{128,192},{192,128},{256,320},{320,256},{384,448},{4... | collective-permute-start | bytes 786440 | tf_op jit(solution)/shard_map/ppermute | solution.py:244
  79.4 3.4 %collective-permute-start.11 = (f32[1,4,32,256]{3,2,1,0:T(8,128)S(1)}, f32[1,4,32,256]{3,2,1,0:T(8,128)}, u32[]{:S(2)}, u32[]{:S(2)}) collective-permute-start(f32[1,4,32,256]{3,2,1,0:T(8,128)S(1)} %get-tuple-element.25.refs_1_), channel_id=1, source_target_pairs={{0,64},{64,0},{128,192},{192,128},{256,320},{320,256},{384,448},{4... | collective-permute-start | bytes 393224 | tf_op jit(solution)/shard_map/ppermute | solution.py:244
  82.8 4.9 %collective-permute-start.14 = (f32[1,4,32,256]{3,2,1,0:T(8,128)S(1)}, f32[1,4,32,256]{3,2,1,0:T(8,128)}, u32[]{:S(2)}, u32[]{:S(2)}) collective-permute-start(f32[1,4,32,256]{3,2,1,0:T(8,128)S(1)} %get-tuple-element.26.refs_2_), channel_id=1, source_target_pairs={{0,448},{64,128},{128,64},{192,256},{256,192},{320,384},{384,320},... | collective-permute-start | bytes 393224 | tf_op jit(solution)/shard_map/ppermute | solution.py:244
  88.6 0.9 copy-done.5
  89.5 0.9 copy-done.7
  90.4 2.1 %shard_map.47.refs_19_ = f32[16,16,512]{2,1,0:T(8,128)S(1)} custom-call(s32[20]{0:T(128)S(1)} %pad_add_fusion.refs_0_, f32[1,4,32,256]{3,2,1,0:T(8,128)S(1)} %copy-done.3, f32[1,4,32,256]{3,2,1,0:T(8,128)S(1)} %get-tuple-element.29.refs_2_, f32[1,4,32,256]{3,2,1,0:T(8,128)S(1)} %copy-done.5, f32[1,4,32,256]{3,2,1,0:T(8,128)S(1)} %copy-done.7, ...), custom_call_target="tpu_custom_call" | custom-call | flops 402653184 | bytes 1572864 | tf_op jit(solution)/shard_map/pallas_call | solution.py:194
  92.5 2.2 %shard_map.48.refs_19_ = f32[16,16,512]{2,1,0:T(8,128)S(1)} custom-call(s32[20]{0:T(128)S(1)} %pad_add_fusion.refs_0_, f32[2,4,32,256]{3,2,1,0:T(8,128)} %collective-permute-done.2.refs_1_, f32[2,4,32,256]{3,2,1,0:T(8,128)} %collective-permute-done.3.refs_2_, f32[16,32,512]{2,1,0:T(8,128)S(1)} %reshape.21.refs_5_.refs_9_.refs_13_.refs_17_.refs_3_.refs_7_.refs_11_.refs_15_, ...), custom_call_target="tpu_custom_call" | custom-call | flops 402653184 | bytes 1572864 | tf_op jit(solution)/shard_map/pallas_call | solution.py:194
  94.7 2.2 %shard_map.49.refs_19_ = f32[16,16,512]{2,1,0:T(8,128)S(1)} custom-call(s32[20]{0:T(128)S(1)} %pad_add_fusion.refs_0_, f32[2,4,32,256]{3,2,1,0:T(8,128)} %collective-permute-done.5.refs_1_, f32[2,4,32,256]{3,2,1,0:T(8,128)} %collective-permute-done.6.refs_2_, f32[16,32,512]{2,1,0:T(8,128)S(1)} %reshape.21.refs_5_.refs_9_.refs_13_.refs_17_.refs_3_.refs_7_.refs_11_.refs_15_, ...), custom_call_target="tpu_custom_call" | custom-call | flops 402653184 | bytes 1572864 | tf_op jit(solution)/shard_map/pallas_call | solution.py:194
  97.0 2.1 %shard_map.50 = f32[16,16,512]{2,1,0:T(8,128)S(1)} custom-call(s32[20]{0:T(128)S(1)} %pad_add_fusion.refs_0_, f32[2,4,32,256]{3,2,1,0:T(8,128)S(1)} %collective-permute-done.7.refs_1_, f32[2,4,32,256]{3,2,1,0:T(8,128)S(1)} %collective-permute-done.8.refs_2_, f32[16,32,512]{2,1,0:T(8,128)S(1)} %reshape.21.refs_5_.refs_9_.refs_13_.refs_17_.refs_3_.refs_7_.refs_11_.refs_15_, ...), custom_call_target="tpu_custom_call" | custom-call | flops 402653184 | bytes 1572864 | tf_op jit(solution)/shard_map/pallas_call | solution.py:194
  99.9 10.7 %all-to-all-start.1 = ((f32[16,16,512]{2,1,0:T(8,128)}), f32[16,16,512]{2,1,0:T(8,128)}, u32[]{:S(2)}, u32[]{:S(2)}) async-start(f32[16,16,512]{2,1,0:T(8,128)} %copy-done), calls=%async_computation.1 | async-start | bytes 1048576 | tf_op jit(solution)/shard_map/all_to_all | solution.py:264
  110.6 0.9 pad_maximum_fusion.3
  111.5 2.9 %collective-permute-start.15 = (f32[2,4,32,256]{3,2,1,0:T(8,128)S(1)}, f32[2,4,32,256]{3,2,1,0:T(8,128)S(1)}, u32[]{:S(2)}, u32[]{:S(2)}) collective-permute-start(f32[2,4,32,256]{3,2,1,0:T(8,128)S(1)} %pad_maximum_fusion.3), channel_id=1, source_target_pairs={{0,64},{64,0},{128,192},{192,128},{256,320},{320,256},{384,448},{4... | collective-permute-start | bytes 786440 | tf_op jit(solution)/shard_map/ppermute | solution.py:244
  114.4 0.9 pad_maximum_fusion.2
  115.3 3.9 %collective-permute-start.12 = (f32[2,4,32,256]{3,2,1,0:T(8,128)S(1)}, f32[2,4,32,256]{3,2,1,0:T(8,128)S(1)}, u32[]{:S(2)}, u32[]{:S(2)}) collective-permute-start(f32[2,4,32,256]{3,2,1,0:T(8,128)S(1)} %pad_maximum_fusion.2), channel_id=1, source_target_pairs={{0,448},{64,128},{128,64},{192,256},{256,192},{320,384},{384,320},... | collective-permute-start | bytes 786440 | tf_op jit(solution)/shard_map/ppermute | solution.py:244
  120.0 4.7 %collective-permute-start.16 = (f32[2,4,32,256]{3,2,1,0:T(8,128)S(1)}, f32[2,4,32,256]{3,2,1,0:T(8,128)S(1)}, u32[]{:S(2)}, u32[]{:S(2)}) collective-permute-start(f32[2,4,32,256]{3,2,1,0:T(8,128)S(1)} %collective-permute-done.15.refs_2_), channel_id=1, source_target_pairs={{0,448},{64,128},{128,64},{192,256},{256,192},{320,384},{384,320},... | collective-permute-start | bytes 786440 | tf_op jit(solution)/shard_map/ppermute | solution.py:244
  124.7 1.8 %collective-permute-done.12.refs_1_ = f32[2,4,32,256]{3,2,1,0:T(8,128)S(1)} collective-permute-done((f32[2,4,32,256]{3,2,1,0:T(8,128)S(1)}, f32[2,4,32,256]{3,2,1,0:T(8,128)S(1)}, u32[]{:S(2)}, u32[]{:S(2)}) %collective-permute-start.12) | collective-permute-done | bytes 262176 | tf_op jit(solution)/shard_map/ppermute | solution.py:244
  126.5 2.0 %collective-permute-start.13 = (f32[2,4,32,256]{3,2,1,0:T(8,128)S(1)}, f32[2,4,32,256]{3,2,1,0:T(8,128)S(1)}, u32[]{:S(2)}, u32[]{:S(2)}) collective-permute-start(f32[2,4,32,256]{3,2,1,0:T(8,128)S(1)} %collective-permute-done.12.refs_1_), channel_id=1, source_target_pairs={{0,64},{64,0},{128,192},{192,128},{256,320},{320,256},{384,448},{4... | collective-permute-start | bytes 786440 | tf_op jit(solution)/shard_map/ppermute | solution.py:244
  128.5 2.0 %collective-permute-done.16.refs_2_ = f32[2,4,32,256]{3,2,1,0:T(8,128)S(1)} collective-permute-done((f32[2,4,32,256]{3,2,1,0:T(8,128)S(1)}, f32[2,4,32,256]{3,2,1,0:T(8,128)S(1)}, u32[]{:S(2)}, u32[]{:S(2)}) %collective-permute-start.16) | collective-permute-done | bytes 262176 | tf_op jit(solution)/shard_map/ppermute | solution.py:244
  130.4 4.3 %collective-permute-done.13.refs_1_ = f32[2,4,32,256]{3,2,1,0:T(8,128)S(1)} collective-permute-done((f32[2,4,32,256]{3,2,1,0:T(8,128)S(1)}, f32[2,4,32,256]{3,2,1,0:T(8,128)S(1)}, u32[]{:S(2)}, u32[]{:S(2)}) %collective-permute-start.13) | collective-permute-done | bytes 262176 | tf_op jit(solution)/shard_map/ppermute | solution.py:244
  134.7 3.8 %collective-permute-start.17 = (f32[2,4,32,256]{3,2,1,0:T(8,128)S(1)}, f32[2,4,32,256]{3,2,1,0:T(8,128)S(1)}, u32[]{:S(2)}, u32[]{:S(2)}) collective-permute-start(f32[2,4,32,256]{3,2,1,0:T(8,128)S(1)} %collective-permute-done.13.refs_1_), channel_id=1, source_target_pairs={{0,448},{64,128},{128,64},{192,256},{256,192},{320,384},{384,320},... | collective-permute-start | bytes 786440 | tf_op jit(solution)/shard_map/ppermute | solution.py:244
  138.6 1.9 %collective-permute-start.18 = (f32[2,4,32,256]{3,2,1,0:T(8,128)S(1)}, f32[2,4,32,256]{3,2,1,0:T(8,128)S(1)}, u32[]{:S(2)}, u32[]{:S(2)}) collective-permute-start(f32[2,4,32,256]{3,2,1,0:T(8,128)S(1)} %collective-permute-done.16.refs_2_), channel_id=1, source_target_pairs={{0,64},{64,0},{128,192},{192,128},{256,320},{320,256},{384,448},{4... | collective-permute-start | bytes 786440 | tf_op jit(solution)/shard_map/ppermute | solution.py:244
  140.5 2.2 %shard_map.51.refs_19_ = f32[16,16,512]{2,1,0:T(8,128)S(1)} custom-call(s32[20]{0:T(128)S(1)} %pad_add_fusion.refs_0_, f32[1,4,32,256]{3,2,1,0:T(8,128)S(1)} %get-tuple-element.25.refs_1_, f32[1,4,32,256]{3,2,1,0:T(8,128)S(1)} %get-tuple-element.26.refs_2_, f32[1,4,32,256]{3,2,1,0:T(8,128)} %collective-permute-done.11.refs_3_, ...), custom_call_target="tpu_custom_call" | custom-call | flops 402653184 | bytes 1572864 | tf_op jit(solution)/shard_map/pallas_call | solution.py:194
  142.7 2.1 %shard_map.52.refs_19_ = f32[16,16,512]{2,1,0:T(8,128)S(1)} custom-call(s32[20]{0:T(128)S(1)} %pad_add_fusion.refs_0_, f32[2,4,32,256]{3,2,1,0:T(8,128)S(1)} %collective-permute-done.12.refs_1_, f32[2,4,32,256]{3,2,1,0:T(8,128)S(1)} %collective-permute-done.15.refs_2_, ...), custom_call_target="tpu_custom_call" | custom-call | flops 402653184 | bytes 1572864 | tf_op jit(solution)/shard_map/pallas_call | solution.py:194
  144.8 2.1 %shard_map.53.refs_19_ = f32[16,16,512]{2,1,0:T(8,128)S(1)} custom-call(s32[20]{0:T(128)S(1)} %pad_add_fusion.refs_0_, f32[2,4,32,256]{3,2,1,0:T(8,128)S(1)} %collective-permute-done.13.refs_1_, f32[2,4,32,256]{3,2,1,0:T(8,128)S(1)} %collective-permute-done.16.refs_2_, ...), custom_call_target="tpu_custom_call" | custom-call | flops 402653184 | bytes 1572864 | tf_op jit(solution)/shard_map/pallas_call | solution.py:194
  147.0 2.1 %shard_map.54 = f32[16,16,512]{2,1,0:T(8,128)S(1)} custom-call(s32[20]{0:T(128)S(1)} %pad_add_fusion.refs_0_, f32[2,4,32,256]{3,2,1,0:T(8,128)S(1)} %collective-permute-done.17.refs_1_, f32[2,4,32,256]{3,2,1,0:T(8,128)S(1)} %collective-permute-done.18.refs_2_, f32[16,32,512]{2,1,0:T(8,128)S(1)} %reshape.21.refs_5_.refs_9_.refs_13_.refs_17_.refs_3_.refs_7_.refs_11_.refs_15_, ...), custom_call_target="tpu_custom_call" | custom-call | flops 402653184 | bytes 1572864 | tf_op jit(solution)/shard_map/pallas_call | solution.py:194
  149.9 12.1 %all-to-all-start.2 = ((f32[16,16,512]{2,1,0:T(8,128)}), f32[16,16,512]{2,1,0:T(8,128)S(1)}, u32[]{:S(2)}, u32[]{:S(2)}) async-start(f32[16,16,512]{2,1,0:T(8,128)} %copy-done.1), calls=%async_computation.2 | async-start | bytes 1048576 | tf_op jit(solution)/shard_map/all_to_all | solution.py:264
  162.0 1.1 reduce_sum.18
  163.2 15.0 %all-to-all-done.2 = f32[16,16,512]{2,1,0:T(8,128)S(1)} async-done(((f32[16,16,512]{2,1,0:T(8,128)}), f32[16,16,512]{2,1,0:T(8,128)S(1)}, u32[]{:S(2)}, u32[]{:S(2)}) %all-to-all-start.2) | async-done | bytes 524320 | tf_op jit(solution)/shard_map/all_to_all | solution.py:264
  (38 shorter events, 5.7 us)
Async XLA Ops:
  2.3 30.6 %all-to-all-start = ((f32[8,32,512]{2,1,0:T(8,128)}), f32[8,32,512]{2,1,0:T(8,128)S(1)}, u32[]{:S(2)}, u32[]{:S(2)}) async-start(f32[8,32,512]{2,1,0:T(8,128)} %shard_map.46), calls=%async_computation | async-start | bytes 1048576 | tf_op jit(solution)/shard_map/all_to_all | solution.py:217
  30.9 27.1 %collective-permute-start.4 = (f32[16,32,512]{2,1,0:T(8,128)S(1)}, f32[16,32,512]{2,1,0:T(8,128)S(1)}, u32[]{:S(2)}, u32[]{:S(2)}) collective-permute-start(f32[16,32,512]{2,1,0:T(8,128)S(1)} %reshape.21.refs_5_.refs_9_.refs_13_.refs_17_.refs_3_.refs_7_.refs_11_.refs_15_), channel_id=1, source_target_pairs={{0,8},{1,9},{2,10},{3,11},{4,12},{5,13},{6,14},{7,15},{8,0},{9,1},... | collective-permute-start | bytes 3145736 | tf_op jit(solution)/shard_map/ppermute | solution.py:246
  33.0 12.9 %copy-start.2 = (f32[1,4,32,256]{3,2,1,0:T(8,128)}, f32[1,4,32,256]{3,2,1,0:T(8,128)S(1)}, u32[]{:S(2)}) copy-start(f32[1,4,32,256]{3,2,1,0:T(8,128)S(1)} %get-tuple-element.32.refs_1_) | copy-start | bytes 393220
  33.0 7.4 %collective-permute-start = (f32[1,4,32,256]{3,2,1,0:T(8,128)S(1)}, f32[1,4,32,256]{3,2,1,0:T(8,128)S(1)}, u32[]{:S(2)}, u32[]{:S(2)}) collective-permute-start(f32[1,4,32,256]{3,2,1,0:T(8,128)S(1)} %get-tuple-element.32.refs_1_), channel_id=1, source_target_pairs={{0,64},{64,0},{128,192},{192,128},{256,320},{320,256},{384,448},{4... | collective-permute-start | bytes 393224 | tf_op jit(solution)/shard_map/ppermute | solution.py:244
  34.9 8.7 %collective-permute-start.1 = (f32[1,4,32,256]{3,2,1,0:T(8,128)S(1)}, f32[1,4,32,256]{3,2,1,0:T(8,128)S(1)}, u32[]{:S(2)}, u32[]{:S(2)}) collective-permute-start(f32[1,4,32,256]{3,2,1,0:T(8,128)S(1)} %get-tuple-element.29.refs_2_), channel_id=1, source_target_pairs={{0,448},{64,128},{128,64},{192,256},{256,192},{320,384},{384,320},... | collective-permute-start | bytes 393224 | tf_op jit(solution)/shard_map/ppermute | solution.py:244
  40.4 5.4 %copy-start.4 = (f32[1,4,32,256]{3,2,1,0:T(8,128)}, f32[1,4,32,256]{3,2,1,0:T(8,128)S(1)}, u32[]{:S(2)}) copy-start(f32[1,4,32,256]{3,2,1,0:T(8,128)S(1)} %collective-permute-done.refs_3_) | copy-start | bytes 393220
  43.6 2.3 %copy-start.6 = (f32[1,4,32,256]{3,2,1,0:T(8,128)}, f32[1,4,32,256]{3,2,1,0:T(8,128)S(1)}, u32[]{:S(2)}) copy-start(f32[1,4,32,256]{3,2,1,0:T(8,128)S(1)} %collective-permute-done.1.refs_4_) | copy-start | bytes 393220
  43.6 14.4 %collective-permute-start.2 = (f32[2,4,32,256]{3,2,1,0:T(8,128)S(1)}, f32[2,4,32,256]{3,2,1,0:T(8,128)}, u32[]{:S(2)}, u32[]{:S(2)}) collective-permute-start(f32[2,4,32,256]{3,2,1,0:T(8,128)S(1)} %pad_maximum_fusion), channel_id=1, source_target_pairs={{0,448},{64,128},{128,64},{192,256},{256,192},{320,384},{384,320},... | collective-permute-start | bytes 786440 | tf_op jit(solution)/shard_map/ppermute | solution.py:244
  45.8 12.1 %collective-permute-start.3 = (f32[2,4,32,256]{3,2,1,0:T(8,128)S(1)}, f32[2,4,32,256]{3,2,1,0:T(8,128)}, u32[]{:S(2)}, u32[]{:S(2)}) collective-permute-start(f32[2,4,32,256]{3,2,1,0:T(8,128)S(1)} %pad_maximum_fusion.1), channel_id=1, source_target_pairs={{0,64},{64,0},{128,192},{192,128},{256,320},{320,256},{384,448},{4... | collective-permute-start | bytes 786440 | tf_op jit(solution)/shard_map/ppermute | solution.py:244
  48.3 34.5 %collective-permute-start.9 = (f32[16,32,512]{2,1,0:T(8,128)S(1)}, f32[16,32,512]{2,1,0:T(8,128)S(1)}, u32[]{:S(2)}, u32[]{:S(2)}) collective-permute-start(f32[16,32,512]{2,1,0:T(8,128)S(1)} %reshape.21.refs_5_.refs_9_.refs_13_.refs_17_.refs_3_.refs_7_.refs_11_.refs_15_), channel_id=1, source_target_pairs={{0,1},{1,0},{2,3},{3,2},{4,5},{5,4},{6,7},{7,6},{8,9},{9,8},{10,11... | collective-permute-start | bytes 3145736 | tf_op jit(solution)/shard_map/ppermute | solution.py:248
  58.0 29.7 %collective-permute-start.10 = (f32[16,32,512]{2,1,0:T(8,128)S(1)}, f32[16,32,512]{2,1,0:T(8,128)}, u32[]{:S(2)}, u32[]{:S(2)}) collective-permute-start(f32[16,32,512]{2,1,0:T(8,128)S(1)} %collective-permute-done.4.refs_6_.refs_10_.refs_14_.refs_18_.refs_4_.refs_8_.refs_12_.refs_16_), channel_id=1, source_target_pairs={{0,1},{1,0},{2,3},{3,2},{4,5},{5,4},{6,7},{7,6},{8,9},{9,8},{10,11... | collective-permute-start | bytes 3145736 | tf_op jit(solution)/shard_map/ppermute | solution.py:251
  59.9 10.9 %collective-permute-start.5 = (f32[2,4,32,256]{3,2,1,0:T(8,128)}, f32[2,4,32,256]{3,2,1,0:T(8,128)}, u32[]{:S(2)}, u32[]{:S(2)}) collective-permute-start(f32[2,4,32,256]{3,2,1,0:T(8,128)} %collective-permute-done.2.refs_1_), channel_id=1, source_target_pairs={{0,64},{64,0},{128,192},{192,128},{256,320},{320,256},{384,448},{4... | collective-permute-start | bytes 786440 | tf_op jit(solution)/shard_map/ppermute | solution.py:244
  61.8 12.1 %collective-permute-start.6 = (f32[2,4,32,256]{3,2,1,0:T(8,128)}, f32[2,4,32,256]{3,2,1,0:T(8,128)}, u32[]{:S(2)}, u32[]{:S(2)}) collective-permute-start(f32[2,4,32,256]{3,2,1,0:T(8,128)} %collective-permute-done.3.refs_2_), channel_id=1, source_target_pairs={{0,448},{64,128},{128,64},{192,256},{256,192},{320,384},{384,320},... | collective-permute-start | bytes 786440 | tf_op jit(solution)/shard_map/ppermute | solution.py:244
  74.0 23.0 %collective-permute-start.7 = (f32[2,4,32,256]{3,2,1,0:T(8,128)}, f32[2,4,32,256]{3,2,1,0:T(8,128)S(1)}, u32[]{:S(2)}, u32[]{:S(2)}) collective-permute-start(f32[2,4,32,256]{3,2,1,0:T(8,128)} %collective-permute-done.5.refs_1_), channel_id=1, source_target_pairs={{0,448},{64,128},{128,64},{192,256},{256,192},{320,384},{384,320},... | collective-permute-start | bytes 786440 | tf_op jit(solution)/shard_map/ppermute | solution.py:244
  76.2 20.8 %collective-permute-start.8 = (f32[2,4,32,256]{3,2,1,0:T(8,128)}, f32[2,4,32,256]{3,2,1,0:T(8,128)S(1)}, u32[]{:S(2)}, u32[]{:S(2)}) collective-permute-start(f32[2,4,32,256]{3,2,1,0:T(8,128)} %collective-permute-done.6.refs_2_), channel_id=1, source_target_pairs={{0,64},{64,0},{128,192},{192,128},{256,320},{320,256},{384,448},{4... | collective-permute-start | bytes 786440 | tf_op jit(solution)/shard_map/ppermute | solution.py:244
  79.4 35.0 %collective-permute-start.11 = (f32[1,4,32,256]{3,2,1,0:T(8,128)S(1)}, f32[1,4,32,256]{3,2,1,0:T(8,128)}, u32[]{:S(2)}, u32[]{:S(2)}) collective-permute-start(f32[1,4,32,256]{3,2,1,0:T(8,128)S(1)} %get-tuple-element.25.refs_1_), channel_id=1, source_target_pairs={{0,64},{64,0},{128,192},{192,128},{256,320},{320,256},{384,448},{4... | collective-permute-start | bytes 393224 | tf_op jit(solution)/shard_map/ppermute | solution.py:244
  82.8 27.8 %collective-permute-start.14 = (f32[1,4,32,256]{3,2,1,0:T(8,128)S(1)}, f32[1,4,32,256]{3,2,1,0:T(8,128)}, u32[]{:S(2)}, u32[]{:S(2)}) collective-permute-start(f32[1,4,32,256]{3,2,1,0:T(8,128)S(1)} %get-tuple-element.26.refs_2_), channel_id=1, source_target_pairs={{0,448},{64,128},{128,64},{192,256},{256,192},{320,384},{384,320},... | collective-permute-start | bytes 393224 | tf_op jit(solution)/shard_map/ppermute | solution.py:244
  87.7 0.9 copy-start.3
  88.6 0.9 copy-start.5
  89.5 0.9 copy-start.7
  99.1 0.8 copy-start
  99.9 50.0 %all-to-all-start.1 = ((f32[16,16,512]{2,1,0:T(8,128)}), f32[16,16,512]{2,1,0:T(8,128)}, u32[]{:S(2)}, u32[]{:S(2)}) async-start(f32[16,16,512]{2,1,0:T(8,128)} %copy-done), calls=%async_computation.1 | async-start | bytes 1048576 | tf_op jit(solution)/shard_map/all_to_all | solution.py:264
  111.5 8.4 %collective-permute-start.15 = (f32[2,4,32,256]{3,2,1,0:T(8,128)S(1)}, f32[2,4,32,256]{3,2,1,0:T(8,128)S(1)}, u32[]{:S(2)}, u32[]{:S(2)}) collective-permute-start(f32[2,4,32,256]{3,2,1,0:T(8,128)S(1)} %pad_maximum_fusion.3), channel_id=1, source_target_pairs={{0,64},{64,0},{128,192},{192,128},{256,320},{320,256},{384,448},{4... | collective-permute-start | bytes 786440 | tf_op jit(solution)/shard_map/ppermute | solution.py:244
  115.3 11.1 %collective-permute-start.12 = (f32[2,4,32,256]{3,2,1,0:T(8,128)S(1)}, f32[2,4,32,256]{3,2,1,0:T(8,128)S(1)}, u32[]{:S(2)}, u32[]{:S(2)}) collective-permute-start(f32[2,4,32,256]{3,2,1,0:T(8,128)S(1)} %pad_maximum_fusion.2), channel_id=1, source_target_pairs={{0,448},{64,128},{128,64},{192,256},{256,192},{320,384},{384,320},... | collective-permute-start | bytes 786440 | tf_op jit(solution)/shard_map/ppermute | solution.py:244
  120.0 10.5 %collective-permute-start.16 = (f32[2,4,32,256]{3,2,1,0:T(8,128)S(1)}, f32[2,4,32,256]{3,2,1,0:T(8,128)S(1)}, u32[]{:S(2)}, u32[]{:S(2)}) collective-permute-start(f32[2,4,32,256]{3,2,1,0:T(8,128)S(1)} %collective-permute-done.15.refs_2_), channel_id=1, source_target_pairs={{0,448},{64,128},{128,64},{192,256},{256,192},{320,384},{384,320},... | collective-permute-start | bytes 786440 | tf_op jit(solution)/shard_map/ppermute | solution.py:244
  126.5 8.3 %collective-permute-start.13 = (f32[2,4,32,256]{3,2,1,0:T(8,128)S(1)}, f32[2,4,32,256]{3,2,1,0:T(8,128)S(1)}, u32[]{:S(2)}, u32[]{:S(2)}) collective-permute-start(f32[2,4,32,256]{3,2,1,0:T(8,128)S(1)} %collective-permute-done.12.refs_1_), channel_id=1, source_target_pairs={{0,64},{64,0},{128,192},{192,128},{256,320},{320,256},{384,448},{4... | collective-permute-start | bytes 786440 | tf_op jit(solution)/shard_map/ppermute | solution.py:244
  134.7 12.2 %collective-permute-start.17 = (f32[2,4,32,256]{3,2,1,0:T(8,128)S(1)}, f32[2,4,32,256]{3,2,1,0:T(8,128)S(1)}, u32[]{:S(2)}, u32[]{:S(2)}) collective-permute-start(f32[2,4,32,256]{3,2,1,0:T(8,128)S(1)} %collective-permute-done.13.refs_1_), channel_id=1, source_target_pairs={{0,448},{64,128},{128,64},{192,256},{256,192},{320,384},{384,320},... | collective-permute-start | bytes 786440 | tf_op jit(solution)/shard_map/ppermute | solution.py:244
  138.6 8.4 %collective-permute-start.18 = (f32[2,4,32,256]{3,2,1,0:T(8,128)S(1)}, f32[2,4,32,256]{3,2,1,0:T(8,128)S(1)}, u32[]{:S(2)}, u32[]{:S(2)}) collective-permute-start(f32[2,4,32,256]{3,2,1,0:T(8,128)S(1)} %collective-permute-done.16.refs_2_), channel_id=1, source_target_pairs={{0,64},{64,0},{128,192},{192,128},{256,320},{320,256},{384,448},{4... | collective-permute-start | bytes 786440 | tf_op jit(solution)/shard_map/ppermute | solution.py:244
  149.1 0.8 copy-start.1
  149.9 28.3 %all-to-all-start.2 = ((f32[16,16,512]{2,1,0:T(8,128)}), f32[16,16,512]{2,1,0:T(8,128)S(1)}, u32[]{:S(2)}, u32[]{:S(2)}) async-start(f32[16,16,512]{2,1,0:T(8,128)} %copy-done.1), calls=%async_computation.2 | async-start | bytes 1048576 | tf_op jit(solution)/shard_map/all_to_all | solution.py:264

commit v6 on v4

--- a/solution.py
+++ b/solution.py
@@ -10,9 +10,9 @@
 
 X, ZH, CORES = 8, 4, 2
 ZL, Y = 2, 8
-GX, GZ = 1, 2
+GX, GZ = 2, 2
 XH, ZG = X // GX, ZH // GZ
-MEMBERS = GX * GZ * CORES
+MEMBERS = GX * GZ
 PEERS = XH * ZG
 F32 = jnp.float32
 BF16 = jnp.bfloat16
@@ -40,16 +40,16 @@
     return pairs
 
 
-GROUP = [(xl, zm, core) for xl in range(GX) for zm in range(GZ) for core in range(CORES)]
+GROUP = [(xl, zm) for xl in range(GX) for zm in range(GZ)]
 BASES = [(xh * GX, zg * GZ) for xh in range(XH) for zg in range(ZG)]
 MEMBER_GROUPS = [
-    [(zl * Y + y) * (X * ZH * CORES) + col_of(x + xl, zh + zm, core) for zl in range(ZL) for xl, zm, core in GROUP]
+    [(zl * Y + y) * (X * ZH * CORES) + col_of(x + xl, zh + zm, core) for zl in range(ZL) for xl, zm in GROUP]
     for y in range(Y)
     for x, zh in BASES
+    for core in range(CORES)
 ]
-PEER_GROUPS = [[col_of(x + xl, zh + zm, core) for x, zh in BASES] for xl, zm, core in GROUP]
-NEAR = [(dx, dz) for dx in range(GX) for dz in range(GZ)]
-FROM = [(dx, dz, dc) for dc in range(CORES) for dx, dz in NEAR]
+PEER_GROUPS = [[col_of(x + xl, zh + zm, core) for x, zh in BASES] for xl, zm in GROUP for core in range(CORES)]
+FROM = [(dx, dz) for dx in range(GX) for dz in range(GZ)]
 
 
 def low_pair(y):
@@ -84,14 +84,10 @@
 SLOTS = sum(COUNTS)
 
 
-HOLD = 3
 EVERY = list(range(MEMBERS))
-LATE = [n for n, (dx, dz, dc) in enumerate(FROM) if dx + dz == 2]
+LATE = [n for n, (dx, dz) in enumerate(FROM) if dx + dz == 2]
 EARLY = [n for n in EVERY if n not in LATE]
-if LATE:
-    PLAN = [((0,), EARLY), ((1,), EARLY), ((2,), EARLY), ((0, 1, 2), LATE), ((3,), EVERY)]
-else:
-    PLAN = [((n,), EVERY) for n in range(len(COUNTS))]
+PLAN = [((0,), EARLY), ((1,), EARLY), ((2,), EARLY), ((0, 1, 2), LATE), ((3,), EVERY)]
 
 
 def row_table():
@@ -104,8 +100,8 @@
 def col_table():
     table = np.zeros((X * ZH * CORES, MEMBERS), np.int32)
     for col in range(table.shape[0]):
-        x, zh, core = col // (ZH * CORES) % GX, col // CORES % GZ, col % CORES
-        table[col] = [((x ^ dx) * GZ + (zh ^ dz)) * CORES + (core ^ dc) for dx, dz, dc in FROM]
+        x, zh = col // (ZH * CORES) % GX, col // CORES % GZ
+        table[col] = [(x ^ dx) * GZ + (zh ^ dz) for dx, dz in FROM]
     return table
 
 
@@ -114,7 +110,7 @@
     return hi, (v - hi.astype(F32)).astype(BF16)
 
 
-def regroup_kernel(t_ref, out_ref):
+def regroup_kernel(core_ref, t_ref, out_ref):
     blocks, rows, virt = t_ref.shape
     run = virt // (X * ZH * CORES)
     src = lax.broadcasted_iota(jnp.int32, (virt, virt), 0)
@@ -122,7 +118,8 @@
     r = dst % run
     zg = (dst // run) % ZG
     xh = (dst // (run * ZG)) % XH
-    core = (dst // (run * PEERS)) % CORES
+    other = (dst // (run * PEERS)) % CORES
+    core = (core_ref[0] + other) % CORES
     zm = (dst // (run * PEERS * CORES)) % GZ
     xl = dst // (run * PEERS * CORES * GZ)
     want = (((((xh * GX + xl) * ZG + zg) * GZ + zm) * CORES) + core) * run + r
@@ -144,21 +141,23 @@
                 out_ref[z * MEMBERS + m, :, i * width : (i + 1) * width] = piece
 
 
-def regroup(t):
+def regroup(t, core):
     blocks, ks, cs, virt = t.shape
     rows = ks * cs
     return pl.pallas_call(
         regroup_kernel,
+        in_specs=[pl.BlockSpec(memory_space=pltpu.SMEM), pl.BlockSpec(memory_space=pltpu.VMEM)],
         out_shape=jax.ShapeDtypeStruct((ZL * MEMBERS, rows, blocks * virt // MEMBERS), F32),
         cost_estimate=pl.CostEstimate(flops=6 * blocks * rows * virt * virt, bytes_accessed=t.size * 8, transcendentals=0),
-    )(t.reshape(blocks, rows, virt))
+    )(core.reshape(1), t.reshape(blocks, rows, virt))
 
 
 def multiply_kernel(has_acc, blocks, picks, n_t, n_w, *refs):
     s_ref = refs[0]
     t_refs = refs[1 : 1 + n_t]
     w_refs = refs[1 + n_t : 1 + n_t + n_w]
-    out_ref = refs[-1]
+    accs = refs[1 + n_t + n_w : -CORES]
+    outs = refs[-CORES:]
     left = jnp.concatenate(
         [t[z, s_ref[SLOTS + n]] for t in t_refs for z in range(t.shape[0]) for n in picks], axis=0
     )
@@ -171,21 +170,22 @@
         (((0,), (0,)), ((), ())),
         preferred_element_type=F32,
     )
-    run = total.shape[0] // (blocks * PEERS)
-    total = total.reshape(blocks, PEERS, run, total.shape[1])
+    run = total.shape[0] // (blocks * CORES * PEERS)
+    total = total.reshape(blocks, CORES, PEERS, run, total.shape[1])
     for i in range(blocks):
         rows = slice(i * run, (i + 1) * run)
-        if has_acc:
-            out_ref[:, rows, :] = refs[1 + n_t + n_w][:, rows, :] + total[i]
-        else:
-            out_ref[:, rows, :] = total[i]
+        for c in range(CORES):
+            if has_acc:
+                outs[c][:, rows, :] = accs[c][:, rows, :] + total[i, c]
+            else:
+                outs[c][:, rows, :] = total[i, c]
 
 
 def multiply(scalars, at, ts, ws, picks, acc, blocks):
     ws = [ws[n] for n in picks]
     rows, width = ts[0].shape[2], ts[0].shape[3]
     wide = ws[0].shape[2]
-    out_shape = (PEERS, width // PEERS, wide)
+    out_shape = (PEERS, width // (CORES * PEERS), wide)
     slots = [sum(COUNTS[:n]) + m for n in at for m in range(COUNTS[n])]
     in_specs = [pl.BlockSpec(t.shape, lambda z, s: (0, 0, 0, 0)) for t in ts]
     in_specs += [
@@ -194,13 +194,13 @@
     args = [scalars, *ts, *(list(ws) * len(slots))]
     whole = pl.BlockSpec(out_shape, lambda z, s: (0, 0, 0))
     if acc is not None:
-        in_specs.append(whole)
-        args.append(acc)
+        in_specs += [whole] * CORES
+        args += acc
     depth = len(slots) * len(ws) * rows
     return pl.pallas_call(
         functools.partial(multiply_kernel, acc is not None, blocks, picks, len(ts), len(slots) * len(ws)),
-        grid_spec=pltpu.PrefetchScalarGridSpec(num_scalar_prefetch=1, grid=(1,), in_specs=in_specs, out_specs=whole),
-        out_shape=jax.ShapeDtypeStruct(out_shape, F32),
+        grid_spec=pltpu.PrefetchScalarGridSpec(num_scalar_prefetch=1, grid=(1,), in_specs=in_specs, out_specs=[whole] * CORES),
+        out_shape=[jax.ShapeDtypeStruct(out_shape, F32)] * CORES,
         compiler_params=pltpu.CompilerParams(vmem_limit_bytes=32 * 2**20),
         cost_estimate=pl.CostEstimate(
             flops=6 * depth * width * wide, bytes_accessed=4 * depth * (width + wide), transcendentals=0
@@ -219,7 +219,7 @@
         ]
     )
 
-    sent = regroup(t_pair)
+    sent = regroup(t_pair, (col % CORES).astype(jnp.int32))
     own = lax.all_to_all(
         sent, ("row", "col"), 0, 0, tiled=True, axis_index_groups=MEMBER_GROUPS
     ).reshape(ZL, MEMBERS, rows, -1)
@@ -229,6 +229,8 @@
     pairs = kj // occupied
     w_t = w_ovov.reshape(cs, wb, occupied, pairs).transpose(2, 0, 3, 1)
     own_w = w_t.reshape(ZL * Y, rows, pairs * wb)
+    first_w = own_w
+    own, own_w = lax.optimization_barrier((own, own_w))
     swap_core = col_perm(lambda x, zh, c: (x, zh, c ^ 1))
     swap_x = col_perm(lambda x, zh, c: (x ^ 1, zh, c))
     swap_z = col_perm(lambda x, zh, c: (x, zh ^ 1, c))
@@ -236,40 +238,29 @@
     meets = [[row_perm(lambda z, q, f=f: (z, f(q))) for f in pair] for pair in MEETS]
     halves = [own[:1], own[1:]]
     got = [(own,)]
-    near = {(0, 0): own_w}
-    far = {}
+    near = {(0, 0): own_w, (0, 1): lax.ppermute(first_w, "col", swap_z)}
     for step in range(1, Y // 2 + 1):
         moved = [lax.ppermute(h, "row", meets[n][(step + 1) % 2]) for n, h in enumerate(halves)]
         if step == 1:
-            if GZ == 2:
-                near[0, 1] = lax.ppermute(own_w, "col", swap_z)
-            if GX == 2:
-                near[1, 0] = lax.ppermute(own_w, "col", swap_x)
-            *moved, held_w = lax.optimization_barrier((*moved, own_w))
-            far[0, 0] = lax.ppermute(held_w, "col", swap_core)
+            *moved, held = lax.optimization_barrier((*moved, own_w))
+            near[1, 0] = lax.ppermute(held, "col", swap_x)
+        if step == 3:
+            *moved, near[0, 1] = lax.optimization_barrier((*moved, near[0, 1]))
+            near[1, 1] = lax.ppermute(near[0, 1], "col", swap_x)
+        if step == 1:
             got[0] += tuple(moved)
             halves = [jnp.concatenate([h, m]) for h, m in zip(halves, moved)]
         else:
             got.append(tuple(moved))
             halves = moved
-        if step == HOLD:
-            keys = list(near)
-            *halves, kept, w_last = lax.optimization_barrier((*halves, near[keys[-1]], near[keys[1]]))
-            got[-1] = tuple(halves)
-            near[keys[-1]], near[keys[1]] = kept, w_last
-            if GX * GZ == 4:
-                near[1, 1] = lax.ppermute(near[0, 1], "col", swap_x)
-            for key in keys[1:]:
-                far[key] = lax.ppermute(near[key], "col", swap_core)
-    if GX * GZ == 4:
-        far[1, 1] = lax.ppermute(near[1, 1], "col", swap_core)
-    ws = [(far if dc else near)[dx, dz] for dx, dz, dc in FROM]
+    ws = [near[key] for key in FROM]
 
     acc = None
     for at, picks in PLAN:
         ts = [t for n in at for t in got[n]]
         acc = multiply(scalars, at, ts, ws, picks, acc, blocks)
 
+    acc = acc[0] + lax.ppermute(acc[1], "col", swap_core)
     arrived = lax.all_to_all(acc, "col", 0, 0, tiled=True, axis_index_groups=PEER_GROUPS)
     total = jnp.sum(arrived, axis=0)
     run = virt // (X * ZH * CORES)

time: 170 us -> 158 us (0.929)
  the two profiles are of different devices: /device:TPU:1 before, /device:TPU:3 now
where the time goes in v6:
time: 158 us; the launch traced here: 157 us
  starting transfers between devices  49.9 us (32%)
  waiting for transfers between devices  37.9 us (24%)
  blocking collectives  35.5 us (22%)
  local copies, waits for them, and re-layouts  19.4 us (12%)
  Pallas kernels  13.4 us (8%)
    all_to_all x1, blocking collectives, shards(): lax.all_to_all(acc, 'col', 0, 0, tiled=True, axis_index_groups=PEER_GROUPS)  35.5 us
    ppermute x8, starting transfers between devices, shards(): lax.ppermute(h, 'row', meets[n][(step + 1) % 2])  27.3 us
    ppermute x1, waiting for transfers between devices, shards(): near = {(0, 0): own_w, (0, 1): lax.ppermute(first_w, 'col', swap_z)}  23.8 us
    pallas_call x5, Pallas kernels, multiply(): pl.pallas_call(functools.partial(multiply_kernel, acc is not None, blocks...  11.1 us
    all_to_all x1, starting transfers between devices, shards(): lax.all_to_all(sent, ('row', 'col'), 0, 0, tiled=True, axis_index_groups=...  10.9 us
    unnamed x25, local copies, waits for them, and re-layouts  8.8 us
    ppermute x1, waiting for transfers between devices, shards(): near[1, 1] = lax.ppermute(near[0, 1], 'col', swap_x)  8.6 us
    transpose x1, local copies, waits for them, and re-layouts, shards(): w_t = w_ovov.reshape(cs, wb, occupied, pairs).transpose(2, 0, 3, 1)  4.83 us
  transfers between devices with their start and end apart: 13, of which 5 were waited for; matrix products, arithmetic and copies ran while one was open for 9% of the time, Pallas kernels for 6%

profile of v6, /device:TPU:3, one launch (start us, length us, event | category | flops | bytes accessed | tf_op | source)
XLA Modules:
  0.0 156.7 jit_solution(16466726230185869918)
XLA Ops:
  0.0 2.3 %shard_map.46 = f32[8,32,512]{2,1,0:T(8,128)} custom-call(s32[1]{0:T(128)} %bitcast.2.core_ref, f32[4,32,512]{2,1,0:T(8,128)} %bitcast.18), custom_call_target="tpu_custom_call" | custom-call | flops 201326592 | bytes 524288 | tf_op jit(solution)/shard_map/pallas_call | solution.py:147
  2.3 10.9 %all-to-all-start = ((f32[8,32,512]{2,1,0:T(8,128)}), f32[8,32,512]{2,1,0:T(8,128)S(1)}, u32[]{:S(2)}, u32[]{:S(2)}) async-start(f32[8,32,512]{2,1,0:T(8,128)} %shard_map.46), calls=%async_computation | async-start | bytes 1048576 | tf_op jit(solution)/shard_map/all_to_all | solution.py:223
  13.2 3.6 %copy.6 = f32[8,32,1024]{1,2,0:T(8,128)} copy(f32[8,32,1024]{2,1,0:T(8,128)} %param.5) | data formatting | bytes 2097152 | tf_op args[1]
  16.8 4.8 %copy.7 = f32[64,8,16,32]{3,2,1,0:T(8,128)} copy(f32[64,8,16,32]{3,2,0,1:T(8,128)} %bitcast.16) | data formatting | bytes 2097152 | tf_op jit(solution)/shard_map/transpose | solution.py:230
  21.6 3.5 %reshape.22.refs_4_.refs_7_.refs_10_.refs_13_.refs_3_.refs_6_.refs_9_.refs_12_.refs_11_.refs_15_ = f32[16,32,512]{2,1,0:T(8,128)S(1)} reshape(f32[64,8,16,32]{3,2,1,0:T(8,128)} %copy.7) | data formatting | bytes 2097152 | tf_op jit(solution)/shard_map/reshape | solution.py:231
  25.2 0.0 all-to-all-done
  25.3 3.7 %collective-permute-start = (f32[1,4,32,512]{3,2,1,0:T(8,128)S(1)}, f32[1,4,32,512]{3,2,1,0:T(8,128)S(1)}, u32[]{:S(2)}, u32[]{:S(2)}) collective-permute-start(f32[1,4,32,512]{3,2,1,0:T(8,128)S(1)} %get-tuple-element.42), channel_id=1, source_target_pairs={{0,64},{64,0},{128,192},{192,128},{256,320},{320,256},{384,448},{4... | collective-permute-start | bytes 786440 | tf_op jit(solution)/shard_map/ppermute | solution.py:243
  28.9 5.4 %collective-permute-start.1 = (f32[1,4,32,512]{3,2,1,0:T(8,128)S(1)}, f32[1,4,32,512]{3,2,1,0:T(8,128)S(1)}, u32[]{:S(2)}, u32[]{:S(2)}) collective-permute-start(f32[1,4,32,512]{3,2,1,0:T(8,128)S(1)} %get-tuple-element.41), channel_id=1, source_target_pairs={{0,448},{64,128},{128,64},{192,256},{256,192},{320,384},{384,320},... | collective-permute-start | bytes 786440 | tf_op jit(solution)/shard_map/ppermute | solution.py:243
  34.4 3.6 %collective-permute-start.6 = (f32[16,32,512]{2,1,0:T(8,128)S(1)}, f32[16,32,512]{2,1,0:T(8,128)S(1)}, u32[]{:S(2)}, u32[]{:S(2)}) collective-permute-start(f32[16,32,512]{2,1,0:T(8,128)S(1)} %reshape.22.refs_4_.refs_7_.refs_10_.refs_13_.refs_3_.refs_6_.refs_9_.refs_12_.refs_11_.refs_15_), channel_id=1, source_target_pairs={{0,2},{1,3},{2,0},{3,1},{4,6},{5,7},{6,4},{7,5},{8,10},{9,11},{10,... | collective-permute-start | bytes 3145736 | tf_op jit(solution)/shard_map/ppermute | solution.py:241
  38.0 0.0 collective-permute-done.refs_2_
  38.0 0.1 collective-permute-done.1.refs_3_
  38.2 1.9 %collective-permute-start.4 = (f32[2,4,32,512]{3,2,1,0:T(8,128)S(1)}, f32[2,4,32,512]{3,2,1,0:T(8,128)S(1)}, u32[]{:S(2)}, u32[]{:S(2)}) collective-permute-start(f32[2,4,32,512]{3,2,1,0:T(8,128)S(1)} %pad_maximum_fusion.1), channel_id=1, source_target_pairs={{0,64},{64,0},{128,192},{192,128},{256,320},{320,256},{384,448},{4... | collective-permute-start | bytes 1572872 | tf_op jit(solution)/shard_map/ppermute | solution.py:243
  40.1 4.6 %collective-permute-start.2 = (f32[2,4,32,512]{3,2,1,0:T(8,128)S(1)}, f32[2,4,32,512]{3,2,1,0:T(8,128)S(1)}, u32[]{:S(2)}, u32[]{:S(2)}) collective-permute-start(f32[2,4,32,512]{3,2,1,0:T(8,128)S(1)} %pad_maximum_fusion), channel_id=1, source_target_pairs={{0,448},{64,128},{128,64},{192,256},{256,192},{320,384},{384,320},... | collective-permute-start | bytes 1572872 | tf_op jit(solution)/shard_map/ppermute | solution.py:243
  44.7 3.8 %collective-permute-done.4.refs_2_.refs_5_ = f32[2,4,32,512]{3,2,1,0:T(8,128)S(1)} collective-permute-done((f32[2,4,32,512]{3,2,1,0:T(8,128)S(1)}, f32[2,4,32,512]{3,2,1,0:T(8,128)S(1)}, u32[]{:S(2)}, u32[]{:S(2)}) %collective-permute-start.4) | collective-permute-done | bytes 524320 | tf_op jit(solution)/shard_map/ppermute | solution.py:243
  48.6 5.9 %collective-permute-start.5 = (f32[2,4,32,512]{3,2,1,0:T(8,128)S(1)}, f32[2,4,32,512]{3,2,1,0:T(8,128)S(1)}, u32[]{:S(2)}, u32[]{:S(2)}) collective-permute-start(f32[2,4,32,512]{3,2,1,0:T(8,128)S(1)} %collective-permute-done.4.refs_2_.refs_5_), channel_id=1, source_target_pairs={{0,448},{64,128},{128,64},{192,256},{256,192},{320,384},{384,320},... | collective-permute-start | bytes 1572872 | tf_op jit(solution)/shard_map/ppermute | solution.py:243
  54.5 0.8 copy-done.4
  55.3 0.0 collective-permute-done.2.refs_1_.refs_4_
  55.3 1.9 %collective-permute-start.3 = (f32[2,4,32,512]{3,2,1,0:T(8,128)S(1)}, f32[2,4,32,512]{3,2,1,0:T(8,128)S(1)}, u32[]{:S(2)}, u32[]{:S(2)}) collective-permute-start(f32[2,4,32,512]{3,2,1,0:T(8,128)S(1)} %collective-permute-done.2.refs_1_.refs_4_), channel_id=1, source_target_pairs={{0,64},{64,0},{128,192},{192,128},{256,320},{320,256},{384,448},{4... | collective-permute-start | bytes 1572872 | tf_op jit(solution)/shard_map/ppermute | solution.py:243
  57.2 0.8 copy-done.6
  58.0 1.9 %collective-permute-start.9 = (f32[16,32,512]{2,1,0:T(8,128)S(1)}, f32[16,32,512]{2,1,0:T(8,128)}, u32[]{:S(2)}, u32[]{:S(2)}) collective-permute-start(f32[16,32,512]{2,1,0:T(8,128)S(1)} %reshape.22.refs_4_.refs_7_.refs_10_.refs_13_.refs_3_.refs_6_.refs_9_.refs_12_.refs_11_.refs_15_), channel_id=1, source_target_pairs={{0,8},{1,9},{2,10},{3,11},{4,12},{5,13},{6,14},{7,15},{8,0},{9,1},... | collective-permute-start | bytes 3145736 | tf_op jit(solution)/shard_map/ppermute | solution.py:246
  59.9 23.8 %collective-permute-done.6.refs_5_.refs_8_.refs_11_.refs_14_.refs_4_.refs_7_.refs_10_.refs_13_.refs_12_.refs_16_ = f32[16,32,512]{2,1,0:T(8,128)S(1)} collective-permute-done((f32[16,32,512]{2,1,0:T(8,128)S(1)}, f32[16,32,512]{2,1,0:T(8,128)S(1)}, u32[]{:S(2)}, u32[]{:S(2)}) %collective-permute-start.6) | collective-permute-done | bytes 1048608 | tf_op jit(solution)/shard_map/ppermute | solution.py:241
  83.8 0.0 collective-permute-done.5.refs_2_.refs_7_
  83.8 0.0 collective-permute-done.3.refs_1_.refs_6_
  83.8 0.8 copy-done.8
  84.6 0.8 copy-done.10
  85.4 1.9 %collective-permute-start.10 = (f32[16,32,512]{2,1,0:T(8,128)S(1)}, f32[16,32,512]{2,1,0:T(8,128)S(1)}, u32[]{:S(2)}, u32[]{:S(2)}) collective-permute-start(f32[16,32,512]{2,1,0:T(8,128)S(1)} %collective-permute-done.6.refs_5_.refs_8_.refs_11_.refs_14_.refs_4_.refs_7_.refs_10_.refs_13_.refs_12_.refs_16_), channel_id=1, source_target_pairs={{0,8},{1,9},{2,10},{3,11},{4,12},{5,13},{6,14},{7,15},{8,0},{9,1},... | collective-permute-start | bytes 3145736 | tf_op jit(solution)/shard_map/ppermute | solution.py:249
  87.3 1.9 %collective-permute-start.7 = (f32[2,4,32,512]{3,2,1,0:T(8,128)}, f32[2,4,32,512]{3,2,1,0:T(8,128)S(1)}, u32[]{:S(2)}, u32[]{:S(2)}) collective-permute-start(f32[2,4,32,512]{3,2,1,0:T(8,128)} %copy-done.10), channel_id=1, source_target_pairs={{0,448},{64,128},{128,64},{192,256},{256,192},{320,384},{384,320},... | collective-permute-start | bytes 1572872 | tf_op jit(solution)/shard_map/ppermute | solution.py:243
  89.3 1.9 %collective-permute-start.8 = (f32[2,4,32,512]{3,2,1,0:T(8,128)}, f32[2,4,32,512]{3,2,1,0:T(8,128)S(1)}, u32[]{:S(2)}, u32[]{:S(2)}) collective-permute-start(f32[2,4,32,512]{3,2,1,0:T(8,128)} %copy-done.8), channel_id=1, source_target_pairs={{0,64},{64,0},{128,192},{192,128},{256,320},{320,256},{384,448},{4... | collective-permute-start | bytes 1572872 | tf_op jit(solution)/shard_map/ppermute | solution.py:243
  91.2 0.7 dynamic-slice_bitcast_fusion
  91.9 0.7 dynamic-slice_bitcast_fusion.1
  92.6 0.1 pad_add_fusion.refs_0_
  92.7 0.0 collective-permute-done.9.refs_6_.refs_9_.refs_12_.refs_15_.refs_5_.refs_8_.refs_11_.refs_14_.refs_13_.refs_17_
  92.7 1.0 copy-done.1
  93.7 0.9 copy-done.3
  94.7 2.4 %shard_map.47 = (f32[8,32,512]{2,1,0:T(8,128)S(1)}, f32[8,32,512]{2,1,0:T(8,128)S(1)}) custom-call(s32[20]{0:T(128)S(1)} %pad_add_fusion.refs_0_, f32[2,4,32,512]{3,2,1,0:T(8,128)S(1)} %bitcast.14, f32[1,4,32,512]{3,2,1,0:T(8,128)S(1)} %collective-permute-done.refs_2_, f32[1,4,32,512]{3,2,1,0:T(8,128)S(1)} %copy-done.3, ...), custom_call_target="tpu_custom_call" | custom-call | flops 603979776 | bytes 1572864 | tf_op jit(solution)/shard_map/pallas_call | solution.py:200
  97.1 2.4 %shard_map.48 = (f32[8,32,512]{2,1,0:T(8,128)S(1)}, f32[8,32,512]{2,1,0:T(8,128)S(1)}) custom-call(s32[20]{0:T(128)S(1)} %pad_add_fusion.refs_0_, f32[2,4,32,512]{3,2,1,0:T(8,128)S(1)} %copy-done.7, f32[2,4,32,512]{3,2,1,0:T(8,128)S(1)} %copy-done.5, ...), custom_call_target="tpu_custom_call" | custom-call | flops 603979776 | bytes 1572864 | tf_op jit(solution)/shard_map/pallas_call | solution.py:200
  99.5 2.4 %shard_map.49 = (f32[8,32,512]{2,1,0:T(8,128)S(1)}, f32[8,32,512]{2,1,0:T(8,128)S(1)}) custom-call(s32[20]{0:T(128)S(1)} %pad_add_fusion.refs_0_, f32[2,4,32,512]{3,2,1,0:T(8,128)S(1)} %copy-done.11, f32[2,4,32,512]{3,2,1,0:T(8,128)S(1)} %copy-done.9, ...), custom_call_target="tpu_custom_call" | custom-call | flops 603979776 | bytes 1572864 | tf_op jit(solution)/shard_map/pallas_call | solution.py:200
  101.9 8.6 %collective-permute-done.10.refs_8_.refs_9_.refs_10_.refs_11_.refs_12_.refs_13_.refs_14_.refs_15_.refs_16_.refs_17_.refs_18_.refs_19_.refs_6_ = f32[16,32,512]{2,1,0:T(8,128)S(1)} collective-permute-done((f32[16,32,512]{2,1,0:T(8,128)S(1)}, f32[16,32,512]{2,1,0:T(8,128)S(1)}, u32[]{:S(2)}, u32[]{:S(2)}) %collective-permute-start.10) | collective-permute-done | bytes 1048608 | tf_op jit(solution)/shard_map/ppermute | solution.py:249
  110.5 1.4 shard_map.50
  112.0 0.0 collective-permute-done.7.refs_1_
  112.0 0.0 collective-permute-done.8.refs_2_
  112.0 2.5 %shard_map.51 = (f32[8,32,512]{2,1,0:T(8,128)S(1)}, f32[8,32,512]{2,1,0:T(8,128)S(1)}) custom-call(s32[20]{0:T(128)S(1)} %pad_add_fusion.refs_0_, f32[2,4,32,512]{3,2,1,0:T(8,128)S(1)} %collective-permute-done.7.refs_1_, f32[2,4,32,512]{3,2,1,0:T(8,128)S(1)} %collective-permute-done.8.refs_2_, ...), custom_call_target="tpu_custom_call" | custom-call | flops 805306368 | bytes 2097152 | tf_op jit(solution)/shard_map/pallas_call | solution.py:200
  114.5 4.3 %collective-permute-start.11 = (f32[8,32,512]{2,1,0:T(8,128)S(1)}, f32[8,32,512]{2,1,0:T(8,128)S(1)}, u32[]{:S(2)}, u32[]{:S(2)}) collective-permute-start(f32[8,32,512]{2,1,0:T(8,128)S(1)} %get-tuple-element.40), channel_id=1, source_target_pairs={{0,1},{1,0},{2,3},{3,2},{4,5},{5,4},{6,7},{7,6},{8,9},{9,8},{10,11... | collective-permute-start | bytes 1572872 | tf_op jit(solution)/shard_map/ppermute | solution.py:263
  118.8 1.5 collective-permute-done.11
  120.3 0.1 add.18
  120.4 35.5 %all_to_all.10 = f32[8,32,512]{2,1,0:T(8,128)S(1)} all-to-all(f32[8,32,512]{2,1,0:T(8,128)S(1)} %add.18), channel_id=1, replica_groups={{0,4,16,20,32,36,48,52},{1,5,17,21,33,37,49,53},{2,6,18,22,34,38,50,54}..., dimensions={0} | all-to-all | bytes 1048576 | tf_op jit(solution)/shard_map/all_to_all | solution.py:264
  155.9 0.1 reshape.23
  156.0 0.7 copy.8
  (22 shorter events, 0.2 us)
Async XLA Ops:
  2.3 22.9 %all-to-all-start = ((f32[8,32,512]{2,1,0:T(8,128)}), f32[8,32,512]{2,1,0:T(8,128)S(1)}, u32[]{:S(2)}, u32[]{:S(2)}) async-start(f32[8,32,512]{2,1,0:T(8,128)} %shard_map.46), calls=%async_computation | async-start | bytes 1048576 | tf_op jit(solution)/shard_map/all_to_all | solution.py:223
  25.2 58.6 %copy-start = (f32[8,32,512]{2,1,0:T(8,128)}, f32[8,32,512]{2,1,0:T(8,128)S(1)}, u32[]{:S(2)}) copy-start(f32[8,32,512]{2,1,0:T(8,128)S(1)} %all-to-all-done) | copy-start | bytes 1572868
  25.3 12.8 %collective-permute-start = (f32[1,4,32,512]{3,2,1,0:T(8,128)S(1)}, f32[1,4,32,512]{3,2,1,0:T(8,128)S(1)}, u32[]{:S(2)}, u32[]{:S(2)}) collective-permute-start(f32[1,4,32,512]{3,2,1,0:T(8,128)S(1)} %get-tuple-element.42), channel_id=1, source_target_pairs={{0,64},{64,0},{128,192},{192,128},{256,320},{320,256},{384,448},{4... | collective-permute-start | bytes 786440 | tf_op jit(solution)/shard_map/ppermute | solution.py:243
  28.9 9.2 %collective-permute-start.1 = (f32[1,4,32,512]{3,2,1,0:T(8,128)S(1)}, f32[1,4,32,512]{3,2,1,0:T(8,128)S(1)}, u32[]{:S(2)}, u32[]{:S(2)}) collective-permute-start(f32[1,4,32,512]{3,2,1,0:T(8,128)S(1)} %get-tuple-element.41), channel_id=1, source_target_pairs={{0,448},{64,128},{128,64},{192,256},{256,192},{320,384},{384,320},... | collective-permute-start | bytes 786440 | tf_op jit(solution)/shard_map/ppermute | solution.py:243
  34.4 49.4 %collective-permute-start.6 = (f32[16,32,512]{2,1,0:T(8,128)S(1)}, f32[16,32,512]{2,1,0:T(8,128)S(1)}, u32[]{:S(2)}, u32[]{:S(2)}) collective-permute-start(f32[16,32,512]{2,1,0:T(8,128)S(1)} %reshape.22.refs_4_.refs_7_.refs_10_.refs_13_.refs_3_.refs_6_.refs_9_.refs_12_.refs_11_.refs_15_), channel_id=1, source_target_pairs={{0,2},{1,3},{2,0},{3,1},{4,6},{5,7},{6,4},{7,5},{8,10},{9,11},{10,... | collective-permute-start | bytes 3145736 | tf_op jit(solution)/shard_map/ppermute | solution.py:241
  38.1 45.7 %copy-start.2 = (f32[1,4,32,512]{3,2,1,0:T(8,128)}, f32[1,4,32,512]{3,2,1,0:T(8,128)S(1)}, u32[]{:S(2)}) copy-start(f32[1,4,32,512]{3,2,1,0:T(8,128)S(1)} %collective-permute-done.1.refs_3_) | copy-start | bytes 786436
  38.2 10.4 %collective-permute-start.4 = (f32[2,4,32,512]{3,2,1,0:T(8,128)S(1)}, f32[2,4,32,512]{3,2,1,0:T(8,128)S(1)}, u32[]{:S(2)}, u32[]{:S(2)}) collective-permute-start(f32[2,4,32,512]{3,2,1,0:T(8,128)S(1)} %pad_maximum_fusion.1), channel_id=1, source_target_pairs={{0,64},{64,0},{128,192},{192,128},{256,320},{320,256},{384,448},{4... | collective-permute-start | bytes 1572872 | tf_op jit(solution)/shard_map/ppermute | solution.py:243
  40.1 15.2 %collective-permute-start.2 = (f32[2,4,32,512]{3,2,1,0:T(8,128)S(1)}, f32[2,4,32,512]{3,2,1,0:T(8,128)S(1)}, u32[]{:S(2)}, u32[]{:S(2)}) collective-permute-start(f32[2,4,32,512]{3,2,1,0:T(8,128)S(1)} %pad_maximum_fusion), channel_id=1, source_target_pairs={{0,448},{64,128},{128,64},{192,256},{256,192},{320,384},{384,320},... | collective-permute-start | bytes 1572872 | tf_op jit(solution)/shard_map/ppermute | solution.py:243
  48.6 35.2 %collective-permute-start.5 = (f32[2,4,32,512]{3,2,1,0:T(8,128)S(1)}, f32[2,4,32,512]{3,2,1,0:T(8,128)S(1)}, u32[]{:S(2)}, u32[]{:S(2)}) collective-permute-start(f32[2,4,32,512]{3,2,1,0:T(8,128)S(1)} %collective-permute-done.4.refs_2_.refs_5_), channel_id=1, source_target_pairs={{0,448},{64,128},{128,64},{192,256},{256,192},{320,384},{384,320},... | collective-permute-start | bytes 1572872 | tf_op jit(solution)/shard_map/ppermute | solution.py:243
  54.5 0.8 copy-start.4
  55.3 28.5 %collective-permute-start.3 = (f32[2,4,32,512]{3,2,1,0:T(8,128)S(1)}, f32[2,4,32,512]{3,2,1,0:T(8,128)S(1)}, u32[]{:S(2)}, u32[]{:S(2)}) collective-permute-start(f32[2,4,32,512]{3,2,1,0:T(8,128)S(1)} %collective-permute-done.2.refs_1_.refs_4_), channel_id=1, source_target_pairs={{0,64},{64,0},{128,192},{192,128},{256,320},{320,256},{384,448},{4... | collective-permute-start | bytes 1572872 | tf_op jit(solution)/shard_map/ppermute | solution.py:243
  57.2 0.8 copy-start.6
  58.0 34.6 %collective-permute-start.9 = (f32[16,32,512]{2,1,0:T(8,128)S(1)}, f32[16,32,512]{2,1,0:T(8,128)}, u32[]{:S(2)}, u32[]{:S(2)}) collective-permute-start(f32[16,32,512]{2,1,0:T(8,128)S(1)} %reshape.22.refs_4_.refs_7_.refs_10_.refs_13_.refs_3_.refs_6_.refs_9_.refs_12_.refs_11_.refs_15_), channel_id=1, source_target_pairs={{0,8},{1,9},{2,10},{3,11},{4,12},{5,13},{6,14},{7,15},{8,0},{9,1},... | collective-permute-start | bytes 3145736 | tf_op jit(solution)/shard_map/ppermute | solution.py:246
  83.8 0.8 copy-start.8
  84.6 0.8 copy-start.10
  85.4 25.1 %collective-permute-start.10 = (f32[16,32,512]{2,1,0:T(8,128)S(1)}, f32[16,32,512]{2,1,0:T(8,128)S(1)}, u32[]{:S(2)}, u32[]{:S(2)}) collective-permute-start(f32[16,32,512]{2,1,0:T(8,128)S(1)} %collective-permute-done.6.refs_5_.refs_8_.refs_11_.refs_14_.refs_4_.refs_7_.refs_10_.refs_13_.refs_12_.refs_16_), channel_id=1, source_target_pairs={{0,8},{1,9},{2,10},{3,11},{4,12},{5,13},{6,14},{7,15},{8,0},{9,1},... | collective-permute-start | bytes 3145736 | tf_op jit(solution)/shard_map/ppermute | solution.py:249
  87.3 24.6 %collective-permute-start.7 = (f32[2,4,32,512]{3,2,1,0:T(8,128)}, f32[2,4,32,512]{3,2,1,0:T(8,128)S(1)}, u32[]{:S(2)}, u32[]{:S(2)}) collective-permute-start(f32[2,4,32,512]{3,2,1,0:T(8,128)} %copy-done.10), channel_id=1, source_target_pairs={{0,448},{64,128},{128,64},{192,256},{256,192},{320,384},{384,320},... | collective-permute-start | bytes 1572872 | tf_op jit(solution)/shard_map/ppermute | solution.py:243
  89.3 22.7 %collective-permute-start.8 = (f32[2,4,32,512]{3,2,1,0:T(8,128)}, f32[2,4,32,512]{3,2,1,0:T(8,128)S(1)}, u32[]{:S(2)}, u32[]{:S(2)}) collective-permute-start(f32[2,4,32,512]{3,2,1,0:T(8,128)} %copy-done.8), channel_id=1, source_target_pairs={{0,64},{64,0},{128,192},{192,128},{256,320},{320,256},{384,448},{4... | collective-permute-start | bytes 1572872 | tf_op jit(solution)/shard_map/ppermute | solution.py:243
  92.7 1.0 copy-start.1
  93.7 0.9 copy-start.3
  94.7 2.4 %copy-start.5 = (f32[2,4,32,512]{3,2,1,0:T(8,128)S(1)}, f32[2,4,32,512]{3,2,1,0:T(8,128)}, u32[]{:S(2)}) copy-start(f32[2,4,32,512]{3,2,1,0:T(8,128)} %copy-done.4) | copy-start | bytes 1572868
  94.7 2.4 %copy-start.7 = (f32[2,4,32,512]{3,2,1,0:T(8,128)S(1)}, f32[2,4,32,512]{3,2,1,0:T(8,128)}, u32[]{:S(2)}) copy-start(f32[2,4,32,512]{3,2,1,0:T(8,128)} %copy-done.6) | copy-start | bytes 1572868
  97.1 2.4 %copy-start.9 = (f32[2,4,32,512]{3,2,1,0:T(8,128)S(1)}, f32[2,4,32,512]{3,2,1,0:T(8,128)}, u32[]{:S(2)}) copy-start(f32[2,4,32,512]{3,2,1,0:T(8,128)} %copy-done.8) | copy-start | bytes 1572868
  97.1 2.4 %copy-start.11 = (f32[2,4,32,512]{3,2,1,0:T(8,128)S(1)}, f32[2,4,32,512]{3,2,1,0:T(8,128)}, u32[]{:S(2)}) copy-start(f32[2,4,32,512]{3,2,1,0:T(8,128)} %copy-done.10) | copy-start | bytes 1572868
  114.5 5.8 %collective-permute-start.11 = (f32[8,32,512]{2,1,0:T(8,128)S(1)}, f32[8,32,512]{2,1,0:T(8,128)S(1)}, u32[]{:S(2)}, u32[]{:S(2)}) collective-permute-start(f32[8,32,512]{2,1,0:T(8,128)S(1)} %get-tuple-element.40), channel_id=1, source_target_pairs={{0,1},{1,0},{2,3},{3,2},{4,5},{5,4},{6,7},{7,6},{8,9},{9,8},{10,11... | collective-permute-start | bytes 1572872 | tf_op jit(solution)/shard_map/ppermute | solution.py:263

commit v7 on v3

--- a/solution.py
+++ b/solution.py
@@ -225,10 +225,10 @@
     occupied = ks * ZL * Y
     pairs = kj // occupied
     own_w = w_ovov.reshape(cs, wb, occupied, pairs).transpose(2, 0, 3, 1).reshape(ZL * Y, rows, pairs * wb)
+    own, own_w = lax.optimization_barrier((own, own_w))
     swap_core = col_perm(lambda x, zh, c: (x, zh, 1 - c))
     swap_x = col_perm(lambda x, zh, c: (x ^ 1, zh, c))
     w_x = lax.ppermute(own_w, "col", swap_x)
-    w_c = lax.ppermute(own_w, "col", swap_core)
 
     meets = [[row_perm(lambda z, q, f=f: (z, f(q))) for f in pair] for pair in MEETS]
     halves = [own[:1], own[1:]]
@@ -236,6 +236,8 @@
     for step in range(1, Y // 2 + 1):
         moved = [lax.ppermute(h, "row", meets[n][(step + 1) % 2]) for n, h in enumerate(halves)]
         if step == 1:
+            *moved, held_w = lax.optimization_barrier((*moved, own_w))
+            w_c = lax.ppermute(held_w, "col", swap_core)
             got[0] += tuple(moved)
             halves = [jnp.concatenate([h, m]) for h, m in zip(halves, moved)]
         else:

time: 153 us -> 154 us (level)
  the two profiles are of different devices: /device:TPU:1 before, /device:TPU:22 now
where the time goes in v7:
time: 154 us; the launch traced here: 153 us
  blocking collectives  55.1 us (36%)
  starting transfers between devices  41.3 us (27%)
  waiting for transfers between devices  27.3 us (18%)
  local copies, waits for them, and re-layouts  16.2 us (11%)
  Pallas kernels  12.9 us (8%)
    all_to_all x1, blocking collectives, shards(): lax.all_to_all(acc, 'col', 0, 0, tiled=True, axis_index_groups=PEER_GROUPS)  55.1 us
    ppermute x8, starting transfers between devices, shards(): lax.ppermute(h, 'row', meets[n][(step + 1) % 2])  29.5 us
    ppermute x8, waiting for transfers between devices, shards(): lax.ppermute(h, 'row', meets[n][(step + 1) % 2])  27.3 us
    pallas_call x4, Pallas kernels, multiply(): pl.pallas_call(functools.partial(multiply_kernel, acc is not None, blocks...  10.7 us
    all_to_all x1, starting transfers between devices, shards(): lax.all_to_all(sent, ('row', 'col'), 0, 0, tiled=True, axis_index_groups=...  6.02 us
    unnamed x9, local copies, waits for them, and re-layouts  5.61 us
    transpose x1, local copies, waits for them, and re-layouts, shards(): w_ovov.reshape(cs, wb, occupied, pairs).transpose(2, 0, 3, 1)  4.77 us
    reshape x1, local copies, waits for them, and re-layouts, shards(): w_ovov.reshape(cs, wb, occupied, pairs).transpose(2, 0, 3, 1)  3.54 us
  transfers between devices with their start and end apart: 12, of which 5 were waited for; matrix products, arithmetic and copies ran while one was open for 9% of the time, Pallas kernels for 5%

profile of v7, /device:TPU:22, one launch (start us, length us, event | category | flops | bytes accessed | tf_op | source)
XLA Modules:
  0.0 153.2 jit_solution(9568830160227257160)
XLA Ops:
  0.0 2.3 %shard_map.46 = f32[8,32,512]{2,1,0:T(8,128)} custom-call(f32[4,32,512]{2,1,0:T(8,128)} %bitcast.16), custom_call_target="tpu_custom_call" | custom-call | flops 201326592 | bytes 524288 | tf_op jit(solution)/shard_map/pallas_call | solution.py:147
  2.3 6.0 %all-to-all-start = ((f32[8,32,512]{2,1,0:T(8,128)}), f32[8,32,512]{2,1,0:T(8,128)S(1)}, u32[]{:S(2)}, u32[]{:S(2)}) async-start(f32[8,32,512]{2,1,0:T(8,128)} %shard_map.46), calls=%async_computation | async-start | bytes 1048576 | tf_op jit(solution)/shard_map/all_to_all | solution.py:220
  8.3 3.6 %copy.6 = f32[8,32,1024]{1,2,0:T(8,128)} copy(f32[8,32,1024]{2,1,0:T(8,128)} %param.5) | data formatting | bytes 2097152 | tf_op args[1]
  11.9 4.8 %copy.7 = f32[64,8,16,32]{3,2,1,0:T(8,128)} copy(f32[64,8,16,32]{3,2,0,1:T(8,128)} %bitcast.14) | data formatting | bytes 2097152 | tf_op jit(solution)/shard_map/transpose | solution.py:227
  16.7 3.5 %reshape.18.refs_4_.refs_8_.refs_12_.refs_16_.refs_3_.refs_7_.refs_11_.refs_15_ = f32[16,32,512]{2,1,0:T(8,128)S(1)} reshape(f32[64,8,16,32]{3,2,1,0:T(8,128)} %copy.7) | data formatting | bytes 2097152 | tf_op jit(solution)/shard_map/reshape | solution.py:227
  20.2 0.0 all-to-all-done
  20.2 0.0 copy-start
  20.3 2.2 %collective-permute-start = (f32[1,4,32,512]{3,2,1,0:T(8,128)S(1)}, f32[1,4,32,512]{3,2,1,0:T(8,128)S(1)}, u32[]{:S(2)}, u32[]{:S(2)}) collective-permute-start(f32[1,4,32,512]{3,2,1,0:T(8,128)S(1)} %get-tuple-element.24), channel_id=1, source_target_pairs={{0,64},{64,0},{128,192},{192,128},{256,320},{320,256},{384,448},{4... | collective-permute-start | bytes 786440 | tf_op jit(solution)/shard_map/ppermute | solution.py:237
  22.5 0.0 copy-done
  22.5 5.0 %collective-permute-start.1 = (f32[1,4,32,512]{3,2,1,0:T(8,128)S(1)}, f32[1,4,32,512]{3,2,1,0:T(8,128)S(1)}, u32[]{:S(2)}, u32[]{:S(2)}) collective-permute-start(f32[1,4,32,512]{3,2,1,0:T(8,128)S(1)} %get-tuple-element.23), channel_id=1, source_target_pairs={{0,448},{64,128},{128,64},{192,256},{256,192},{320,384},{384,320},... | collective-permute-start | bytes 786440 | tf_op jit(solution)/shard_map/ppermute | solution.py:237
  27.5 1.9 %collective-permute-start.4 = (f32[16,32,512]{2,1,0:T(8,128)S(1)}, f32[16,32,512]{2,1,0:T(8,128)S(1)}, u32[]{:S(2)}, u32[]{:S(2)}) collective-permute-start(f32[16,32,512]{2,1,0:T(8,128)S(1)} %reshape.18.refs_4_.refs_8_.refs_12_.refs_16_.refs_3_.refs_7_.refs_11_.refs_15_), channel_id=1, source_target_pairs={{0,8},{1,9},{2,10},{3,11},{4,12},{5,13},{6,14},{7,15},{8,0},{9,1},... | collective-permute-start | bytes 3145736 | tf_op jit(solution)/shard_map/ppermute | solution.py:231
  29.4 1.1 collective-permute-done.refs_2_
  30.5 3.3 %collective-permute-done.1.refs_3_ = f32[1,4,32,512]{3,2,1,0:T(8,128)S(1)} collective-permute-done((f32[1,4,32,512]{3,2,1,0:T(8,128)S(1)}, f32[1,4,32,512]{3,2,1,0:T(8,128)S(1)}, u32[]{:S(2)}, u32[]{:S(2)}) %collective-permute-start.1) | collective-permute-done | bytes 262176 | tf_op jit(solution)/shard_map/ppermute | solution.py:237
  33.8 0.0 copy-start.2
  33.8 1.9 %collective-permute-start.5 = (f32[16,32,512]{2,1,0:T(8,128)S(1)}, f32[16,32,512]{2,1,0:T(8,128)S(1)}, u32[]{:S(2)}, u32[]{:S(2)}) collective-permute-start(f32[16,32,512]{2,1,0:T(8,128)S(1)} %reshape.18.refs_4_.refs_8_.refs_12_.refs_16_.refs_3_.refs_7_.refs_11_.refs_15_), channel_id=1, source_target_pairs={{0,1},{1,0},{2,3},{3,2},{4,5},{5,4},{6,7},{7,6},{8,9},{9,8},{10,11... | collective-permute-start | bytes 3145736 | tf_op jit(solution)/shard_map/ppermute | solution.py:240
  35.8 4.4 %collective-permute-start.3 = (f32[2,4,32,512]{3,2,1,0:T(8,128)S(1)}, f32[2,4,32,512]{3,2,1,0:T(8,128)}, u32[]{:S(2)}, u32[]{:S(2)}) collective-permute-start(f32[2,4,32,512]{3,2,1,0:T(8,128)S(1)} %pad_maximum_fusion.1), channel_id=1, source_target_pairs={{0,64},{64,0},{128,192},{192,128},{256,320},{320,256},{384,448},{4... | collective-permute-start | bytes 1572872 | tf_op jit(solution)/shard_map/ppermute | solution.py:237
  40.2 3.1 %collective-permute-start.2 = (f32[2,4,32,512]{3,2,1,0:T(8,128)S(1)}, f32[2,4,32,512]{3,2,1,0:T(8,128)}, u32[]{:S(2)}, u32[]{:S(2)}) collective-permute-start(f32[2,4,32,512]{3,2,1,0:T(8,128)S(1)} %pad_maximum_fusion), channel_id=1, source_target_pairs={{0,448},{64,128},{128,64},{192,256},{256,192},{320,384},{384,320},... | collective-permute-start | bytes 1572872 | tf_op jit(solution)/shard_map/ppermute | solution.py:237
  43.4 9.5 %collective-permute-done.3.refs_2_ = f32[2,4,32,512]{3,2,1,0:T(8,128)} collective-permute-done((f32[2,4,32,512]{3,2,1,0:T(8,128)S(1)}, f32[2,4,32,512]{3,2,1,0:T(8,128)}, u32[]{:S(2)}, u32[]{:S(2)}) %collective-permute-start.3) | collective-permute-done | bytes 524320 | tf_op jit(solution)/shard_map/ppermute | solution.py:237
  52.8 3.4 %collective-permute-done.2.refs_1_ = f32[2,4,32,512]{3,2,1,0:T(8,128)} collective-permute-done((f32[2,4,32,512]{3,2,1,0:T(8,128)S(1)}, f32[2,4,32,512]{3,2,1,0:T(8,128)}, u32[]{:S(2)}, u32[]{:S(2)}) %collective-permute-start.2) | collective-permute-done | bytes 524320 | tf_op jit(solution)/shard_map/ppermute | solution.py:237
  56.3 0.0 collective-permute-done.4.refs_5_.refs_9_.refs_13_.refs_17_.refs_4_.refs_8_.refs_12_.refs_16_
  56.3 0.0 collective-permute-done.5.refs_6_.refs_10_.refs_14_.refs_18_.refs_5_.refs_9_.refs_13_.refs_17_
  56.3 0.0 copy-done.2
  56.3 1.9 %collective-permute-start.10 = (f32[16,32,512]{2,1,0:T(8,128)S(1)}, f32[16,32,512]{2,1,0:T(8,128)}, u32[]{:S(2)}, u32[]{:S(2)}) collective-permute-start(f32[16,32,512]{2,1,0:T(8,128)S(1)} %collective-permute-done.4.refs_5_.refs_9_.refs_13_.refs_17_.refs_4_.refs_8_.refs_12_.refs_16_), channel_id=1, source_target_pairs={{0,1},{1,0},{2,3},{3,2},{4,5},{5,4},{6,7},{7,6},{8,9},{9,8},{10,11... | collective-permute-start | bytes 3145736 | tf_op jit(solution)/shard_map/ppermute | solution.py:249
  58.2 3.4 %collective-permute-start.6 = (f32[2,4,32,512]{3,2,1,0:T(8,128)}, f32[2,4,32,512]{3,2,1,0:T(8,128)}, u32[]{:S(2)}, u32[]{:S(2)}) collective-permute-start(f32[2,4,32,512]{3,2,1,0:T(8,128)} %collective-permute-done.2.refs_1_), channel_id=1, source_target_pairs={{0,64},{64,0},{128,192},{192,128},{256,320},{320,256},{384,448},{4... | collective-permute-start | bytes 1572872 | tf_op jit(solution)/shard_map/ppermute | solution.py:237
  61.6 3.1 %collective-permute-start.8 = (f32[2,4,32,512]{3,2,1,0:T(8,128)}, f32[2,4,32,512]{3,2,1,0:T(8,128)}, u32[]{:S(2)}, u32[]{:S(2)}) collective-permute-start(f32[2,4,32,512]{3,2,1,0:T(8,128)} %collective-permute-done.3.refs_2_), channel_id=1, source_target_pairs={{0,448},{64,128},{128,64},{192,256},{256,192},{320,384},{384,320},... | collective-permute-start | bytes 1572872 | tf_op jit(solution)/shard_map/ppermute | solution.py:237
  64.8 10.0 %collective-permute-done.6.refs_1_ = f32[2,4,32,512]{3,2,1,0:T(8,128)} collective-permute-done((f32[2,4,32,512]{3,2,1,0:T(8,128)}, f32[2,4,32,512]{3,2,1,0:T(8,128)}, u32[]{:S(2)}, u32[]{:S(2)}) %collective-permute-start.6) | collective-permute-done | bytes 524320 | tf_op jit(solution)/shard_map/ppermute | solution.py:237
  74.7 3.1 %collective-permute-start.7 = (f32[2,4,32,512]{3,2,1,0:T(8,128)}, f32[2,4,32,512]{3,2,1,0:T(8,128)S(1)}, u32[]{:S(2)}, u32[]{:S(2)}) collective-permute-start(f32[2,4,32,512]{3,2,1,0:T(8,128)} %collective-permute-done.6.refs_1_), channel_id=1, source_target_pairs={{0,448},{64,128},{128,64},{192,256},{256,192},{320,384},{384,320},... | collective-permute-start | bytes 1572872 | tf_op jit(solution)/shard_map/ppermute | solution.py:237
  77.9 0.0 collective-permute-done.8.refs_2_
  77.9 5.1 %collective-permute-start.9 = (f32[2,4,32,512]{3,2,1,0:T(8,128)}, f32[2,4,32,512]{3,2,1,0:T(8,128)S(1)}, u32[]{:S(2)}, u32[]{:S(2)}) collective-permute-start(f32[2,4,32,512]{3,2,1,0:T(8,128)} %collective-permute-done.8.refs_2_), channel_id=1, source_target_pairs={{0,64},{64,0},{128,192},{192,128},{256,320},{320,256},{384,448},{4... | collective-permute-start | bytes 1572872 | tf_op jit(solution)/shard_map/ppermute | solution.py:237
  83.0 0.7 dynamic-slice_bitcast_fusion.1
  83.7 0.7 dynamic-slice_bitcast_fusion
  84.4 0.1 pad_add_fusion.refs_0_
  84.5 0.0 collective-permute-done.10.refs_7_.refs_11_.refs_15_.refs_19_.refs_6_.refs_10_.refs_14_.refs_18_
  84.5 0.0 copy-start.1
  84.5 1.0 copy-done.1
  85.5 0.0 copy-start.3
  85.5 0.9 copy-done.3
  86.5 2.5 %shard_map.47.refs_19_ = f32[16,32,512]{2,1,0:T(8,128)S(1)} custom-call(s32[20]{0:T(128)S(1)} %pad_add_fusion.refs_0_, f32[2,4,32,512]{3,2,1,0:T(8,128)S(1)} %bitcast.13, f32[1,4,32,512]{3,2,1,0:T(8,128)S(1)} %collective-permute-done.refs_2_, f32[1,4,32,512]{3,2,1,0:T(8,128)S(1)} %copy-done.3, ...), custom_call_target="tpu_custom_call" | custom-call | flops 805306368 | bytes 2097152 | tf_op jit(solution)/shard_map/pallas_call | solution.py:197
  89.0 2.8 %shard_map.48.refs_19_ = f32[16,32,512]{2,1,0:T(8,128)S(1)} custom-call(s32[20]{0:T(128)S(1)} %pad_add_fusion.refs_0_, f32[2,4,32,512]{3,2,1,0:T(8,128)} %collective-permute-done.2.refs_1_, f32[2,4,32,512]{3,2,1,0:T(8,128)} %collective-permute-done.3.refs_2_, f32[16,32,512]{2,1,0:T(8,128)S(1)} %reshape.18.refs_4_.refs_8_.refs_12_.refs_16_.refs_3_.refs_7_.refs_11_.refs_15_, ...), custom_call_target="tpu_custom_call" | custom-call | flops 805306368 | bytes 2097152 | tf_op jit(solution)/shard_map/pallas_call | solution.py:197
  91.8 2.8 %shard_map.49.refs_19_ = f32[16,32,512]{2,1,0:T(8,128)S(1)} custom-call(s32[20]{0:T(128)S(1)} %pad_add_fusion.refs_0_, f32[2,4,32,512]{3,2,1,0:T(8,128)} %collective-permute-done.6.refs_1_, f32[2,4,32,512]{3,2,1,0:T(8,128)} %collective-permute-done.8.refs_2_, f32[16,32,512]{2,1,0:T(8,128)S(1)} %reshape.18.refs_4_.refs_8_.refs_12_.refs_16_.refs_3_.refs_7_.refs_11_.refs_15_, ...), custom_call_target="tpu_custom_call" | custom-call | flops 805306368 | bytes 2097152 | tf_op jit(solution)/shard_map/pallas_call | solution.py:197
  94.7 0.0 collective-permute-done.7.refs_1_
  94.7 0.0 collective-permute-done.9.refs_2_
  94.7 2.5 %shard_map.50 = f32[16,32,512]{2,1,0:T(8,128)S(1)} custom-call(s32[20]{0:T(128)S(1)} %pad_add_fusion.refs_0_, f32[2,4,32,512]{3,2,1,0:T(8,128)S(1)} %collective-permute-done.7.refs_1_, f32[2,4,32,512]{3,2,1,0:T(8,128)S(1)} %collective-permute-done.9.refs_2_, f32[16,32,512]{2,1,0:T(8,128)S(1)} %reshape.18.refs_4_.refs_8_.refs_12_.refs_16_.refs_3_.refs_7_.refs_11_.refs_15_, ...), custom_call_target="tpu_custom_call" | custom-call | flops 805306368 | bytes 2097152 | tf_op jit(solution)/shard_map/pallas_call | solution.py:197
  97.2 55.1 %all_to_all.10 = f32[16,32,512]{2,1,0:T(8,128)S(1)} all-to-all(f32[16,32,512]{2,1,0:T(8,128)S(1)} %shard_map.50), channel_id=1, replica_groups={{0,2,4,6,16,18,20,22,32,34,36,38,48,50,52,54},{1,3,5,7,17,19,21,23,33,3..., dimensions={0} | all-to-all | bytes 2097152 | tf_op jit(solution)/shard_map/all_to_all | solution.py:256
  152.3 0.1 reduce_sum.9
  152.4 0.1 reshape.19
  152.5 0.7 copy.8
  (3 shorter events, 0.1 us)
Async XLA Ops:
  2.3 17.9 %all-to-all-start = ((f32[8,32,512]{2,1,0:T(8,128)}), f32[8,32,512]{2,1,0:T(8,128)S(1)}, u32[]{:S(2)}, u32[]{:S(2)}) async-start(f32[8,32,512]{2,1,0:T(8,128)} %shard_map.46), calls=%async_computation | async-start | bytes 1048576 | tf_op jit(solution)/shard_map/all_to_all | solution.py:220
  20.2 2.3 %copy-start = (f32[8,32,512]{2,1,0:T(8,128)}, f32[8,32,512]{2,1,0:T(8,128)S(1)}, u32[]{:S(2)}) copy-start(f32[8,32,512]{2,1,0:T(8,128)S(1)} %all-to-all-done) | copy-start | bytes 1572868
  20.3 10.3 %collective-permute-start = (f32[1,4,32,512]{3,2,1,0:T(8,128)S(1)}, f32[1,4,32,512]{3,2,1,0:T(8,128)S(1)}, u32[]{:S(2)}, u32[]{:S(2)}) collective-permute-start(f32[1,4,32,512]{3,2,1,0:T(8,128)S(1)} %get-tuple-element.24), channel_id=1, source_target_pairs={{0,64},{64,0},{128,192},{192,128},{256,320},{320,256},{384,448},{4... | collective-permute-start | bytes 786440 | tf_op jit(solution)/shard_map/ppermute | solution.py:237
  22.5 11.3 %collective-permute-start.1 = (f32[1,4,32,512]{3,2,1,0:T(8,128)S(1)}, f32[1,4,32,512]{3,2,1,0:T(8,128)S(1)}, u32[]{:S(2)}, u32[]{:S(2)}) collective-permute-start(f32[1,4,32,512]{3,2,1,0:T(8,128)S(1)} %get-tuple-element.23), channel_id=1, source_target_pairs={{0,448},{64,128},{128,64},{192,256},{256,192},{320,384},{384,320},... | collective-permute-start | bytes 786440 | tf_op jit(solution)/shard_map/ppermute | solution.py:237
  27.5 28.8 %collective-permute-start.4 = (f32[16,32,512]{2,1,0:T(8,128)S(1)}, f32[16,32,512]{2,1,0:T(8,128)S(1)}, u32[]{:S(2)}, u32[]{:S(2)}) collective-permute-start(f32[16,32,512]{2,1,0:T(8,128)S(1)} %reshape.18.refs_4_.refs_8_.refs_12_.refs_16_.refs_3_.refs_7_.refs_11_.refs_15_), channel_id=1, source_target_pairs={{0,8},{1,9},{2,10},{3,11},{4,12},{5,13},{6,14},{7,15},{8,0},{9,1},... | collective-permute-start | bytes 3145736 | tf_op jit(solution)/shard_map/ppermute | solution.py:231
  33.8 22.4 %copy-start.2 = (f32[1,4,32,512]{3,2,1,0:T(8,128)}, f32[1,4,32,512]{3,2,1,0:T(8,128)S(1)}, u32[]{:S(2)}) copy-start(f32[1,4,32,512]{3,2,1,0:T(8,128)S(1)} %collective-permute-done.1.refs_3_) | copy-start | bytes 786436
  33.8 22.4 %collective-permute-start.5 = (f32[16,32,512]{2,1,0:T(8,128)S(1)}, f32[16,32,512]{2,1,0:T(8,128)S(1)}, u32[]{:S(2)}, u32[]{:S(2)}) collective-permute-start(f32[16,32,512]{2,1,0:T(8,128)S(1)} %reshape.18.refs_4_.refs_8_.refs_12_.refs_16_.refs_3_.refs_7_.refs_11_.refs_15_), channel_id=1, source_target_pairs={{0,1},{1,0},{2,3},{3,2},{4,5},{5,4},{6,7},{7,6},{8,9},{9,8},{10,11... | collective-permute-start | bytes 3145736 | tf_op jit(solution)/shard_map/ppermute | solution.py:240
  35.8 17.0 %collective-permute-start.3 = (f32[2,4,32,512]{3,2,1,0:T(8,128)S(1)}, f32[2,4,32,512]{3,2,1,0:T(8,128)}, u32[]{:S(2)}, u32[]{:S(2)}) collective-permute-start(f32[2,4,32,512]{3,2,1,0:T(8,128)S(1)} %pad_maximum_fusion.1), channel_id=1, source_target_pairs={{0,64},{64,0},{128,192},{192,128},{256,320},{320,256},{384,448},{4... | collective-permute-start | bytes 1572872 | tf_op jit(solution)/shard_map/ppermute | solution.py:237
  40.2 16.0 %collective-permute-start.2 = (f32[2,4,32,512]{3,2,1,0:T(8,128)S(1)}, f32[2,4,32,512]{3,2,1,0:T(8,128)}, u32[]{:S(2)}, u32[]{:S(2)}) collective-permute-start(f32[2,4,32,512]{3,2,1,0:T(8,128)S(1)} %pad_maximum_fusion), channel_id=1, source_target_pairs={{0,448},{64,128},{128,64},{192,256},{256,192},{320,384},{384,320},... | collective-permute-start | bytes 1572872 | tf_op jit(solution)/shard_map/ppermute | solution.py:237
  56.3 28.2 %collective-permute-start.10 = (f32[16,32,512]{2,1,0:T(8,128)S(1)}, f32[16,32,512]{2,1,0:T(8,128)}, u32[]{:S(2)}, u32[]{:S(2)}) collective-permute-start(f32[16,32,512]{2,1,0:T(8,128)S(1)} %collective-permute-done.4.refs_5_.refs_9_.refs_13_.refs_17_.refs_4_.refs_8_.refs_12_.refs_16_), channel_id=1, source_target_pairs={{0,1},{1,0},{2,3},{3,2},{4,5},{5,4},{6,7},{7,6},{8,9},{9,8},{10,11... | collective-permute-start | bytes 3145736 | tf_op jit(solution)/shard_map/ppermute | solution.py:249
  58.2 16.5 %collective-permute-start.6 = (f32[2,4,32,512]{3,2,1,0:T(8,128)}, f32[2,4,32,512]{3,2,1,0:T(8,128)}, u32[]{:S(2)}, u32[]{:S(2)}) collective-permute-start(f32[2,4,32,512]{3,2,1,0:T(8,128)} %collective-permute-done.2.refs_1_), channel_id=1, source_target_pairs={{0,64},{64,0},{128,192},{192,128},{256,320},{320,256},{384,448},{4... | collective-permute-start | bytes 1572872 | tf_op jit(solution)/shard_map/ppermute | solution.py:237
  61.6 16.3 %collective-permute-start.8 = (f32[2,4,32,512]{3,2,1,0:T(8,128)}, f32[2,4,32,512]{3,2,1,0:T(8,128)}, u32[]{:S(2)}, u32[]{:S(2)}) collective-permute-start(f32[2,4,32,512]{3,2,1,0:T(8,128)} %collective-permute-done.3.refs_2_), channel_id=1, source_target_pairs={{0,448},{64,128},{128,64},{192,256},{256,192},{320,384},{384,320},... | collective-permute-start | bytes 1572872 | tf_op jit(solution)/shard_map/ppermute | solution.py:237
  74.7 19.9 %collective-permute-start.7 = (f32[2,4,32,512]{3,2,1,0:T(8,128)}, f32[2,4,32,512]{3,2,1,0:T(8,128)S(1)}, u32[]{:S(2)}, u32[]{:S(2)}) collective-permute-start(f32[2,4,32,512]{3,2,1,0:T(8,128)} %collective-permute-done.6.refs_1_), channel_id=1, source_target_pairs={{0,448},{64,128},{128,64},{192,256},{256,192},{320,384},{384,320},... | collective-permute-start | bytes 1572872 | tf_op jit(solution)/shard_map/ppermute | solution.py:237
  77.9 16.8 %collective-permute-start.9 = (f32[2,4,32,512]{3,2,1,0:T(8,128)}, f32[2,4,32,512]{3,2,1,0:T(8,128)S(1)}, u32[]{:S(2)}, u32[]{:S(2)}) collective-permute-start(f32[2,4,32,512]{3,2,1,0:T(8,128)} %collective-permute-done.8.refs_2_), channel_id=1, source_target_pairs={{0,64},{64,0},{128,192},{192,128},{256,320},{320,256},{384,448},{4... | collective-permute-start | bytes 1572872 | tf_op jit(solution)/shard_map/ppermute | solution.py:237
  84.5 1.0 copy-start.1
  85.5 0.9 copy-start.3

commit v8 on v3

--- a/solution.py
+++ b/solution.py
@@ -14,6 +14,7 @@
 XH = X // GX
 MEMBERS = GX * CORES
 PEERS = XH * ZH
+LANES = 128
 F32 = jnp.float32
 BF16 = jnp.bfloat16
 
@@ -151,6 +152,62 @@
     )(t.reshape(blocks, rows, virt))
 
 
+def arrange_kernel(pairs, wb, w_ref, out_ref, mid_ref, onehot_ref):
+    ks = LANES // pairs
+    cs = w_ref.shape[0] // wb
+    wide = pairs * wb
+
+    @pl.when(pl.program_id(0) == 0)
+    def _():
+        src = lax.broadcasted_iota(jnp.int32, (wide, wide), 0)
+        dst = lax.broadcasted_iota(jnp.int32, (wide, wide), 1)
+        onehot_ref[...] = jnp.where(src == dst % wb * pairs + dst // wb, 1.0, 0.0).astype(BF16)
+
+    run = lax.broadcasted_iota(jnp.int32, (cs, LANES), 1) // pairs
+    for h in range(wb // ks):
+        tiles = [w_ref[pl.ds(h * ks + n, cs, stride=wb), :] for n in range(ks)]
+        d = 1
+        while d < ks:
+            low = run // d % 2 == 0
+            for n in range(ks):
+                if n // d % 2 == 0:
+                    a, b = tiles[n], tiles[n + d]
+                    tiles[n] = jnp.where(low, a, pltpu.roll(b, d * pairs, 1))
+                    tiles[n + d] = jnp.where(low, pltpu.roll(a, LANES - d * pairs, 1), b)
+            d *= 2
+        for n in range(ks):
+            mid_ref[n * cs : (n + 1) * cs, h * LANES : (h + 1) * LANES] = tiles[n]
+    v = mid_ref[...]
+    hi = v.astype(BF16)
+    rest = v - hi.astype(F32)
+    mid = rest.astype(BF16)
+    low = (rest - mid.astype(F32)).astype(BF16)
+    n = v.shape[0]
+    got = jnp.dot(jnp.concatenate([hi, mid, low], axis=0), onehot_ref[...], preferred_element_type=F32)
+    out_ref[...] = ((got[:n] + got[n : 2 * n]) + got[2 * n :]).reshape(out_ref.shape)
+
+
+def arrange(w, occupied, rows_of):
+    cs, wb, kj = w.shape
+    pairs = kj // occupied
+    blocks = occupied * cs // rows_of
+    steps = kj // LANES
+    return pl.pallas_call(
+        functools.partial(arrange_kernel, pairs, wb),
+        grid=(steps,),
+        in_specs=[pl.BlockSpec((cs * wb, LANES), lambda g: (0, g))],
+        out_specs=pl.BlockSpec((blocks // steps, rows_of, pairs * wb), lambda g: (g, 0, 0)),
+        out_shape=jax.ShapeDtypeStruct((blocks, rows_of, pairs * wb), F32),
+        scratch_shapes=[
+            pltpu.VMEM((LANES // pairs * cs, pairs * wb), F32),
+            pltpu.VMEM((pairs * wb, pairs * wb), BF16),
+        ],
+        cost_estimate=pl.CostEstimate(
+            flops=6 * occupied * cs * (pairs * wb) ** 2, bytes_accessed=8 * w.size, transcendentals=0
+        ),
+    )(w.reshape(cs * wb, kj))
+
+
 def multiply_kernel(has_acc, blocks, order_at, n_t, n_w, *refs):
     s_ref = refs[0]
     t_refs = refs[1 : 1 + n_t]
@@ -224,7 +281,7 @@
     depth, wb, kj = w_ovov.shape
     occupied = ks * ZL * Y
     pairs = kj // occupied
-    own_w = w_ovov.reshape(cs, wb, occupied, pairs).transpose(2, 0, 3, 1).reshape(ZL * Y, rows, pairs * wb)
+    own_w = arrange(w_ovov, occupied, rows)
     swap_core = col_perm(lambda x, zh, c: (x, zh, 1 - c))
     swap_x = col_perm(lambda x, zh, c: (x ^ 1, zh, c))
     w_x = lax.ppermute(own_w, "col", swap_x)

time: 153 us -> 150 us (0.980)
  local copies, waits for them, and re-layouts: 16.2 us -> 5.66 us
  Pallas kernels: 13.1 us -> 20.1 us
    pallas_call x0 -> x1, Pallas kernels: none -> 7.22 us  [arrange(): pl.pallas_call(functools.partial(arrange_kernel, pairs, wb), grid=(steps,...]
    transpose x1 -> x0, local copies, waits for them, and re-layouts: 4.78 us -> none  [shards(): w_ovov.reshape(cs, wb, occupied, pairs).transpose(2, 0, 3, 1)]
    reshape x1 -> x0, local copies, waits for them, and re-layouts: 3.54 us -> none  [shards(): w_ovov.reshape(cs, wb, occupied, pairs).transpose(2, 0, 3, 1)]
    unnamed x5 -> x10, local copies, waits for them, and re-layouts: 4.56 us -> 3.39 us
  transfers between devices with their start and end apart: 12 -> 12, of which waited for: 8 -> 6; matrix products, arithmetic and copies ran while one was open for 10% -> 1% of each run, Pallas kernels for 6% -> 10%
where the time goes in v8:
time: 150 us; the launch traced here: 149 us
  starting transfers between devices  46.1 us (31%)
  blocking collectives  45 us (30%)
  waiting for transfers between devices  31.3 us (21%)
  Pallas kernels  20.1 us (13%)
  local copies, waits for them, and re-layouts  5.66 us (4%)
    all_to_all x1, blocking collectives, shards(): lax.all_to_all(acc, 'col', 0, 0, tiled=True, axis_index_groups=PEER_GROUPS)  45 us
    ppermute x8, waiting for transfers between devices, shards(): lax.ppermute(h, 'row', meets[n][(step + 1) % 2])  28 us
    ppermute x8, starting transfers between devices, shards(): lax.ppermute(h, 'row', meets[n][(step + 1) % 2])  19.1 us
    all_to_all x1, starting transfers between devices, shards(): lax.all_to_all(sent, ('row', 'col'), 0, 0, tiled=True, axis_index_groups=...  17.5 us
    pallas_call x4, Pallas kernels, multiply(): pl.pallas_call(functools.partial(multiply_kernel, acc is not None, blocks...  10.7 us
    pallas_call x1, Pallas kernels, arrange(): pl.pallas_call(functools.partial(arrange_kernel, pairs, wb), grid=(steps,...  7.22 us
    ppermute x1, starting transfers between devices, shards(): w_xc = lax.ppermute(w_x, 'col', swap_core)  3.58 us
    unnamed x10, local copies, waits for them, and re-layouts  3.39 us
  transfers between devices with their start and end apart: 12, of which 6 were waited for; matrix products, arithmetic and copies ran while one was open for 1% of the time, Pallas kernels for 10%

profile of v8, /device:TPU:1, one launch (start us, length us, event | category | flops | bytes accessed | tf_op | source)
XLA Modules:
  0.0 148.5 jit_solution(3774375991509076142)
XLA Ops:
  0.0 2.2 %shard_map.46 = f32[8,32,512]{2,1,0:T(8,128)} custom-call(f32[4,32,512]{2,1,0:T(8,128)} %bitcast.14), custom_call_target="tpu_custom_call" | custom-call | flops 201326592 | bytes 524288 | tf_op jit(solution)/shard_map/pallas_call | solution.py:148
  2.2 17.5 %all-to-all-start = ((f32[8,32,512]{2,1,0:T(8,128)}), f32[8,32,512]{2,1,0:T(8,128)S(1)}, u32[]{:S(2)}, u32[]{:S(2)}) async-start(f32[8,32,512]{2,1,0:T(8,128)} %shard_map.46), calls=%async_computation | async-start | bytes 1048576 | tf_op jit(solution)/shard_map/all_to_all | solution.py:277
  19.8 7.2 %shard_map.47.refs_4_.refs_8_.refs_12_.refs_16_.refs_3_.refs_7_.refs_11_.refs_15_ = f32[16,32,512]{2,1,0:T(8,128)} custom-call(f32[256,1024]{1,0:T(8,128)} %bitcast.15), custom_call_target="tpu_custom_call" | custom-call | flops 805306368 | bytes 2097152 | tf_op jit(solution)/shard_map/pallas_call | solution.py:195
  27.0 3.3 %collective-permute-start.4 = (f32[16,32,512]{2,1,0:T(8,128)}, f32[16,32,512]{2,1,0:T(8,128)S(1)}, u32[]{:S(2)}, u32[]{:S(2)}) collective-permute-start(f32[16,32,512]{2,1,0:T(8,128)} %shard_map.47.refs_4_.refs_8_.refs_12_.refs_16_.refs_3_.refs_7_.refs_11_.refs_15_), channel_id=1, source_target_pairs={{0,8},{1,9},{2,10},{3,11},{4,12},{5,13},{6,14},{7,15},{8,0},{9,1},... | collective-permute-start | bytes 3145736 | tf_op jit(solution)/shard_map/ppermute | solution.py:287
  30.3 2.6 %collective-permute-start.5 = (f32[16,32,512]{2,1,0:T(8,128)}, f32[16,32,512]{2,1,0:T(8,128)S(1)}, u32[]{:S(2)}, u32[]{:S(2)}) collective-permute-start(f32[16,32,512]{2,1,0:T(8,128)} %shard_map.47.refs_4_.refs_8_.refs_12_.refs_16_.refs_3_.refs_7_.refs_11_.refs_15_), channel_id=1, source_target_pairs={{0,1},{1,0},{2,3},{3,2},{4,5},{5,4},{6,7},{7,6},{8,9},{9,8},{10,11... | collective-permute-start | bytes 3145736 | tf_op jit(solution)/shard_map/ppermute | solution.py:288
  32.9 0.0 all-to-all-done
  32.9 0.0 copy-start.1
  32.9 0.7 copy-done.1
  33.7 1.9 %collective-permute-start.2 = (f32[1,4,32,512]{3,2,1,0:T(8,128)S(1)}, f32[1,4,32,512]{3,2,1,0:T(8,128)S(1)}, u32[]{:S(2)}, u32[]{:S(2)}) collective-permute-start(f32[1,4,32,512]{3,2,1,0:T(8,128)S(1)} %get-tuple-element.13), channel_id=1, source_target_pairs={{0,448},{64,128},{128,64},{192,256},{256,192},{320,384},{384,320},... | collective-permute-start | bytes 786440 | tf_op jit(solution)/shard_map/ppermute | solution.py:294
  35.6 0.0 copy-start
  35.6 2.1 %collective-permute-start = (f32[1,4,32,512]{3,2,1,0:T(8,128)S(1)}, f32[1,4,32,512]{3,2,1,0:T(8,128)S(1)}, u32[]{:S(2)}, u32[]{:S(2)}) collective-permute-start(f32[1,4,32,512]{3,2,1,0:T(8,128)S(1)} %get-tuple-element.14), channel_id=1, source_target_pairs={{0,64},{64,0},{128,192},{192,128},{256,320},{320,256},{384,448},{4... | collective-permute-start | bytes 786440 | tf_op jit(solution)/shard_map/ppermute | solution.py:294
  37.6 7.0 %collective-permute-done.2.refs_3_ = f32[1,4,32,512]{3,2,1,0:T(8,128)S(1)} collective-permute-done((f32[1,4,32,512]{3,2,1,0:T(8,128)S(1)}, f32[1,4,32,512]{3,2,1,0:T(8,128)S(1)}, u32[]{:S(2)}, u32[]{:S(2)}) %collective-permute-start.2) | collective-permute-done | bytes 262176 | tf_op jit(solution)/shard_map/ppermute | solution.py:294
  44.7 1.9 %collective-permute-start.3 = (f32[2,4,32,512]{3,2,1,0:T(8,128)S(1)}, f32[2,4,32,512]{3,2,1,0:T(8,128)}, u32[]{:S(2)}, u32[]{:S(2)}) collective-permute-start(f32[2,4,32,512]{3,2,1,0:T(8,128)S(1)} %pad_maximum_fusion.1), channel_id=1, source_target_pairs={{0,64},{64,0},{128,192},{192,128},{256,320},{320,256},{384,448},{4... | collective-permute-start | bytes 1572872 | tf_op jit(solution)/shard_map/ppermute | solution.py:294
  46.6 0.0 collective-permute-done.refs_2_
  46.7 0.0 copy-start.3
  46.7 0.6 copy-done.3
  47.4 3.1 %collective-permute-start.1 = (f32[2,4,32,512]{3,2,1,0:T(8,128)S(1)}, f32[2,4,32,512]{3,2,1,0:T(8,128)}, u32[]{:S(2)}, u32[]{:S(2)}) collective-permute-start(f32[2,4,32,512]{3,2,1,0:T(8,128)S(1)} %pad_maximum_fusion), channel_id=1, source_target_pairs={{0,448},{64,128},{128,64},{192,256},{256,192},{320,384},{384,320},... | collective-permute-start | bytes 1572872 | tf_op jit(solution)/shard_map/ppermute | solution.py:294
  50.5 3.3 %collective-permute-done.4.refs_5_.refs_9_.refs_13_.refs_17_.refs_4_.refs_8_.refs_12_.refs_16_ = f32[16,32,512]{2,1,0:T(8,128)S(1)} collective-permute-done((f32[16,32,512]{2,1,0:T(8,128)}, f32[16,32,512]{2,1,0:T(8,128)S(1)}, u32[]{:S(2)}, u32[]{:S(2)}) %collective-permute-start.4) | collective-permute-done | bytes 1048608 | tf_op jit(solution)/shard_map/ppermute | solution.py:287
  53.8 0.0 collective-permute-done.5.refs_6_.refs_10_.refs_14_.refs_18_.refs_5_.refs_9_.refs_13_.refs_17_
  53.8 5.6 %collective-permute-done.3.refs_2_ = f32[2,4,32,512]{3,2,1,0:T(8,128)} collective-permute-done((f32[2,4,32,512]{3,2,1,0:T(8,128)S(1)}, f32[2,4,32,512]{3,2,1,0:T(8,128)}, u32[]{:S(2)}, u32[]{:S(2)}) %collective-permute-start.3) | collective-permute-done | bytes 524320 | tf_op jit(solution)/shard_map/ppermute | solution.py:294
  59.4 3.8 %collective-permute-done.1.refs_1_ = f32[2,4,32,512]{3,2,1,0:T(8,128)} collective-permute-done((f32[2,4,32,512]{3,2,1,0:T(8,128)S(1)}, f32[2,4,32,512]{3,2,1,0:T(8,128)}, u32[]{:S(2)}, u32[]{:S(2)}) %collective-permute-start.1) | collective-permute-done | bytes 524320 | tf_op jit(solution)/shard_map/ppermute | solution.py:294
  63.2 3.6 %collective-permute-start.10 = (f32[16,32,512]{2,1,0:T(8,128)S(1)}, f32[16,32,512]{2,1,0:T(8,128)}, u32[]{:S(2)}, u32[]{:S(2)}) collective-permute-start(f32[16,32,512]{2,1,0:T(8,128)S(1)} %collective-permute-done.4.refs_5_.refs_9_.refs_13_.refs_17_.refs_4_.refs_8_.refs_12_.refs_16_), channel_id=1, source_target_pairs={{0,1},{1,0},{2,3},{3,2},{4,5},{5,4},{6,7},{7,6},{8,9},{9,8},{10,11... | collective-permute-start | bytes 3145736 | tf_op jit(solution)/shard_map/ppermute | solution.py:304
  66.8 2.2 %collective-permute-start.6 = (f32[2,4,32,512]{3,2,1,0:T(8,128)}, f32[2,4,32,512]{3,2,1,0:T(8,128)}, u32[]{:S(2)}, u32[]{:S(2)}) collective-permute-start(f32[2,4,32,512]{3,2,1,0:T(8,128)} %collective-permute-done.1.refs_1_), channel_id=1, source_target_pairs={{0,64},{64,0},{128,192},{192,128},{256,320},{320,256},{384,448},{4... | collective-permute-start | bytes 1572872 | tf_op jit(solution)/shard_map/ppermute | solution.py:294
  69.0 2.9 %collective-permute-start.8 = (f32[2,4,32,512]{3,2,1,0:T(8,128)}, f32[2,4,32,512]{3,2,1,0:T(8,128)}, u32[]{:S(2)}, u32[]{:S(2)}) collective-permute-start(f32[2,4,32,512]{3,2,1,0:T(8,128)} %collective-permute-done.3.refs_2_), channel_id=1, source_target_pairs={{0,448},{64,128},{128,64},{192,256},{256,192},{320,384},{384,320},... | collective-permute-start | bytes 1572872 | tf_op jit(solution)/shard_map/ppermute | solution.py:294
  71.9 10.7 %collective-permute-done.6.refs_1_ = f32[2,4,32,512]{3,2,1,0:T(8,128)} collective-permute-done((f32[2,4,32,512]{3,2,1,0:T(8,128)}, f32[2,4,32,512]{3,2,1,0:T(8,128)}, u32[]{:S(2)}, u32[]{:S(2)}) %collective-permute-start.6) | collective-permute-done | bytes 524320 | tf_op jit(solution)/shard_map/ppermute | solution.py:294
  82.6 3.1 %collective-permute-start.7 = (f32[2,4,32,512]{3,2,1,0:T(8,128)}, f32[2,4,32,512]{3,2,1,0:T(8,128)S(1)}, u32[]{:S(2)}, u32[]{:S(2)}) collective-permute-start(f32[2,4,32,512]{3,2,1,0:T(8,128)} %collective-permute-done.6.refs_1_), channel_id=1, source_target_pairs={{0,448},{64,128},{128,64},{192,256},{256,192},{320,384},{384,320},... | collective-permute-start | bytes 1572872 | tf_op jit(solution)/shard_map/ppermute | solution.py:294
  85.7 0.0 collective-permute-done.8.refs_2_
  85.7 1.9 %collective-permute-start.9 = (f32[2,4,32,512]{3,2,1,0:T(8,128)}, f32[2,4,32,512]{3,2,1,0:T(8,128)S(1)}, u32[]{:S(2)}, u32[]{:S(2)}) collective-permute-start(f32[2,4,32,512]{3,2,1,0:T(8,128)} %collective-permute-done.8.refs_2_), channel_id=1, source_target_pairs={{0,64},{64,0},{128,192},{192,128},{256,320},{320,256},{384,448},{4... | collective-permute-start | bytes 1572872 | tf_op jit(solution)/shard_map/ppermute | solution.py:294
  87.6 0.7 dynamic-slice_bitcast_fusion.1
  88.3 0.7 dynamic-slice_bitcast_fusion
  89.0 0.1 pad_add_fusion.refs_0_
  89.1 0.0 collective-permute-done.10.refs_7_.refs_11_.refs_15_.refs_19_.refs_6_.refs_10_.refs_14_.refs_18_
  89.1 0.0 copy-done
  89.1 0.0 copy-start.2
  89.1 1.0 copy-done.2
  90.1 0.0 copy-start.4
  90.1 0.9 copy-done.4
  91.1 2.5 %shard_map.48.refs_19_ = f32[16,32,512]{2,1,0:T(8,128)S(1)} custom-call(s32[20]{0:T(128)S(1)} %pad_add_fusion.refs_0_, f32[2,4,32,512]{3,2,1,0:T(8,128)S(1)} %bitcast.12, f32[1,4,32,512]{3,2,1,0:T(8,128)S(1)} %copy-done.4, f32[1,4,32,512]{3,2,1,0:T(8,128)S(1)} %collective-permute-done.2.refs_3_, f32[16,32,512]{2,1,0:T(8,128)S(1)} %copy-done, ...), custom_call_target="tpu_custom_call" | custom-call | flops 805306368 | bytes 2097152 | tf_op jit(solution)/shard_map/pallas_call | solution.py:254
  93.6 2.8 %shard_map.49.refs_19_ = f32[16,32,512]{2,1,0:T(8,128)S(1)} custom-call(s32[20]{0:T(128)S(1)} %pad_add_fusion.refs_0_, f32[2,4,32,512]{3,2,1,0:T(8,128)} %collective-permute-done.1.refs_1_, f32[2,4,32,512]{3,2,1,0:T(8,128)} %collective-permute-done.3.refs_2_, f32[16,32,512]{2,1,0:T(8,128)S(1)} %copy-done, ...), custom_call_target="tpu_custom_call" | custom-call | flops 805306368 | bytes 2097152 | tf_op jit(solution)/shard_map/pallas_call | solution.py:254
  96.5 2.8 %shard_map.50.refs_19_ = f32[16,32,512]{2,1,0:T(8,128)S(1)} custom-call(s32[20]{0:T(128)S(1)} %pad_add_fusion.refs_0_, f32[2,4,32,512]{3,2,1,0:T(8,128)} %collective-permute-done.6.refs_1_, f32[2,4,32,512]{3,2,1,0:T(8,128)} %collective-permute-done.8.refs_2_, f32[16,32,512]{2,1,0:T(8,128)S(1)} %copy-done, ...), custom_call_target="tpu_custom_call" | custom-call | flops 805306368 | bytes 2097152 | tf_op jit(solution)/shard_map/pallas_call | solution.py:254
  99.3 0.0 collective-permute-done.7.refs_1_
  99.3 0.8 collective-permute-done.9.refs_2_
  100.1 2.5 %shard_map.51 = f32[16,32,512]{2,1,0:T(8,128)S(1)} custom-call(s32[20]{0:T(128)S(1)} %pad_add_fusion.refs_0_, f32[2,4,32,512]{3,2,1,0:T(8,128)S(1)} %collective-permute-done.7.refs_1_, f32[2,4,32,512]{3,2,1,0:T(8,128)S(1)} %collective-permute-done.9.refs_2_, f32[16,32,512]{2,1,0:T(8,128)S(1)} %copy-done, ...), custom_call_target="tpu_custom_call" | custom-call | flops 805306368 | bytes 2097152 | tf_op jit(solution)/shard_map/pallas_call | solution.py:254
  102.6 45.0 %all_to_all.10 = f32[16,32,512]{2,1,0:T(8,128)S(1)} all-to-all(f32[16,32,512]{2,1,0:T(8,128)S(1)} %shard_map.51), channel_id=1, replica_groups={{0,2,4,6,16,18,20,22,32,34,36,38,48,50,52,54},{1,3,5,7,17,19,21,23,33,3..., dimensions={0} | all-to-all | bytes 2097152 | tf_op jit(solution)/shard_map/all_to_all | solution.py:311
  147.6 0.1 reduce_sum.9
  147.7 0.1 reshape.17
  147.8 0.7 copy.5
  (3 shorter events, 0.1 us)
Async XLA Ops:
  2.2 30.6 %all-to-all-start = ((f32[8,32,512]{2,1,0:T(8,128)}), f32[8,32,512]{2,1,0:T(8,128)S(1)}, u32[]{:S(2)}, u32[]{:S(2)}) async-start(f32[8,32,512]{2,1,0:T(8,128)} %shard_map.46), calls=%async_computation | async-start | bytes 1048576 | tf_op jit(solution)/shard_map/all_to_all | solution.py:277
  27.0 26.8 %collective-permute-start.4 = (f32[16,32,512]{2,1,0:T(8,128)}, f32[16,32,512]{2,1,0:T(8,128)S(1)}, u32[]{:S(2)}, u32[]{:S(2)}) collective-permute-start(f32[16,32,512]{2,1,0:T(8,128)} %shard_map.47.refs_4_.refs_8_.refs_12_.refs_16_.refs_3_.refs_7_.refs_11_.refs_15_), channel_id=1, source_target_pairs={{0,8},{1,9},{2,10},{3,11},{4,12},{5,13},{6,14},{7,15},{8,0},{9,1},... | collective-permute-start | bytes 3145736 | tf_op jit(solution)/shard_map/ppermute | solution.py:287
  30.3 23.5 %collective-permute-start.5 = (f32[16,32,512]{2,1,0:T(8,128)}, f32[16,32,512]{2,1,0:T(8,128)S(1)}, u32[]{:S(2)}, u32[]{:S(2)}) collective-permute-start(f32[16,32,512]{2,1,0:T(8,128)} %shard_map.47.refs_4_.refs_8_.refs_12_.refs_16_.refs_3_.refs_7_.refs_11_.refs_15_), channel_id=1, source_target_pairs={{0,1},{1,0},{2,3},{3,2},{4,5},{5,4},{6,7},{7,6},{8,9},{9,8},{10,11... | collective-permute-start | bytes 3145736 | tf_op jit(solution)/shard_map/ppermute | solution.py:288
  32.9 0.8 copy-start.1
  33.7 11.0 %collective-permute-start.2 = (f32[1,4,32,512]{3,2,1,0:T(8,128)S(1)}, f32[1,4,32,512]{3,2,1,0:T(8,128)S(1)}, u32[]{:S(2)}, u32[]{:S(2)}) collective-permute-start(f32[1,4,32,512]{3,2,1,0:T(8,128)S(1)} %get-tuple-element.13), channel_id=1, source_target_pairs={{0,448},{64,128},{128,64},{192,256},{256,192},{320,384},{384,320},... | collective-permute-start | bytes 786440 | tf_op jit(solution)/shard_map/ppermute | solution.py:294
  35.6 53.5 %copy-start = (f32[16,32,512]{2,1,0:T(8,128)S(1)}, f32[16,32,512]{2,1,0:T(8,128)}, u32[]{:S(2)}) copy-start(f32[16,32,512]{2,1,0:T(8,128)} %shard_map.47.refs_4_.refs_8_.refs_12_.refs_16_.refs_3_.refs_7_.refs_11_.refs_15_) | copy-start | bytes 3145732
  35.6 11.1 %collective-permute-start = (f32[1,4,32,512]{3,2,1,0:T(8,128)S(1)}, f32[1,4,32,512]{3,2,1,0:T(8,128)S(1)}, u32[]{:S(2)}, u32[]{:S(2)}) collective-permute-start(f32[1,4,32,512]{3,2,1,0:T(8,128)S(1)} %get-tuple-element.14), channel_id=1, source_target_pairs={{0,64},{64,0},{128,192},{192,128},{256,320},{320,256},{384,448},{4... | collective-permute-start | bytes 786440 | tf_op jit(solution)/shard_map/ppermute | solution.py:294
  44.7 14.7 %collective-permute-start.3 = (f32[2,4,32,512]{3,2,1,0:T(8,128)S(1)}, f32[2,4,32,512]{3,2,1,0:T(8,128)}, u32[]{:S(2)}, u32[]{:S(2)}) collective-permute-start(f32[2,4,32,512]{3,2,1,0:T(8,128)S(1)} %pad_maximum_fusion.1), channel_id=1, source_target_pairs={{0,64},{64,0},{128,192},{192,128},{256,320},{320,256},{384,448},{4... | collective-permute-start | bytes 1572872 | tf_op jit(solution)/shard_map/ppermute | solution.py:294
  46.7 0.7 copy-start.3
  47.4 15.9 %collective-permute-start.1 = (f32[2,4,32,512]{3,2,1,0:T(8,128)S(1)}, f32[2,4,32,512]{3,2,1,0:T(8,128)}, u32[]{:S(2)}, u32[]{:S(2)}) collective-permute-start(f32[2,4,32,512]{3,2,1,0:T(8,128)S(1)} %pad_maximum_fusion), channel_id=1, source_target_pairs={{0,448},{64,128},{128,64},{192,256},{256,192},{320,384},{384,320},... | collective-permute-start | bytes 1572872 | tf_op jit(solution)/shard_map/ppermute | solution.py:294
  63.2 25.9 %collective-permute-start.10 = (f32[16,32,512]{2,1,0:T(8,128)S(1)}, f32[16,32,512]{2,1,0:T(8,128)}, u32[]{:S(2)}, u32[]{:S(2)}) collective-permute-start(f32[16,32,512]{2,1,0:T(8,128)S(1)} %collective-permute-done.4.refs_5_.refs_9_.refs_13_.refs_17_.refs_4_.refs_8_.refs_12_.refs_16_), channel_id=1, source_target_pairs={{0,1},{1,0},{2,3},{3,2},{4,5},{5,4},{6,7},{7,6},{8,9},{9,8},{10,11... | collective-permute-start | bytes 3145736 | tf_op jit(solution)/shard_map/ppermute | solution.py:304
  66.8 15.8 %collective-permute-start.6 = (f32[2,4,32,512]{3,2,1,0:T(8,128)}, f32[2,4,32,512]{3,2,1,0:T(8,128)}, u32[]{:S(2)}, u32[]{:S(2)}) collective-permute-start(f32[2,4,32,512]{3,2,1,0:T(8,128)} %collective-permute-done.1.refs_1_), channel_id=1, source_target_pairs={{0,64},{64,0},{128,192},{192,128},{256,320},{320,256},{384,448},{4... | collective-permute-start | bytes 1572872 | tf_op jit(solution)/shard_map/ppermute | solution.py:294
  69.0 16.7 %collective-permute-start.8 = (f32[2,4,32,512]{3,2,1,0:T(8,128)}, f32[2,4,32,512]{3,2,1,0:T(8,128)}, u32[]{:S(2)}, u32[]{:S(2)}) collective-permute-start(f32[2,4,32,512]{3,2,1,0:T(8,128)} %collective-permute-done.3.refs_2_), channel_id=1, source_target_pairs={{0,448},{64,128},{128,64},{192,256},{256,192},{320,384},{384,320},... | collective-permute-start | bytes 1572872 | tf_op jit(solution)/shard_map/ppermute | solution.py:294
  82.6 16.7 %collective-permute-start.7 = (f32[2,4,32,512]{3,2,1,0:T(8,128)}, f32[2,4,32,512]{3,2,1,0:T(8,128)S(1)}, u32[]{:S(2)}, u32[]{:S(2)}) collective-permute-start(f32[2,4,32,512]{3,2,1,0:T(8,128)} %collective-permute-done.6.refs_1_), channel_id=1, source_target_pairs={{0,448},{64,128},{128,64},{192,256},{256,192},{320,384},{384,320},... | collective-permute-start | bytes 1572872 | tf_op jit(solution)/shard_map/ppermute | solution.py:294
  85.7 14.4 %collective-permute-start.9 = (f32[2,4,32,512]{3,2,1,0:T(8,128)}, f32[2,4,32,512]{3,2,1,0:T(8,128)S(1)}, u32[]{:S(2)}, u32[]{:S(2)}) collective-permute-start(f32[2,4,32,512]{3,2,1,0:T(8,128)} %collective-permute-done.8.refs_2_), channel_id=1, source_target_pairs={{0,64},{64,0},{128,192},{192,128},{256,320},{320,256},{384,448},{4... | collective-permute-start | bytes 1572872 | tf_op jit(solution)/shard_map/ppermute | solution.py:294
  89.1 1.0 copy-start.2
  90.1 0.9 copy-start.4

commit v9 on v6

--- a/solution.py
+++ b/solution.py
@@ -14,6 +14,7 @@
 XH, ZG = X // GX, ZH // GZ
 MEMBERS = GX * GZ
 PEERS = XH * ZG
+LANES = 128
 F32 = jnp.float32
 BF16 = jnp.bfloat16
 
@@ -84,10 +85,11 @@
 SLOTS = sum(COUNTS)
 
 
+HOLD = 2
 EVERY = list(range(MEMBERS))
 LATE = [n for n, (dx, dz) in enumerate(FROM) if dx + dz == 2]
 EARLY = [n for n in EVERY if n not in LATE]
-PLAN = [((0,), EARLY), ((1,), EARLY), ((2,), EARLY), ((0, 1, 2), LATE), ((3,), EVERY)]
+PLAN = [((0,), EARLY), ((1,), EARLY), ((2,), EARLY), ((3,), EARLY), ((0, 1, 2, 3), LATE)]
 
 
 def row_table():
@@ -152,6 +154,62 @@
     )(core.reshape(1), t.reshape(blocks, rows, virt))
 
 
+def arrange_kernel(pairs, wb, w_ref, out_ref, mid_ref, onehot_ref):
+    ks = LANES // pairs
+    cs = w_ref.shape[0] // wb
+    wide = pairs * wb
+
+    @pl.when(pl.program_id(0) == 0)
+    def _():
+        src = lax.broadcasted_iota(jnp.int32, (wide, wide), 0)
+        dst = lax.broadcasted_iota(jnp.int32, (wide, wide), 1)
+        onehot_ref[...] = jnp.where(src == dst % wb * pairs + dst // wb, 1.0, 0.0).astype(BF16)
+
+    run = lax.broadcasted_iota(jnp.int32, (cs, LANES), 1) // pairs
+    for h in range(wb // ks):
+        tiles = [w_ref[pl.ds(h * ks + n, cs, stride=wb), :] for n in range(ks)]
+        d = 1
+        while d < ks:
+            low = run // d % 2 == 0
+            for n in range(ks):
+                if n // d % 2 == 0:
+                    a, b = tiles[n], tiles[n + d]
+                    tiles[n] = jnp.where(low, a, pltpu.roll(b, d * pairs, 1))
+                    tiles[n + d] = jnp.where(low, pltpu.roll(a, LANES - d * pairs, 1), b)
+            d *= 2
+        for n in range(ks):
+            mid_ref[n * cs : (n + 1) * cs, h * LANES : (h + 1) * LANES] = tiles[n]
+    v = mid_ref[...]
+    hi = v.astype(BF16)
+    rest = v - hi.astype(F32)
+    mid = rest.astype(BF16)
+    low = (rest - mid.astype(F32)).astype(BF16)
+    n = v.shape[0]
+    got = jnp.dot(jnp.concatenate([hi, mid, low], axis=0), onehot_ref[...], preferred_element_type=F32)
+    out_ref[...] = ((got[:n] + got[n : 2 * n]) + got[2 * n :]).reshape(out_ref.shape)
+
+
+def arrange(w, occupied, rows_of):
+    cs, wb, kj = w.shape
+    pairs = kj // occupied
+    blocks = occupied * cs // rows_of
+    steps = kj // LANES
+    return pl.pallas_call(
+        functools.partial(arrange_kernel, pairs, wb),
+        grid=(steps,),
+        in_specs=[pl.BlockSpec((cs * wb, LANES), lambda g: (0, g))],
+        out_specs=pl.BlockSpec((blocks // steps, rows_of, pairs * wb), lambda g: (g, 0, 0)),
+        out_shape=jax.ShapeDtypeStruct((blocks, rows_of, pairs * wb), F32),
+        scratch_shapes=[
+            pltpu.VMEM((LANES // pairs * cs, pairs * wb), F32),
+            pltpu.VMEM((pairs * wb, pairs * wb), BF16),
+        ],
+        cost_estimate=pl.CostEstimate(
+            flops=6 * occupied * cs * (pairs * wb) ** 2, bytes_accessed=8 * w.size, transcendentals=0
+        ),
+    )(w.reshape(cs * wb, kj))
+
+
 def multiply_kernel(has_acc, blocks, picks, n_t, n_w, *refs):
     s_ref = refs[0]
     t_refs = refs[1 : 1 + n_t]
@@ -227,9 +285,7 @@
     depth, wb, kj = w_ovov.shape
     occupied = ks * ZL * Y
     pairs = kj // occupied
-    w_t = w_ovov.reshape(cs, wb, occupied, pairs).transpose(2, 0, 3, 1)
-    own_w = w_t.reshape(ZL * Y, rows, pairs * wb)
-    first_w = own_w
+    own_w = arrange(w_ovov, occupied, rows)
     own, own_w = lax.optimization_barrier((own, own_w))
     swap_core = col_perm(lambda x, zh, c: (x, zh, c ^ 1))
     swap_x = col_perm(lambda x, zh, c: (x ^ 1, zh, c))
@@ -238,14 +294,16 @@
     meets = [[row_perm(lambda z, q, f=f: (z, f(q))) for f in pair] for pair in MEETS]
     halves = [own[:1], own[1:]]
     got = [(own,)]
-    near = {(0, 0): own_w, (0, 1): lax.ppermute(first_w, "col", swap_z)}
+    near = {(0, 0): own_w}
+    raw = lax.ppermute(w_ovov, "col", swap_z)
     for step in range(1, Y // 2 + 1):
         moved = [lax.ppermute(h, "row", meets[n][(step + 1) % 2]) for n, h in enumerate(halves)]
         if step == 1:
             *moved, held = lax.optimization_barrier((*moved, own_w))
             near[1, 0] = lax.ppermute(held, "col", swap_x)
-        if step == 3:
-            *moved, near[0, 1] = lax.optimization_barrier((*moved, near[0, 1]))
+        if step == HOLD:
+            *moved, raw = lax.optimization_barrier((*moved, raw))
+            near[0, 1] = arrange(raw, occupied, rows)
             near[1, 1] = lax.ppermute(near[0, 1], "col", swap_x)
         if step == 1:
             got[0] += tuple(moved)

time: 158 us -> 162 us (1.025)
  the two profiles are of different devices: /device:TPU:3 before, /device:TPU:160 now
where the time goes in v9:
time: 162 us; the launch traced here: 161 us
  starting transfers between devices  50.7 us (31%)
  waiting for transfers between devices  36.6 us (23%)
  blocking collectives  36.5 us (23%)
  Pallas kernels  29.6 us (18%)
  local copies, waits for them, and re-layouts  6.93 us (4%)
    all_to_all x1, blocking collectives, shards(): lax.all_to_all(acc, 'col', 0, 0, tiled=True, axis_index_groups=PEER_GROUPS)  36.5 us
    ppermute x8, starting transfers between devices, shards(): lax.ppermute(h, 'row', meets[n][(step + 1) % 2])  27.8 us
    all_to_all x1, waiting for transfers between devices, shards(): lax.all_to_all(sent, ('row', 'col'), 0, 0, tiled=True, axis_index_groups=...  25.1 us
    pallas_call x2, Pallas kernels, arrange(): pl.pallas_call(functools.partial(arrange_kernel, pairs, wb), grid=(steps,...  14.4 us
    pallas_call x5, Pallas kernels, multiply(): pl.pallas_call(functools.partial(multiply_kernel, acc is not None, blocks...  12.8 us
    all_to_all x1, starting transfers between devices, shards(): lax.all_to_all(sent, ('row', 'col'), 0, 0, tiled=True, axis_index_groups=...  9.66 us
    ppermute x8, waiting for transfers between devices, shards(): lax.ppermute(h, 'row', meets[n][(step + 1) % 2])  9.66 us
    unnamed x18, local copies, waits for them, and re-layouts  4.66 us
  transfers between devices with their start and end apart: 13, of which 5 were waited for; matrix products, arithmetic and copies ran while one was open for 1% of the time, Pallas kernels for 15%

profile of v9, /device:TPU:160, one launch (start us, length us, event | category | flops | bytes accessed | tf_op | source)
XLA Modules:
  0.0 160.8 jit_solution(14189640833083900862)
XLA Ops:
  0.0 2.3 %shard_map.46 = f32[8,32,512]{2,1,0:T(8,128)} custom-call(s32[1]{0:T(128)} %bitcast.2.core_ref, f32[4,32,512]{2,1,0:T(8,128)} %bitcast.14), custom_call_target="tpu_custom_call" | custom-call | flops 201326592 | bytes 524288 | tf_op jit(solution)/shard_map/pallas_call | solution.py:149
  2.3 9.7 %all-to-all-start = ((f32[8,32,512]{2,1,0:T(8,128)}), f32[8,32,512]{2,1,0:T(8,128)S(1)}, u32[]{:S(2)}, u32[]{:S(2)}) async-start(f32[8,32,512]{2,1,0:T(8,128)} %shard_map.46), calls=%async_computation | async-start | bytes 1048576 | tf_op jit(solution)/shard_map/all_to_all | solution.py:281
  12.0 4.3 %collective-permute-start.4 = (f32[8,32,1024]{2,1,0:T(8,128)S(1)}, f32[8,32,1024]{2,1,0:T(8,128)}, u32[]{:S(2)}, u32[]{:S(2)}) collective-permute-start(f32[8,32,1024]{2,1,0:T(8,128)S(1)} %copy-done.8), channel_id=1, source_target_pairs={{0,2},{1,3},{2,0},{3,1},{4,6},{5,7},{6,4},{7,5},{8,10},{9,11},{10,... | collective-permute-start | bytes 3145736 | tf_op jit(solution)/shard_map/ppermute | solution.py:298
  16.3 7.2 %shard_map.47.refs_4_.refs_7_.refs_10_.refs_13_.refs_3_.refs_6_.refs_9_.refs_12_ = f32[16,32,512]{2,1,0:T(8,128)} custom-call(f32[256,1024]{1,0:T(8,128)} %bitcast.15), custom_call_target="tpu_custom_call" | custom-call | flops 805306368 | bytes 2097152 | tf_op jit(solution)/shard_map/pallas_call | solution.py:197
  23.5 25.1 %all-to-all-done = f32[8,32,512]{2,1,0:T(8,128)S(1)} async-done(((f32[8,32,512]{2,1,0:T(8,128)}), f32[8,32,512]{2,1,0:T(8,128)S(1)}, u32[]{:S(2)}, u32[]{:S(2)}) %all-to-all-start) | async-done | bytes 524320 | tf_op jit(solution)/shard_map/all_to_all | solution.py:281
  48.6 0.8 copy-done.2
  49.4 2.2 %collective-permute-start.1 = (f32[1,4,32,512]{3,2,1,0:T(8,128)S(1)}, f32[1,4,32,512]{3,2,1,0:T(8,128)S(1)}, u32[]{:S(2)}, u32[]{:S(2)}) collective-permute-start(f32[1,4,32,512]{3,2,1,0:T(8,128)S(1)} %get-tuple-element.41), channel_id=1, source_target_pairs={{0,448},{64,128},{128,64},{192,256},{256,192},{320,384},{384,320},... | collective-permute-start | bytes 786440 | tf_op jit(solution)/shard_map/ppermute | solution.py:300
  51.6 6.3 %collective-permute-start = (f32[1,4,32,512]{3,2,1,0:T(8,128)S(1)}, f32[1,4,32,512]{3,2,1,0:T(8,128)S(1)}, u32[]{:S(2)}, u32[]{:S(2)}) collective-permute-start(f32[1,4,32,512]{3,2,1,0:T(8,128)S(1)} %get-tuple-element.42), channel_id=1, source_target_pairs={{0,64},{64,0},{128,192},{192,128},{256,320},{320,256},{384,448},{4... | collective-permute-start | bytes 786440 | tf_op jit(solution)/shard_map/ppermute | solution.py:300
  57.9 0.0 collective-permute-done.1.refs_3_
  57.9 4.3 %collective-permute-done.refs_2_ = f32[1,4,32,512]{3,2,1,0:T(8,128)S(1)} collective-permute-done((f32[1,4,32,512]{3,2,1,0:T(8,128)S(1)}, f32[1,4,32,512]{3,2,1,0:T(8,128)S(1)}, u32[]{:S(2)}, u32[]{:S(2)}) %collective-permute-start) | collective-permute-done | bytes 262176 | tf_op jit(solution)/shard_map/ppermute | solution.py:300
  62.3 0.7 copy-done.5
  63.0 3.9 %collective-permute-start.3 = (f32[2,4,32,512]{3,2,1,0:T(8,128)S(1)}, f32[2,4,32,512]{3,2,1,0:T(8,128)}, u32[]{:S(2)}, u32[]{:S(2)}) collective-permute-start(f32[2,4,32,512]{3,2,1,0:T(8,128)S(1)} %pad_maximum_fusion.1), channel_id=1, source_target_pairs={{0,64},{64,0},{128,192},{192,128},{256,320},{320,256},{384,448},{4... | collective-permute-start | bytes 1572872 | tf_op jit(solution)/shard_map/ppermute | solution.py:300
  66.9 2.3 %collective-permute-start.2 = (f32[2,4,32,512]{3,2,1,0:T(8,128)S(1)}, f32[2,4,32,512]{3,2,1,0:T(8,128)}, u32[]{:S(2)}, u32[]{:S(2)}) collective-permute-start(f32[2,4,32,512]{3,2,1,0:T(8,128)S(1)} %pad_maximum_fusion), channel_id=1, source_target_pairs={{0,448},{64,128},{128,64},{192,256},{256,192},{320,384},{384,320},... | collective-permute-start | bytes 1572872 | tf_op jit(solution)/shard_map/ppermute | solution.py:300
  69.2 0.0 copy-done
  69.2 3.7 %collective-permute-start.10 = (f32[16,32,512]{2,1,0:T(8,128)S(1)}, f32[16,32,512]{2,1,0:T(8,128)S(1)}, u32[]{:S(2)}, u32[]{:S(2)}) collective-permute-start(f32[16,32,512]{2,1,0:T(8,128)S(1)} %copy-done), channel_id=1, source_target_pairs={{0,8},{1,9},{2,10},{3,11},{4,12},{5,13},{6,14},{7,15},{8,0},{9,1},... | collective-permute-start | bytes 3145736 | tf_op jit(solution)/shard_map/ppermute | solution.py:303
  72.9 0.0 collective-permute-done.4
  72.9 2.0 %collective-permute-done.3.refs_2_.refs_5_ = f32[2,4,32,512]{3,2,1,0:T(8,128)} collective-permute-done((f32[2,4,32,512]{3,2,1,0:T(8,128)S(1)}, f32[2,4,32,512]{3,2,1,0:T(8,128)}, u32[]{:S(2)}, u32[]{:S(2)}) %collective-permute-start.3) | collective-permute-done | bytes 524320 | tf_op jit(solution)/shard_map/ppermute | solution.py:300
  74.8 3.4 %collective-permute-done.2.refs_1_.refs_4_ = f32[2,4,32,512]{3,2,1,0:T(8,128)} collective-permute-done((f32[2,4,32,512]{3,2,1,0:T(8,128)S(1)}, f32[2,4,32,512]{3,2,1,0:T(8,128)}, u32[]{:S(2)}, u32[]{:S(2)}) %collective-permute-start.2) | collective-permute-done | bytes 524320 | tf_op jit(solution)/shard_map/ppermute | solution.py:300
  78.2 3.4 %collective-permute-start.5 = (f32[2,4,32,512]{3,2,1,0:T(8,128)}, f32[2,4,32,512]{3,2,1,0:T(8,128)}, u32[]{:S(2)}, u32[]{:S(2)}) collective-permute-start(f32[2,4,32,512]{3,2,1,0:T(8,128)} %collective-permute-done.2.refs_1_.refs_4_), channel_id=1, source_target_pairs={{0,64},{64,0},{128,192},{192,128},{256,320},{320,256},{384,448},{4... | collective-permute-start | bytes 1572872 | tf_op jit(solution)/shard_map/ppermute | solution.py:300
  81.6 2.3 %collective-permute-start.6 = (f32[2,4,32,512]{3,2,1,0:T(8,128)}, f32[2,4,32,512]{3,2,1,0:T(8,128)}, u32[]{:S(2)}, u32[]{:S(2)}) collective-permute-start(f32[2,4,32,512]{3,2,1,0:T(8,128)} %collective-permute-done.3.refs_2_.refs_5_), channel_id=1, source_target_pairs={{0,448},{64,128},{128,64},{192,256},{256,192},{320,384},{384,320},... | collective-permute-start | bytes 1572872 | tf_op jit(solution)/shard_map/ppermute | solution.py:300
  83.9 7.2 %shard_map.48.refs_5_.refs_8_.refs_11_.refs_14_.refs_4_.refs_7_.refs_10_.refs_13_ = f32[16,32,512]{2,1,0:T(8,128)} custom-call(f32[256,1024]{1,0:T(8,128)} %bitcast.6.w_ref), custom_call_target="tpu_custom_call" | custom-call | flops 805306368 | bytes 2097152 | tf_op jit(solution)/shard_map/pallas_call | solution.py:197
  91.1 3.4 %collective-permute-start.9 = (f32[16,32,512]{2,1,0:T(8,128)}, f32[16,32,512]{2,1,0:T(8,128)S(1)}, u32[]{:S(2)}, u32[]{:S(2)}) collective-permute-start(f32[16,32,512]{2,1,0:T(8,128)} %shard_map.48.refs_5_.refs_8_.refs_11_.refs_14_.refs_4_.refs_7_.refs_10_.refs_13_), channel_id=1, source_target_pairs={{0,8},{1,9},{2,10},{3,11},{4,12},{5,13},{6,14},{7,15},{8,0},{9,1},... | collective-permute-start | bytes 3145736 | tf_op jit(solution)/shard_map/ppermute | solution.py:307
  94.5 0.0 collective-permute-done.5.refs_1_.refs_6_
  94.5 3.6 %collective-permute-start.7 = (f32[2,4,32,512]{3,2,1,0:T(8,128)}, f32[2,4,32,512]{3,2,1,0:T(8,128)}, u32[]{:S(2)}, u32[]{:S(2)}) collective-permute-start(f32[2,4,32,512]{3,2,1,0:T(8,128)} %collective-permute-done.5.refs_1_.refs_6_), channel_id=1, source_target_pairs={{0,448},{64,128},{128,64},{192,256},{256,192},{320,384},{384,320},... | collective-permute-start | bytes 1572872 | tf_op jit(solution)/shard_map/ppermute | solution.py:300
  98.1 0.0 collective-permute-done.6.refs_2_.refs_7_
  98.1 3.8 %collective-permute-start.8 = (f32[2,4,32,512]{3,2,1,0:T(8,128)}, f32[2,4,32,512]{3,2,1,0:T(8,128)}, u32[]{:S(2)}, u32[]{:S(2)}) collective-permute-start(f32[2,4,32,512]{3,2,1,0:T(8,128)} %collective-permute-done.6.refs_2_.refs_7_), channel_id=1, source_target_pairs={{0,64},{64,0},{128,192},{192,128},{256,320},{320,256},{384,448},{4... | collective-permute-start | bytes 1572872 | tf_op jit(solution)/shard_map/ppermute | solution.py:300
  101.9 0.7 dynamic-slice_bitcast_fusion
  102.6 0.7 dynamic-slice_bitcast_fusion.1
  103.3 0.1 pad_add_fusion.refs_0_
  103.4 0.0 collective-permute-done.10.refs_6_.refs_9_.refs_12_.refs_15_.refs_5_.refs_8_.refs_11_.refs_14_
  103.4 1.2 copy-done.1
  104.6 1.0 copy-done.3
  105.7 0.9 copy-done.6
  106.6 1.4 shard_map.49
  108.1 2.6 %shard_map.50 = (f32[8,32,512]{2,1,0:T(8,128)S(1)}, f32[8,32,512]{2,1,0:T(8,128)S(1)}) custom-call(s32[20]{0:T(128)S(1)} %pad_add_fusion.refs_0_, f32[2,4,32,512]{3,2,1,0:T(8,128)} %collective-permute-done.2.refs_1_.refs_4_, f32[2,4,32,512]{3,2,1,0:T(8,128)} %collective-permute-done.3.refs_2_.refs_5_, f32[16,32,512]{2,1,0:T(8,128)S(1)} %copy-done, ...), custom_call_target="tpu_custom_call" | custom-call | flops 603979776 | bytes 1572864 | tf_op jit(solution)/shard_map/pallas_call | solution.py:258
  110.7 2.6 %shard_map.51 = (f32[8,32,512]{2,1,0:T(8,128)S(1)}, f32[8,32,512]{2,1,0:T(8,128)S(1)}) custom-call(s32[20]{0:T(128)S(1)} %pad_add_fusion.refs_0_, f32[2,4,32,512]{3,2,1,0:T(8,128)} %collective-permute-done.5.refs_1_.refs_6_, f32[2,4,32,512]{3,2,1,0:T(8,128)} %collective-permute-done.6.refs_2_.refs_7_, f32[16,32,512]{2,1,0:T(8,128)S(1)} %copy-done, ...), custom_call_target="tpu_custom_call" | custom-call | flops 603979776 | bytes 1572864 | tf_op jit(solution)/shard_map/pallas_call | solution.py:258
  113.4 0.0 collective-permute-done.7.refs_1_.refs_8_
  113.4 0.0 collective-permute-done.8.refs_2_.refs_9_
  113.4 0.0 copy-start.7
  113.4 2.6 %shard_map.52 = (f32[8,32,512]{2,1,0:T(8,128)S(1)}, f32[8,32,512]{2,1,0:T(8,128)S(1)}) custom-call(s32[20]{0:T(128)S(1)} %pad_add_fusion.refs_0_, f32[2,4,32,512]{3,2,1,0:T(8,128)} %collective-permute-done.7.refs_1_.refs_8_, f32[2,4,32,512]{3,2,1,0:T(8,128)} %collective-permute-done.8.refs_2_.refs_9_, f32[16,32,512]{2,1,0:T(8,128)S(1)} %copy-done, ...), custom_call_target="tpu_custom_call" | custom-call | flops 603979776 | bytes 1572864 | tf_op jit(solution)/shard_map/pallas_call | solution.py:258
  116.1 0.0 collective-permute-done.9.refs_10_.refs_11_.refs_12_.refs_13_.refs_14_.refs_15_.refs_16_.refs_17_.refs_18_.refs_19_.refs_20_.refs_21_.refs_22_.refs_23_.refs_24_.refs_25_
  116.1 3.4 %shard_map.53 = (f32[8,32,512]{2,1,0:T(8,128)S(1)}, f32[8,32,512]{2,1,0:T(8,128)S(1)}) custom-call(s32[20]{0:T(128)S(1)} %pad_add_fusion.refs_0_, f32[2,4,32,512]{3,2,1,0:T(8,128)S(1)} %bitcast.12, f32[1,4,32,512]{3,2,1,0:T(8,128)S(1)} %copy-done.7, f32[1,4,32,512]{3,2,1,0:T(8,128)S(1)} %collective-permute-done.1.refs_3_, ...), custom_call_target="tpu_custom_call" | custom-call | flops 805306368 | bytes 2097152 | tf_op jit(solution)/shard_map/pallas_call | solution.py:258
  119.5 1.9 %collective-permute-start.11 = (f32[8,32,512]{2,1,0:T(8,128)S(1)}, f32[8,32,512]{2,1,0:T(8,128)S(1)}, u32[]{:S(2)}, u32[]{:S(2)}) collective-permute-start(f32[8,32,512]{2,1,0:T(8,128)S(1)} %get-tuple-element.40), channel_id=1, source_target_pairs={{0,1},{1,0},{2,3},{3,2},{4,5},{5,4},{6,7},{7,6},{8,9},{9,8},{10,11... | collective-permute-start | bytes 1572872 | tf_op jit(solution)/shard_map/ppermute | solution.py:321
  121.5 1.9 %collective-permute-done.11 = f32[8,32,512]{2,1,0:T(8,128)S(1)} collective-permute-done((f32[8,32,512]{2,1,0:T(8,128)S(1)}, f32[8,32,512]{2,1,0:T(8,128)S(1)}, u32[]{:S(2)}, u32[]{:S(2)}) %collective-permute-start.11) | collective-permute-done | bytes 524320 | tf_op jit(solution)/shard_map/ppermute | solution.py:321
  123.3 0.1 add.18
  123.4 36.5 %all_to_all.10 = f32[8,32,512]{2,1,0:T(8,128)S(1)} all-to-all(f32[8,32,512]{2,1,0:T(8,128)S(1)} %add.18), channel_id=1, replica_groups={{0,4,16,20,32,36,48,52},{1,5,17,21,33,37,49,53},{2,6,18,22,34,38,50,54}..., dimensions={0} | all-to-all | bytes 1048576 | tf_op jit(solution)/shard_map/all_to_all | solution.py:322
  160.0 0.1 reshape.23
  160.1 0.7 copy.5
  (15 shorter events, 0.2 us)
Async XLA Ops:
  0.0 12.0 %copy-start.8 = (f32[8,32,1024]{2,1,0:T(8,128)S(1)}, f32[8,32,1024]{2,1,0:T(8,128)}, u32[]{:S(2)}) copy-start(f32[8,32,1024]{2,1,0:T(8,128)} %param.5) | copy-start | bytes 3145732
  2.3 46.2 %all-to-all-start = ((f32[8,32,512]{2,1,0:T(8,128)}), f32[8,32,512]{2,1,0:T(8,128)S(1)}, u32[]{:S(2)}, u32[]{:S(2)}) async-start(f32[8,32,512]{2,1,0:T(8,128)} %shard_map.46), calls=%async_computation | async-start | bytes 1048576 | tf_op jit(solution)/shard_map/all_to_all | solution.py:281
  12.0 60.9 %collective-permute-start.4 = (f32[8,32,1024]{2,1,0:T(8,128)S(1)}, f32[8,32,1024]{2,1,0:T(8,128)}, u32[]{:S(2)}, u32[]{:S(2)}) collective-permute-start(f32[8,32,1024]{2,1,0:T(8,128)S(1)} %copy-done.8), channel_id=1, source_target_pairs={{0,2},{1,3},{2,0},{3,1},{4,6},{5,7},{6,4},{7,5},{8,10},{9,11},{10,... | collective-permute-start | bytes 3145736 | tf_op jit(solution)/shard_map/ppermute | solution.py:298
  48.5 0.8 copy-start.2
  49.4 8.6 %collective-permute-start.1 = (f32[1,4,32,512]{3,2,1,0:T(8,128)S(1)}, f32[1,4,32,512]{3,2,1,0:T(8,128)S(1)}, u32[]{:S(2)}, u32[]{:S(2)}) collective-permute-start(f32[1,4,32,512]{3,2,1,0:T(8,128)S(1)} %get-tuple-element.41), channel_id=1, source_target_pairs={{0,448},{64,128},{128,64},{192,256},{256,192},{320,384},{384,320},... | collective-permute-start | bytes 786440 | tf_op jit(solution)/shard_map/ppermute | solution.py:300
  51.6 17.6 %copy-start = (f32[16,32,512]{2,1,0:T(8,128)S(1)}, f32[16,32,512]{2,1,0:T(8,128)}, u32[]{:S(2)}) copy-start(f32[16,32,512]{2,1,0:T(8,128)} %shard_map.47.refs_4_.refs_7_.refs_10_.refs_13_.refs_3_.refs_6_.refs_9_.refs_12_) | copy-start | bytes 3145732
  51.6 10.6 %collective-permute-start = (f32[1,4,32,512]{3,2,1,0:T(8,128)S(1)}, f32[1,4,32,512]{3,2,1,0:T(8,128)S(1)}, u32[]{:S(2)}, u32[]{:S(2)}) collective-permute-start(f32[1,4,32,512]{3,2,1,0:T(8,128)S(1)} %get-tuple-element.42), channel_id=1, source_target_pairs={{0,64},{64,0},{128,192},{192,128},{256,320},{320,256},{384,448},{4... | collective-permute-start | bytes 786440 | tf_op jit(solution)/shard_map/ppermute | solution.py:300
  62.2 0.7 copy-start.5
  63.0 11.8 %collective-permute-start.3 = (f32[2,4,32,512]{3,2,1,0:T(8,128)S(1)}, f32[2,4,32,512]{3,2,1,0:T(8,128)}, u32[]{:S(2)}, u32[]{:S(2)}) collective-permute-start(f32[2,4,32,512]{3,2,1,0:T(8,128)S(1)} %pad_maximum_fusion.1), channel_id=1, source_target_pairs={{0,64},{64,0},{128,192},{192,128},{256,320},{320,256},{384,448},{4... | collective-permute-start | bytes 1572872 | tf_op jit(solution)/shard_map/ppermute | solution.py:300
  66.9 11.3 %collective-permute-start.2 = (f32[2,4,32,512]{3,2,1,0:T(8,128)S(1)}, f32[2,4,32,512]{3,2,1,0:T(8,128)}, u32[]{:S(2)}, u32[]{:S(2)}) collective-permute-start(f32[2,4,32,512]{3,2,1,0:T(8,128)S(1)} %pad_maximum_fusion), channel_id=1, source_target_pairs={{0,448},{64,128},{128,64},{192,256},{256,192},{320,384},{384,320},... | collective-permute-start | bytes 1572872 | tf_op jit(solution)/shard_map/ppermute | solution.py:300
  69.2 34.2 %collective-permute-start.10 = (f32[16,32,512]{2,1,0:T(8,128)S(1)}, f32[16,32,512]{2,1,0:T(8,128)S(1)}, u32[]{:S(2)}, u32[]{:S(2)}) collective-permute-start(f32[16,32,512]{2,1,0:T(8,128)S(1)} %copy-done), channel_id=1, source_target_pairs={{0,8},{1,9},{2,10},{3,11},{4,12},{5,13},{6,14},{7,15},{8,0},{9,1},... | collective-permute-start | bytes 3145736 | tf_op jit(solution)/shard_map/ppermute | solution.py:303
  78.2 16.3 %collective-permute-start.5 = (f32[2,4,32,512]{3,2,1,0:T(8,128)}, f32[2,4,32,512]{3,2,1,0:T(8,128)}, u32[]{:S(2)}, u32[]{:S(2)}) collective-permute-start(f32[2,4,32,512]{3,2,1,0:T(8,128)} %collective-permute-done.2.refs_1_.refs_4_), channel_id=1, source_target_pairs={{0,64},{64,0},{128,192},{192,128},{256,320},{320,256},{384,448},{4... | collective-permute-start | bytes 1572872 | tf_op jit(solution)/shard_map/ppermute | solution.py:300
  81.6 16.5 %collective-permute-start.6 = (f32[2,4,32,512]{3,2,1,0:T(8,128)}, f32[2,4,32,512]{3,2,1,0:T(8,128)}, u32[]{:S(2)}, u32[]{:S(2)}) collective-permute-start(f32[2,4,32,512]{3,2,1,0:T(8,128)} %collective-permute-done.3.refs_2_.refs_5_), channel_id=1, source_target_pairs={{0,448},{64,128},{128,64},{192,256},{256,192},{320,384},{384,320},... | collective-permute-start | bytes 1572872 | tf_op jit(solution)/shard_map/ppermute | solution.py:300
  91.1 25.0 %collective-permute-start.9 = (f32[16,32,512]{2,1,0:T(8,128)}, f32[16,32,512]{2,1,0:T(8,128)S(1)}, u32[]{:S(2)}, u32[]{:S(2)}) collective-permute-start(f32[16,32,512]{2,1,0:T(8,128)} %shard_map.48.refs_5_.refs_8_.refs_11_.refs_14_.refs_4_.refs_7_.refs_10_.refs_13_), channel_id=1, source_target_pairs={{0,8},{1,9},{2,10},{3,11},{4,12},{5,13},{6,14},{7,15},{8,0},{9,1},... | collective-permute-start | bytes 3145736 | tf_op jit(solution)/shard_map/ppermute | solution.py:307
  94.5 18.9 %collective-permute-start.7 = (f32[2,4,32,512]{3,2,1,0:T(8,128)}, f32[2,4,32,512]{3,2,1,0:T(8,128)}, u32[]{:S(2)}, u32[]{:S(2)}) collective-permute-start(f32[2,4,32,512]{3,2,1,0:T(8,128)} %collective-permute-done.5.refs_1_.refs_6_), channel_id=1, source_target_pairs={{0,448},{64,128},{128,64},{192,256},{256,192},{320,384},{384,320},... | collective-permute-start | bytes 1572872 | tf_op jit(solution)/shard_map/ppermute | solution.py:300
  98.1 15.3 %collective-permute-start.8 = (f32[2,4,32,512]{3,2,1,0:T(8,128)}, f32[2,4,32,512]{3,2,1,0:T(8,128)}, u32[]{:S(2)}, u32[]{:S(2)}) collective-permute-start(f32[2,4,32,512]{3,2,1,0:T(8,128)} %collective-permute-done.6.refs_2_.refs_7_), channel_id=1, source_target_pairs={{0,64},{64,0},{128,192},{192,128},{256,320},{320,256},{384,448},{4... | collective-permute-start | bytes 1572872 | tf_op jit(solution)/shard_map/ppermute | solution.py:300
  103.4 1.2 copy-start.1
  104.6 1.0 copy-start.3
  105.7 0.9 copy-start.6
  113.4 2.7 %copy-start.4 = (f32[8,32,512]{2,1,0:T(8,128)S(1)}, f32[8,32,512]{2,1,0:T(8,128)}, u32[]{:S(2)}) copy-start(f32[8,32,512]{2,1,0:T(8,128)} %copy-done.2) | copy-start | bytes 1572868
  113.4 2.7 %copy-start.7 = (f32[1,4,32,512]{3,2,1,0:T(8,128)S(1)}, f32[1,4,32,512]{3,2,1,0:T(8,128)}, u32[]{:S(2)}) copy-start(f32[1,4,32,512]{3,2,1,0:T(8,128)} %copy-done.5) | copy-start | bytes 786436
  119.5 3.8 %collective-permute-start.11 = (f32[8,32,512]{2,1,0:T(8,128)S(1)}, f32[8,32,512]{2,1,0:T(8,128)S(1)}, u32[]{:S(2)}, u32[]{:S(2)}) collective-permute-start(f32[8,32,512]{2,1,0:T(8,128)S(1)} %get-tuple-element.40), channel_id=1, source_target_pairs={{0,1},{1,0},{2,3},{3,2},{4,5},{5,4},{6,7},{7,6},{8,9},{9,8},{10,11... | collective-permute-start | bytes 1572872 | tf_op jit(solution)/shard_map/ppermute | solution.py:321

commit v10 on v8

--- a/solution.py
+++ b/solution.py
@@ -298,9 +298,8 @@
         else:
             got.append(tuple(moved))
             halves = moved
-        if step == 2:
-            *halves, w_x, w_c = lax.optimization_barrier((*halves, w_x, w_c))
-            got[-1] = tuple(halves)
+        if step == 1:
+            w_x, _ = lax.optimization_barrier((w_x, halves[1]))
     w_xc = lax.ppermute(w_x, "col", swap_core)
     ws = [own_w, w_x, w_c, w_xc]
 

time: 150 us -> 140 us (0.933)
  the two profiles are of different devices: /device:TPU:1 before, /device:TPU:2 now
where the time goes in v10:
time: 140 us; the launch traced here: 139 us
  blocking collectives  44.1 us (32%)
  starting transfers between devices  43.1 us (31%)
  waiting for transfers between devices  25.7 us (18%)
  Pallas kernels  20.2 us (14%)
  local copies, waits for them, and re-layouts  5.68 us (4%)
    all_to_all x1, blocking collectives, shards(): lax.all_to_all(acc, 'col', 0, 0, tiled=True, axis_index_groups=PEER_GROUPS)  44.1 us
    ppermute x8, waiting for transfers between devices, shards(): lax.ppermute(h, 'row', meets[n][(step + 1) % 2])  21 us
    ppermute x8, starting transfers between devices, shards(): lax.ppermute(h, 'row', meets[n][(step + 1) % 2])  20.7 us
    all_to_all x1, starting transfers between devices, shards(): lax.all_to_all(sent, ('row', 'col'), 0, 0, tiled=True, axis_index_groups=...  16.6 us
    pallas_call x4, Pallas kernels, multiply(): pl.pallas_call(functools.partial(multiply_kernel, acc is not None, blocks...  10.7 us
    pallas_call x1, Pallas kernels, arrange(): pl.pallas_call(functools.partial(arrange_kernel, pairs, wb), grid=(steps,...  7.23 us
    ppermute x1, waiting for transfers between devices, shards(): w_x = lax.ppermute(own_w, 'col', swap_x)  4.69 us
    unnamed x10, local copies, waits for them, and re-layouts  3.41 us
  transfers between devices with their start and end apart: 12, of which 6 were waited for; matrix products, arithmetic and copies ran while one was open for 1% of the time, Pallas kernels for 11%

profile of v10, /device:TPU:2, one launch (start us, length us, event | category | flops | bytes accessed | tf_op | source)
XLA Modules:
  0.0 139.2 jit_solution(778053074631446795)
XLA Ops:
  0.0 2.3 %shard_map.46 = f32[8,32,512]{2,1,0:T(8,128)} custom-call(f32[4,32,512]{2,1,0:T(8,128)} %bitcast.14), custom_call_target="tpu_custom_call" | custom-call | flops 201326592 | bytes 524288 | tf_op jit(solution)/shard_map/pallas_call | solution.py:148
  2.3 16.6 %all-to-all-start = ((f32[8,32,512]{2,1,0:T(8,128)}), f32[8,32,512]{2,1,0:T(8,128)S(1)}, u32[]{:S(2)}, u32[]{:S(2)}) async-start(f32[8,32,512]{2,1,0:T(8,128)} %shard_map.46), calls=%async_computation | async-start | bytes 1048576 | tf_op jit(solution)/shard_map/all_to_all | solution.py:277
  18.8 7.2 %shard_map.47.refs_4_.refs_8_.refs_12_.refs_16_.refs_3_.refs_7_.refs_11_.refs_15_ = f32[16,32,512]{2,1,0:T(8,128)} custom-call(f32[256,1024]{1,0:T(8,128)} %bitcast.15), custom_call_target="tpu_custom_call" | custom-call | flops 805306368 | bytes 2097152 | tf_op jit(solution)/shard_map/pallas_call | solution.py:195
  26.1 2.0 %collective-permute-start.8 = (f32[16,32,512]{2,1,0:T(8,128)}, f32[16,32,512]{2,1,0:T(8,128)S(1)}, u32[]{:S(2)}, u32[]{:S(2)}) collective-permute-start(f32[16,32,512]{2,1,0:T(8,128)} %shard_map.47.refs_4_.refs_8_.refs_12_.refs_16_.refs_3_.refs_7_.refs_11_.refs_15_), channel_id=1, source_target_pairs={{0,8},{1,9},{2,10},{3,11},{4,12},{5,13},{6,14},{7,15},{8,0},{9,1},... | collective-permute-start | bytes 3145736 | tf_op jit(solution)/shard_map/ppermute | solution.py:287
  28.1 0.0 all-to-all-done
  28.1 0.0 copy-start.1
  28.2 0.8 copy-done.1
  29.0 1.9 %collective-permute-start.4 = (f32[1,4,32,512]{3,2,1,0:T(8,128)S(1)}, f32[1,4,32,512]{3,2,1,0:T(8,128)S(1)}, u32[]{:S(2)}, u32[]{:S(2)}) collective-permute-start(f32[1,4,32,512]{3,2,1,0:T(8,128)S(1)} %get-tuple-element.7), channel_id=1, source_target_pairs={{0,448},{64,128},{128,64},{192,256},{256,192},{320,384},{384,320},... | collective-permute-start | bytes 786440 | tf_op jit(solution)/shard_map/ppermute | solution.py:294
  30.9 0.0 copy-start
  30.9 2.1 %collective-permute-start = (f32[1,4,32,512]{3,2,1,0:T(8,128)S(1)}, f32[1,4,32,512]{3,2,1,0:T(8,128)S(1)}, u32[]{:S(2)}, u32[]{:S(2)}) collective-permute-start(f32[1,4,32,512]{3,2,1,0:T(8,128)S(1)} %get-tuple-element.8), channel_id=1, source_target_pairs={{0,64},{64,0},{128,192},{192,128},{256,320},{320,256},{384,448},{4... | collective-permute-start | bytes 786440 | tf_op jit(solution)/shard_map/ppermute | solution.py:294
  32.9 7.4 %collective-permute-done.4.refs_3_ = f32[1,4,32,512]{3,2,1,0:T(8,128)S(1)} collective-permute-done((f32[1,4,32,512]{3,2,1,0:T(8,128)S(1)}, f32[1,4,32,512]{3,2,1,0:T(8,128)S(1)}, u32[]{:S(2)}, u32[]{:S(2)}) %collective-permute-start.4) | collective-permute-done | bytes 262176 | tf_op jit(solution)/shard_map/ppermute | solution.py:294
  40.4 1.9 %collective-permute-start.5 = (f32[2,4,32,512]{3,2,1,0:T(8,128)S(1)}, f32[2,4,32,512]{3,2,1,0:T(8,128)}, u32[]{:S(2)}, u32[]{:S(2)}) collective-permute-start(f32[2,4,32,512]{3,2,1,0:T(8,128)S(1)} %pad_maximum_fusion.1), channel_id=1, source_target_pairs={{0,64},{64,0},{128,192},{192,128},{256,320},{320,256},{384,448},{4... | collective-permute-start | bytes 1572872 | tf_op jit(solution)/shard_map/ppermute | solution.py:294
  42.3 0.0 collective-permute-done.refs_2_
  42.3 0.0 copy-start.3
  42.4 0.6 copy-done.3
  43.0 3.7 %collective-permute-start.1 = (f32[2,4,32,512]{3,2,1,0:T(8,128)S(1)}, f32[2,4,32,512]{3,2,1,0:T(8,128)}, u32[]{:S(2)}, u32[]{:S(2)}) collective-permute-start(f32[2,4,32,512]{3,2,1,0:T(8,128)S(1)} %pad_maximum_fusion), channel_id=1, source_target_pairs={{0,448},{64,128},{128,64},{192,256},{256,192},{320,384},{384,320},... | collective-permute-start | bytes 1572872 | tf_op jit(solution)/shard_map/ppermute | solution.py:294
  46.7 0.0 copy-done
  46.8 1.9 %collective-permute-start.9 = (f32[16,32,512]{2,1,0:T(8,128)S(1)}, f32[16,32,512]{2,1,0:T(8,128)S(1)}, u32[]{:S(2)}, u32[]{:S(2)}) collective-permute-start(f32[16,32,512]{2,1,0:T(8,128)S(1)} %copy-done), channel_id=1, source_target_pairs={{0,1},{1,0},{2,3},{3,2},{4,5},{5,4},{6,7},{7,6},{8,9},{9,8},{10,11... | collective-permute-start | bytes 3145736 | tf_op jit(solution)/shard_map/ppermute | solution.py:288
  48.7 4.7 %collective-permute-done.8.refs_5_.refs_9_.refs_13_.refs_17_.refs_4_.refs_8_.refs_12_.refs_16_ = f32[16,32,512]{2,1,0:T(8,128)S(1)} collective-permute-done((f32[16,32,512]{2,1,0:T(8,128)}, f32[16,32,512]{2,1,0:T(8,128)S(1)}, u32[]{:S(2)}, u32[]{:S(2)}) %collective-permute-start.8) | collective-permute-done | bytes 1048608 | tf_op jit(solution)/shard_map/ppermute | solution.py:287
  53.4 1.9 %collective-permute-start.10 = (f32[16,32,512]{2,1,0:T(8,128)S(1)}, f32[16,32,512]{2,1,0:T(8,128)}, u32[]{:S(2)}, u32[]{:S(2)}) collective-permute-start(f32[16,32,512]{2,1,0:T(8,128)S(1)} %collective-permute-done.8.refs_5_.refs_9_.refs_13_.refs_17_.refs_4_.refs_8_.refs_12_.refs_16_), channel_id=1, source_target_pairs={{0,1},{1,0},{2,3},{3,2},{4,5},{5,4},{6,7},{7,6},{8,9},{9,8},{10,11... | collective-permute-start | bytes 3145736 | tf_op jit(solution)/shard_map/ppermute | solution.py:303
  55.3 0.2 collective-permute-done.5.refs_2_
  55.5 2.5 %collective-permute-start.6 = (f32[2,4,32,512]{3,2,1,0:T(8,128)}, f32[2,4,32,512]{3,2,1,0:T(8,128)}, u32[]{:S(2)}, u32[]{:S(2)}) collective-permute-start(f32[2,4,32,512]{3,2,1,0:T(8,128)} %collective-permute-done.5.refs_2_), channel_id=1, source_target_pairs={{0,448},{64,128},{128,64},{192,256},{256,192},{320,384},{384,320},... | collective-permute-start | bytes 1572872 | tf_op jit(solution)/shard_map/ppermute | solution.py:294
  58.0 1.3 collective-permute-done.1.refs_1_
  59.3 3.0 %collective-permute-start.2 = (f32[2,4,32,512]{3,2,1,0:T(8,128)}, f32[2,4,32,512]{3,2,1,0:T(8,128)}, u32[]{:S(2)}, u32[]{:S(2)}) collective-permute-start(f32[2,4,32,512]{3,2,1,0:T(8,128)} %collective-permute-done.1.refs_1_), channel_id=1, source_target_pairs={{0,64},{64,0},{128,192},{192,128},{256,320},{320,256},{384,448},{4... | collective-permute-start | bytes 1572872 | tf_op jit(solution)/shard_map/ppermute | solution.py:294
  62.3 10.7 %collective-permute-done.6.refs_2_ = f32[2,4,32,512]{3,2,1,0:T(8,128)} collective-permute-done((f32[2,4,32,512]{3,2,1,0:T(8,128)}, f32[2,4,32,512]{3,2,1,0:T(8,128)}, u32[]{:S(2)}, u32[]{:S(2)}) %collective-permute-start.6) | collective-permute-done | bytes 524320 | tf_op jit(solution)/shard_map/ppermute | solution.py:294
  73.1 1.9 %collective-permute-start.7 = (f32[2,4,32,512]{3,2,1,0:T(8,128)}, f32[2,4,32,512]{3,2,1,0:T(8,128)S(1)}, u32[]{:S(2)}, u32[]{:S(2)}) collective-permute-start(f32[2,4,32,512]{3,2,1,0:T(8,128)} %collective-permute-done.6.refs_2_), channel_id=1, source_target_pairs={{0,64},{64,0},{128,192},{192,128},{256,320},{320,256},{384,448},{4... | collective-permute-start | bytes 1572872 | tf_op jit(solution)/shard_map/ppermute | solution.py:294
  75.0 0.0 collective-permute-done.2.refs_1_
  75.0 3.6 %collective-permute-start.3 = (f32[2,4,32,512]{3,2,1,0:T(8,128)}, f32[2,4,32,512]{3,2,1,0:T(8,128)S(1)}, u32[]{:S(2)}, u32[]{:S(2)}) collective-permute-start(f32[2,4,32,512]{3,2,1,0:T(8,128)} %collective-permute-done.2.refs_1_), channel_id=1, source_target_pairs={{0,448},{64,128},{128,64},{192,256},{256,192},{320,384},{384,320},... | collective-permute-start | bytes 1572872 | tf_op jit(solution)/shard_map/ppermute | solution.py:294
  78.6 0.7 dynamic-slice_bitcast_fusion.1
  79.3 0.7 dynamic-slice_bitcast_fusion
  80.0 0.1 pad_add_fusion.refs_0_
  80.1 0.0 collective-permute-done.9.refs_6_.refs_10_.refs_14_.refs_18_.refs_5_.refs_9_.refs_13_.refs_17_
  80.1 0.0 collective-permute-done.10.refs_7_.refs_11_.refs_15_.refs_19_.refs_6_.refs_10_.refs_14_.refs_18_
  80.1 0.0 copy-start.2
  80.1 1.0 copy-done.2
  81.2 0.0 copy-start.4
  81.2 0.9 copy-done.4
  82.1 2.5 %shard_map.48.refs_19_ = f32[16,32,512]{2,1,0:T(8,128)S(1)} custom-call(s32[20]{0:T(128)S(1)} %pad_add_fusion.refs_0_, f32[2,4,32,512]{3,2,1,0:T(8,128)S(1)} %bitcast.12, f32[1,4,32,512]{3,2,1,0:T(8,128)S(1)} %copy-done.4, f32[1,4,32,512]{3,2,1,0:T(8,128)S(1)} %collective-permute-done.4.refs_3_, f32[16,32,512]{2,1,0:T(8,128)S(1)} %copy-done, ...), custom_call_target="tpu_custom_call" | custom-call | flops 805306368 | bytes 2097152 | tf_op jit(solution)/shard_map/pallas_call | solution.py:254
  84.6 2.8 %shard_map.49.refs_19_ = f32[16,32,512]{2,1,0:T(8,128)S(1)} custom-call(s32[20]{0:T(128)S(1)} %pad_add_fusion.refs_0_, f32[2,4,32,512]{3,2,1,0:T(8,128)} %collective-permute-done.1.refs_1_, f32[2,4,32,512]{3,2,1,0:T(8,128)} %collective-permute-done.5.refs_2_, f32[16,32,512]{2,1,0:T(8,128)S(1)} %copy-done, ...), custom_call_target="tpu_custom_call" | custom-call | flops 805306368 | bytes 2097152 | tf_op jit(solution)/shard_map/pallas_call | solution.py:254
  87.5 2.8 %shard_map.50.refs_19_ = f32[16,32,512]{2,1,0:T(8,128)S(1)} custom-call(s32[20]{0:T(128)S(1)} %pad_add_fusion.refs_0_, f32[2,4,32,512]{3,2,1,0:T(8,128)} %collective-permute-done.2.refs_1_, f32[2,4,32,512]{3,2,1,0:T(8,128)} %collective-permute-done.6.refs_2_, f32[16,32,512]{2,1,0:T(8,128)S(1)} %copy-done, ...), custom_call_target="tpu_custom_call" | custom-call | flops 805306368 | bytes 2097152 | tf_op jit(solution)/shard_map/pallas_call | solution.py:254
  90.3 0.0 collective-permute-done.7.refs_2_
  90.3 1.4 collective-permute-done.3.refs_1_
  91.7 2.5 %shard_map.51 = f32[16,32,512]{2,1,0:T(8,128)S(1)} custom-call(s32[20]{0:T(128)S(1)} %pad_add_fusion.refs_0_, f32[2,4,32,512]{3,2,1,0:T(8,128)S(1)} %collective-permute-done.3.refs_1_, f32[2,4,32,512]{3,2,1,0:T(8,128)S(1)} %collective-permute-done.7.refs_2_, f32[16,32,512]{2,1,0:T(8,128)S(1)} %copy-done, ...), custom_call_target="tpu_custom_call" | custom-call | flops 805306368 | bytes 2097152 | tf_op jit(solution)/shard_map/pallas_call | solution.py:254
  94.2 44.1 %all_to_all.10 = f32[16,32,512]{2,1,0:T(8,128)S(1)} all-to-all(f32[16,32,512]{2,1,0:T(8,128)S(1)} %shard_map.51), channel_id=1, replica_groups={{0,2,4,6,16,18,20,22,32,34,36,38,48,50,52,54},{1,3,5,7,17,19,21,23,33,3..., dimensions={0} | all-to-all | bytes 2097152 | tf_op jit(solution)/shard_map/all_to_all | solution.py:310
  138.3 0.1 reduce_sum.9
  138.4 0.1 reshape.17
  138.5 0.7 copy.5
  (3 shorter events, 0.1 us)
Async XLA Ops:
  2.3 25.9 %all-to-all-start = ((f32[8,32,512]{2,1,0:T(8,128)}), f32[8,32,512]{2,1,0:T(8,128)S(1)}, u32[]{:S(2)}, u32[]{:S(2)}) async-start(f32[8,32,512]{2,1,0:T(8,128)} %shard_map.46), calls=%async_computation | async-start | bytes 1048576 | tf_op jit(solution)/shard_map/all_to_all | solution.py:277
  26.1 27.3 %collective-permute-start.8 = (f32[16,32,512]{2,1,0:T(8,128)}, f32[16,32,512]{2,1,0:T(8,128)S(1)}, u32[]{:S(2)}, u32[]{:S(2)}) collective-permute-start(f32[16,32,512]{2,1,0:T(8,128)} %shard_map.47.refs_4_.refs_8_.refs_12_.refs_16_.refs_3_.refs_7_.refs_11_.refs_15_), channel_id=1, source_target_pairs={{0,8},{1,9},{2,10},{3,11},{4,12},{5,13},{6,14},{7,15},{8,0},{9,1},... | collective-permute-start | bytes 3145736 | tf_op jit(solution)/shard_map/ppermute | solution.py:287
  28.1 0.8 copy-start.1
  29.0 11.4 %collective-permute-start.4 = (f32[1,4,32,512]{3,2,1,0:T(8,128)S(1)}, f32[1,4,32,512]{3,2,1,0:T(8,128)S(1)}, u32[]{:S(2)}, u32[]{:S(2)}) collective-permute-start(f32[1,4,32,512]{3,2,1,0:T(8,128)S(1)} %get-tuple-element.7), channel_id=1, source_target_pairs={{0,448},{64,128},{128,64},{192,256},{256,192},{320,384},{384,320},... | collective-permute-start | bytes 786440 | tf_op jit(solution)/shard_map/ppermute | solution.py:294
  30.9 15.9 %copy-start = (f32[16,32,512]{2,1,0:T(8,128)S(1)}, f32[16,32,512]{2,1,0:T(8,128)}, u32[]{:S(2)}) copy-start(f32[16,32,512]{2,1,0:T(8,128)} %shard_map.47.refs_4_.refs_8_.refs_12_.refs_16_.refs_3_.refs_7_.refs_11_.refs_15_) | copy-start | bytes 3145732
  30.9 11.4 %collective-permute-start = (f32[1,4,32,512]{3,2,1,0:T(8,128)S(1)}, f32[1,4,32,512]{3,2,1,0:T(8,128)S(1)}, u32[]{:S(2)}, u32[]{:S(2)}) collective-permute-start(f32[1,4,32,512]{3,2,1,0:T(8,128)S(1)} %get-tuple-element.8), channel_id=1, source_target_pairs={{0,64},{64,0},{128,192},{192,128},{256,320},{320,256},{384,448},{4... | collective-permute-start | bytes 786440 | tf_op jit(solution)/shard_map/ppermute | solution.py:294
  40.4 15.1 %collective-permute-start.5 = (f32[2,4,32,512]{3,2,1,0:T(8,128)S(1)}, f32[2,4,32,512]{3,2,1,0:T(8,128)}, u32[]{:S(2)}, u32[]{:S(2)}) collective-permute-start(f32[2,4,32,512]{3,2,1,0:T(8,128)S(1)} %pad_maximum_fusion.1), channel_id=1, source_target_pairs={{0,64},{64,0},{128,192},{192,128},{256,320},{320,256},{384,448},{4... | collective-permute-start | bytes 1572872 | tf_op jit(solution)/shard_map/ppermute | solution.py:294
  42.3 0.7 copy-start.3
  43.0 16.3 %collective-permute-start.1 = (f32[2,4,32,512]{3,2,1,0:T(8,128)S(1)}, f32[2,4,32,512]{3,2,1,0:T(8,128)}, u32[]{:S(2)}, u32[]{:S(2)}) collective-permute-start(f32[2,4,32,512]{3,2,1,0:T(8,128)S(1)} %pad_maximum_fusion), channel_id=1, source_target_pairs={{0,448},{64,128},{128,64},{192,256},{256,192},{320,384},{384,320},... | collective-permute-start | bytes 1572872 | tf_op jit(solution)/shard_map/ppermute | solution.py:294
  46.8 33.3 %collective-permute-start.9 = (f32[16,32,512]{2,1,0:T(8,128)S(1)}, f32[16,32,512]{2,1,0:T(8,128)S(1)}, u32[]{:S(2)}, u32[]{:S(2)}) collective-permute-start(f32[16,32,512]{2,1,0:T(8,128)S(1)} %copy-done), channel_id=1, source_target_pairs={{0,1},{1,0},{2,3},{3,2},{4,5},{5,4},{6,7},{7,6},{8,9},{9,8},{10,11... | collective-permute-start | bytes 3145736 | tf_op jit(solution)/shard_map/ppermute | solution.py:288
  53.4 26.7 %collective-permute-start.10 = (f32[16,32,512]{2,1,0:T(8,128)S(1)}, f32[16,32,512]{2,1,0:T(8,128)}, u32[]{:S(2)}, u32[]{:S(2)}) collective-permute-start(f32[16,32,512]{2,1,0:T(8,128)S(1)} %collective-permute-done.8.refs_5_.refs_9_.refs_13_.refs_17_.refs_4_.refs_8_.refs_12_.refs_16_), channel_id=1, source_target_pairs={{0,1},{1,0},{2,3},{3,2},{4,5},{5,4},{6,7},{7,6},{8,9},{9,8},{10,11... | collective-permute-start | bytes 3145736 | tf_op jit(solution)/shard_map/ppermute | solution.py:303
  55.5 17.6 %collective-permute-start.6 = (f32[2,4,32,512]{3,2,1,0:T(8,128)}, f32[2,4,32,512]{3,2,1,0:T(8,128)}, u32[]{:S(2)}, u32[]{:S(2)}) collective-permute-start(f32[2,4,32,512]{3,2,1,0:T(8,128)} %collective-permute-done.5.refs_2_), channel_id=1, source_target_pairs={{0,448},{64,128},{128,64},{192,256},{256,192},{320,384},{384,320},... | collective-permute-start | bytes 1572872 | tf_op jit(solution)/shard_map/ppermute | solution.py:294
  59.3 15.7 %collective-permute-start.2 = (f32[2,4,32,512]{3,2,1,0:T(8,128)}, f32[2,4,32,512]{3,2,1,0:T(8,128)}, u32[]{:S(2)}, u32[]{:S(2)}) collective-permute-start(f32[2,4,32,512]{3,2,1,0:T(8,128)} %collective-permute-done.1.refs_1_), channel_id=1, source_target_pairs={{0,64},{64,0},{128,192},{192,128},{256,320},{320,256},{384,448},{4... | collective-permute-start | bytes 1572872 | tf_op jit(solution)/shard_map/ppermute | solution.py:294
  73.1 17.2 %collective-permute-start.7 = (f32[2,4,32,512]{3,2,1,0:T(8,128)}, f32[2,4,32,512]{3,2,1,0:T(8,128)S(1)}, u32[]{:S(2)}, u32[]{:S(2)}) collective-permute-start(f32[2,4,32,512]{3,2,1,0:T(8,128)} %collective-permute-done.6.refs_2_), channel_id=1, source_target_pairs={{0,64},{64,0},{128,192},{192,128},{256,320},{320,256},{384,448},{4... | collective-permute-start | bytes 1572872 | tf_op jit(solution)/shard_map/ppermute | solution.py:294
  75.0 16.7 %collective-permute-start.3 = (f32[2,4,32,512]{3,2,1,0:T(8,128)}, f32[2,4,32,512]{3,2,1,0:T(8,128)S(1)}, u32[]{:S(2)}, u32[]{:S(2)}) collective-permute-start(f32[2,4,32,512]{3,2,1,0:T(8,128)} %collective-permute-done.2.refs_1_), channel_id=1, source_target_pairs={{0,448},{64,128},{128,64},{192,256},{256,192},{320,384},{384,320},... | collective-permute-start | bytes 1572872 | tf_op jit(solution)/shard_map/ppermute | solution.py:294
  80.1 1.0 copy-start.2
  81.2 0.9 copy-start.4

commit v11 on v8

--- a/solution.py
+++ b/solution.py
@@ -285,7 +285,6 @@
     swap_core = col_perm(lambda x, zh, c: (x, zh, 1 - c))
     swap_x = col_perm(lambda x, zh, c: (x ^ 1, zh, c))
     w_x = lax.ppermute(own_w, "col", swap_x)
-    w_c = lax.ppermute(own_w, "col", swap_core)
 
     meets = [[row_perm(lambda z, q, f=f: (z, f(q))) for f in pair] for pair in MEETS]
     halves = [own[:1], own[1:]]
@@ -298,14 +297,20 @@
         else:
             got.append(tuple(moved))
             halves = moved
+        if step == 1:
+            *halves, held_w = lax.optimization_barrier((*halves, own_w))
+            w_c = lax.ppermute(held_w, "col", swap_core)
         if step == 2:
-            *halves, w_x, w_c = lax.optimization_barrier((*halves, w_x, w_c))
+            *halves, w_x = lax.optimization_barrier((*halves, w_x))
             got[-1] = tuple(halves)
-    w_xc = lax.ppermute(w_x, "col", swap_core)
-    ws = [own_w, w_x, w_c, w_xc]
-
-    acc = None
-    for at, ts in enumerate(got):
+            w_xc = lax.ppermute(w_x, "col", swap_core)
+            ws = [own_w, w_x, w_c, w_xc]
+        if step == 3:
+            acc = multiply(scalars, 0, got[0], ws, None, blocks)
+            *halves, acc = lax.optimization_barrier((*halves, acc))
+            got[-1] = tuple(halves)
+
+    for at, ts in enumerate(got[1:], 1):
         acc = multiply(scalars, at, ts, ws, acc, blocks)
 
     arrived = lax.all_to_all(acc, "col", 0, 0, tiled=True, axis_index_groups=PEER_GROUPS)

time: 150 us -> 151 us (level)
  the two profiles are of different devices: /device:TPU:1 before, /device:TPU:12 now
where the time goes in v11:
time: 151 us; the launch traced here: 150 us
  blocking collectives  52.9 us (35%)
  starting transfers between devices  37.7 us (25%)
  waiting for transfers between devices  32.9 us (22%)
  Pallas kernels  20.2 us (13%)
  local copies, waits for them, and re-layouts  5.69 us (4%)
    all_to_all x1, blocking collectives, shards(): lax.all_to_all(acc, 'col', 0, 0, tiled=True, axis_index_groups=PEER_GROUPS)  52.9 us
    ppermute x8, waiting for transfers between devices, shards(): lax.ppermute(h, 'row', meets[n][(step + 1) % 2])  32.9 us
    ppermute x8, starting transfers between devices, shards(): lax.ppermute(h, 'row', meets[n][(step + 1) % 2])  25.3 us
    pallas_call x4, Pallas kernels, multiply(): pl.pallas_call(functools.partial(multiply_kernel, acc is not None, blocks...  10.7 us
    pallas_call x1, Pallas kernels, arrange(): pl.pallas_call(functools.partial(arrange_kernel, pairs, wb), grid=(steps,...  7.24 us
    all_to_all x1, starting transfers between devices, shards(): lax.all_to_all(sent, ('row', 'col'), 0, 0, tiled=True, axis_index_groups=...  4.59 us
    ppermute x1, starting transfers between devices, shards(): w_x = lax.ppermute(own_w, 'col', swap_x)  3.92 us
    unnamed x10, local copies, waits for them, and re-layouts  3.42 us
  transfers between devices with their start and end apart: 12, of which 8 were waited for; matrix products, arithmetic and copies ran while one was open for 1% of the time, Pallas kernels for 10%

profile of v11, /device:TPU:12, one launch (start us, length us, event | category | flops | bytes accessed | tf_op | source)
XLA Modules:
  0.0 149.8 jit_solution(18432111817978042659)
XLA Ops:
  0.0 2.3 %shard_map.46 = f32[8,32,512]{2,1,0:T(8,128)} custom-call(f32[4,32,512]{2,1,0:T(8,128)} %bitcast.14), custom_call_target="tpu_custom_call" | custom-call | flops 201326592 | bytes 524288 | tf_op jit(solution)/shard_map/pallas_call | solution.py:148
  2.3 4.6 %all-to-all-start = ((f32[8,32,512]{2,1,0:T(8,128)}), f32[8,32,512]{2,1,0:T(8,128)S(1)}, u32[]{:S(2)}, u32[]{:S(2)}) async-start(f32[8,32,512]{2,1,0:T(8,128)} %shard_map.46), calls=%async_computation | async-start | bytes 1048576 | tf_op jit(solution)/shard_map/all_to_all | solution.py:277
  6.8 7.2 %shard_map.47.refs_4_.refs_8_.refs_12_.refs_16_.refs_3_.refs_7_.refs_11_.refs_15_ = f32[16,32,512]{2,1,0:T(8,128)} custom-call(f32[256,1024]{1,0:T(8,128)} %bitcast.15), custom_call_target="tpu_custom_call" | custom-call | flops 805306368 | bytes 2097152 | tf_op jit(solution)/shard_map/pallas_call | solution.py:195
  14.1 3.9 %collective-permute-start.4 = (f32[16,32,512]{2,1,0:T(8,128)}, f32[16,32,512]{2,1,0:T(8,128)S(1)}, u32[]{:S(2)}, u32[]{:S(2)}) collective-permute-start(f32[16,32,512]{2,1,0:T(8,128)} %shard_map.47.refs_4_.refs_8_.refs_12_.refs_16_.refs_3_.refs_7_.refs_11_.refs_15_), channel_id=1, source_target_pairs={{0,8},{1,9},{2,10},{3,11},{4,12},{5,13},{6,14},{7,15},{8,0},{9,1},... | collective-permute-start | bytes 3145736 | tf_op jit(solution)/shard_map/ppermute | solution.py:287
  18.0 0.0 all-to-all-done
  18.0 0.0 copy-start.1
  18.1 0.8 copy-done.1
  18.8 6.2 %collective-permute-start.1 = (f32[1,4,32,512]{3,2,1,0:T(8,128)S(1)}, f32[1,4,32,512]{3,2,1,0:T(8,128)S(1)}, u32[]{:S(2)}, u32[]{:S(2)}) collective-permute-start(f32[1,4,32,512]{3,2,1,0:T(8,128)S(1)} %get-tuple-element.23), channel_id=1, source_target_pairs={{0,448},{64,128},{128,64},{192,256},{256,192},{320,384},{384,320},... | collective-permute-start | bytes 786440 | tf_op jit(solution)/shard_map/ppermute | solution.py:293
  25.0 0.0 copy-start
  25.0 2.1 %collective-permute-start = (f32[1,4,32,512]{3,2,1,0:T(8,128)S(1)}, f32[1,4,32,512]{3,2,1,0:T(8,128)S(1)}, u32[]{:S(2)}, u32[]{:S(2)}) collective-permute-start(f32[1,4,32,512]{3,2,1,0:T(8,128)S(1)} %get-tuple-element.24), channel_id=1, source_target_pairs={{0,64},{64,0},{128,192},{192,128},{256,320},{320,256},{384,448},{4... | collective-permute-start | bytes 786440 | tf_op jit(solution)/shard_map/ppermute | solution.py:293
  27.1 4.3 %collective-permute-done.1.refs_3_ = f32[1,4,32,512]{3,2,1,0:T(8,128)S(1)} collective-permute-done((f32[1,4,32,512]{3,2,1,0:T(8,128)S(1)}, f32[1,4,32,512]{3,2,1,0:T(8,128)S(1)}, u32[]{:S(2)}, u32[]{:S(2)}) %collective-permute-start.1) | collective-permute-done | bytes 262176 | tf_op jit(solution)/shard_map/ppermute | solution.py:293
  31.4 3.5 %collective-permute-done.refs_2_ = f32[1,4,32,512]{3,2,1,0:T(8,128)S(1)} collective-permute-done((f32[1,4,32,512]{3,2,1,0:T(8,128)S(1)}, f32[1,4,32,512]{3,2,1,0:T(8,128)S(1)}, u32[]{:S(2)}, u32[]{:S(2)}) %collective-permute-start) | collective-permute-done | bytes 262176 | tf_op jit(solution)/shard_map/ppermute | solution.py:293
  34.8 0.0 copy-start.3
  34.9 0.7 copy-done.3
  35.5 2.6 %collective-permute-start.2 = (f32[2,4,32,512]{3,2,1,0:T(8,128)S(1)}, f32[2,4,32,512]{3,2,1,0:T(8,128)}, u32[]{:S(2)}, u32[]{:S(2)}) collective-permute-start(f32[2,4,32,512]{3,2,1,0:T(8,128)S(1)} %pad_maximum_fusion), channel_id=1, source_target_pairs={{0,448},{64,128},{128,64},{192,256},{256,192},{320,384},{384,320},... | collective-permute-start | bytes 1572872 | tf_op jit(solution)/shard_map/ppermute | solution.py:293
  38.2 3.1 %collective-permute-start.3 = (f32[2,4,32,512]{3,2,1,0:T(8,128)S(1)}, f32[2,4,32,512]{3,2,1,0:T(8,128)}, u32[]{:S(2)}, u32[]{:S(2)}) collective-permute-start(f32[2,4,32,512]{3,2,1,0:T(8,128)S(1)} %pad_maximum_fusion.1), channel_id=1, source_target_pairs={{0,64},{64,0},{128,192},{192,128},{256,320},{320,256},{384,448},{4... | collective-permute-start | bytes 1572872 | tf_op jit(solution)/shard_map/ppermute | solution.py:293
  41.3 0.0 copy-done
  41.3 1.9 %collective-permute-start.7 = (f32[16,32,512]{2,1,0:T(8,128)S(1)}, f32[16,32,512]{2,1,0:T(8,128)S(1)}, u32[]{:S(2)}, u32[]{:S(2)}) collective-permute-start(f32[16,32,512]{2,1,0:T(8,128)S(1)} %copy-done), channel_id=1, source_target_pairs={{0,1},{1,0},{2,3},{3,2},{4,5},{5,4},{6,7},{7,6},{8,9},{9,8},{10,11... | collective-permute-start | bytes 3145736 | tf_op jit(solution)/shard_map/ppermute | solution.py:302
  43.3 0.0 collective-permute-done.4.refs_5_.refs_9_.refs_13_.refs_17_.refs_4_.refs_8_.refs_12_.refs_16_
  43.3 8.0 %collective-permute-done.2.refs_1_ = f32[2,4,32,512]{3,2,1,0:T(8,128)} collective-permute-done((f32[2,4,32,512]{3,2,1,0:T(8,128)S(1)}, f32[2,4,32,512]{3,2,1,0:T(8,128)}, u32[]{:S(2)}, u32[]{:S(2)}) %collective-permute-start.2) | collective-permute-done | bytes 524320 | tf_op jit(solution)/shard_map/ppermute | solution.py:293
  51.2 1.5 collective-permute-done.3.refs_2_
  52.7 1.9 %collective-permute-start.8 = (f32[16,32,512]{2,1,0:T(8,128)S(1)}, f32[16,32,512]{2,1,0:T(8,128)}, u32[]{:S(2)}, u32[]{:S(2)}) collective-permute-start(f32[16,32,512]{2,1,0:T(8,128)S(1)} %collective-permute-done.4.refs_5_.refs_9_.refs_13_.refs_17_.refs_4_.refs_8_.refs_12_.refs_16_), channel_id=1, source_target_pairs={{0,1},{1,0},{2,3},{3,2},{4,5},{5,4},{6,7},{7,6},{8,9},{9,8},{10,11... | collective-permute-start | bytes 3145736 | tf_op jit(solution)/shard_map/ppermute | solution.py:306
  54.7 3.1 %collective-permute-start.5 = (f32[2,4,32,512]{3,2,1,0:T(8,128)}, f32[2,4,32,512]{3,2,1,0:T(8,128)}, u32[]{:S(2)}, u32[]{:S(2)}) collective-permute-start(f32[2,4,32,512]{3,2,1,0:T(8,128)} %collective-permute-done.2.refs_1_), channel_id=1, source_target_pairs={{0,64},{64,0},{128,192},{192,128},{256,320},{320,256},{384,448},{4... | collective-permute-start | bytes 1572872 | tf_op jit(solution)/shard_map/ppermute | solution.py:293
  57.8 3.2 %collective-permute-start.6 = (f32[2,4,32,512]{3,2,1,0:T(8,128)}, f32[2,4,32,512]{3,2,1,0:T(8,128)}, u32[]{:S(2)}, u32[]{:S(2)}) collective-permute-start(f32[2,4,32,512]{3,2,1,0:T(8,128)} %collective-permute-done.3.refs_2_), channel_id=1, source_target_pairs={{0,448},{64,128},{128,64},{192,256},{256,192},{320,384},{384,320},... | collective-permute-start | bytes 1572872 | tf_op jit(solution)/shard_map/ppermute | solution.py:293
  61.0 0.7 dynamic-slice_bitcast_fusion
  61.7 0.7 dynamic-slice_bitcast_fusion.1
  62.4 0.1 pad_add_fusion.refs_0_
  62.4 0.0 collective-permute-done.7.refs_6_.refs_10_.refs_14_.refs_18_.refs_5_.refs_9_.refs_13_.refs_17_
  62.4 0.0 collective-permute-done.8.refs_7_.refs_11_.refs_15_.refs_19_.refs_6_.refs_10_.refs_14_.refs_18_
  62.4 0.0 copy-start.2
  62.4 1.0 copy-done.2
  63.5 0.0 copy-start.4
  63.5 0.9 copy-done.4
  64.4 2.5 %shard_map.48.refs_19_ = f32[16,32,512]{2,1,0:T(8,128)S(1)} custom-call(s32[20]{0:T(128)S(1)} %pad_add_fusion.refs_0_, f32[2,4,32,512]{3,2,1,0:T(8,128)S(1)} %bitcast.12, f32[1,4,32,512]{3,2,1,0:T(8,128)S(1)} %copy-done.4, f32[1,4,32,512]{3,2,1,0:T(8,128)S(1)} %collective-permute-done.1.refs_3_, f32[16,32,512]{2,1,0:T(8,128)S(1)} %copy-done, ...), custom_call_target="tpu_custom_call" | custom-call | flops 805306368 | bytes 2097152 | tf_op jit(solution)/shard_map/pallas_call | solution.py:254
  67.0 4.2 %collective-permute-done.5.refs_1_ = f32[2,4,32,512]{3,2,1,0:T(8,128)} collective-permute-done((f32[2,4,32,512]{3,2,1,0:T(8,128)}, f32[2,4,32,512]{3,2,1,0:T(8,128)}, u32[]{:S(2)}, u32[]{:S(2)}) %collective-permute-start.5) | collective-permute-done | bytes 524320 | tf_op jit(solution)/shard_map/ppermute | solution.py:293
  71.2 4.1 %collective-permute-done.6.refs_2_ = f32[2,4,32,512]{3,2,1,0:T(8,128)} collective-permute-done((f32[2,4,32,512]{3,2,1,0:T(8,128)}, f32[2,4,32,512]{3,2,1,0:T(8,128)}, u32[]{:S(2)}, u32[]{:S(2)}) %collective-permute-start.6) | collective-permute-done | bytes 524320 | tf_op jit(solution)/shard_map/ppermute | solution.py:293
  75.3 3.1 %collective-permute-start.9 = (f32[2,4,32,512]{3,2,1,0:T(8,128)}, f32[2,4,32,512]{3,2,1,0:T(8,128)S(1)}, u32[]{:S(2)}, u32[]{:S(2)}) collective-permute-start(f32[2,4,32,512]{3,2,1,0:T(8,128)} %collective-permute-done.5.refs_1_), channel_id=1, source_target_pairs={{0,448},{64,128},{128,64},{192,256},{256,192},{320,384},{384,320},... | collective-permute-start | bytes 1572872 | tf_op jit(solution)/shard_map/ppermute | solution.py:293
  78.4 1.9 %collective-permute-start.10 = (f32[2,4,32,512]{3,2,1,0:T(8,128)}, f32[2,4,32,512]{3,2,1,0:T(8,128)S(1)}, u32[]{:S(2)}, u32[]{:S(2)}) collective-permute-start(f32[2,4,32,512]{3,2,1,0:T(8,128)} %collective-permute-done.6.refs_2_), channel_id=1, source_target_pairs={{0,64},{64,0},{128,192},{192,128},{256,320},{320,256},{384,448},{4... | collective-permute-start | bytes 1572872 | tf_op jit(solution)/shard_map/ppermute | solution.py:293
  80.3 2.8 %shard_map.49.refs_19_ = f32[16,32,512]{2,1,0:T(8,128)S(1)} custom-call(s32[20]{0:T(128)S(1)} %pad_add_fusion.refs_0_, f32[2,4,32,512]{3,2,1,0:T(8,128)} %collective-permute-done.2.refs_1_, f32[2,4,32,512]{3,2,1,0:T(8,128)} %collective-permute-done.3.refs_2_, f32[16,32,512]{2,1,0:T(8,128)S(1)} %copy-done, ...), custom_call_target="tpu_custom_call" | custom-call | flops 805306368 | bytes 2097152 | tf_op jit(solution)/shard_map/pallas_call | solution.py:254
  83.2 2.8 %shard_map.50.refs_19_ = f32[16,32,512]{2,1,0:T(8,128)S(1)} custom-call(s32[20]{0:T(128)S(1)} %pad_add_fusion.refs_0_, f32[2,4,32,512]{3,2,1,0:T(8,128)} %collective-permute-done.5.refs_1_, f32[2,4,32,512]{3,2,1,0:T(8,128)} %collective-permute-done.6.refs_2_, f32[16,32,512]{2,1,0:T(8,128)S(1)} %copy-done, ...), custom_call_target="tpu_custom_call" | custom-call | flops 805306368 | bytes 2097152 | tf_op jit(solution)/shard_map/pallas_call | solution.py:254
  86.0 5.8 %collective-permute-done.9.refs_1_ = f32[2,4,32,512]{3,2,1,0:T(8,128)S(1)} collective-permute-done((f32[2,4,32,512]{3,2,1,0:T(8,128)}, f32[2,4,32,512]{3,2,1,0:T(8,128)S(1)}, u32[]{:S(2)}, u32[]{:S(2)}) %collective-permute-start.9) | collective-permute-done | bytes 524320 | tf_op jit(solution)/shard_map/ppermute | solution.py:293
  91.8 1.7 %collective-permute-done.10.refs_2_ = f32[2,4,32,512]{3,2,1,0:T(8,128)S(1)} collective-permute-done((f32[2,4,32,512]{3,2,1,0:T(8,128)}, f32[2,4,32,512]{3,2,1,0:T(8,128)S(1)}, u32[]{:S(2)}, u32[]{:S(2)}) %collective-permute-start.10) | collective-permute-done | bytes 524320 | tf_op jit(solution)/shard_map/ppermute | solution.py:293
  93.5 2.5 %shard_map.51 = f32[16,32,512]{2,1,0:T(8,128)S(1)} custom-call(s32[20]{0:T(128)S(1)} %pad_add_fusion.refs_0_, f32[2,4,32,512]{3,2,1,0:T(8,128)S(1)} %collective-permute-done.9.refs_1_, f32[2,4,32,512]{3,2,1,0:T(8,128)S(1)} %collective-permute-done.10.refs_2_, f32[16,32,512]{2,1,0:T(8,128)S(1)} %copy-done, ...), custom_call_target="tpu_custom_call" | custom-call | flops 805306368 | bytes 2097152 | tf_op jit(solution)/shard_map/pallas_call | solution.py:254
  96.0 52.9 %all_to_all.10 = f32[16,32,512]{2,1,0:T(8,128)S(1)} all-to-all(f32[16,32,512]{2,1,0:T(8,128)S(1)} %shard_map.51), channel_id=1, replica_groups={{0,2,4,6,16,18,20,22,32,34,36,38,48,50,52,54},{1,3,5,7,17,19,21,23,33,3..., dimensions={0} | all-to-all | bytes 2097152 | tf_op jit(solution)/shard_map/all_to_all | solution.py:316
  148.9 0.1 reduce_sum.9
  148.9 0.1 reshape.17
  149.0 0.7 copy.5
  (3 shorter events, 0.1 us)
Async XLA Ops:
  2.3 15.8 %all-to-all-start = ((f32[8,32,512]{2,1,0:T(8,128)}), f32[8,32,512]{2,1,0:T(8,128)S(1)}, u32[]{:S(2)}, u32[]{:S(2)}) async-start(f32[8,32,512]{2,1,0:T(8,128)} %shard_map.46), calls=%async_computation | async-start | bytes 1048576 | tf_op jit(solution)/shard_map/all_to_all | solution.py:277
  14.1 29.2 %collective-permute-start.4 = (f32[16,32,512]{2,1,0:T(8,128)}, f32[16,32,512]{2,1,0:T(8,128)S(1)}, u32[]{:S(2)}, u32[]{:S(2)}) collective-permute-start(f32[16,32,512]{2,1,0:T(8,128)} %shard_map.47.refs_4_.refs_8_.refs_12_.refs_16_.refs_3_.refs_7_.refs_11_.refs_15_), channel_id=1, source_target_pairs={{0,8},{1,9},{2,10},{3,11},{4,12},{5,13},{6,14},{7,15},{8,0},{9,1},... | collective-permute-start | bytes 3145736 | tf_op jit(solution)/shard_map/ppermute | solution.py:287
  18.0 0.8 copy-start.1
  18.8 12.5 %collective-permute-start.1 = (f32[1,4,32,512]{3,2,1,0:T(8,128)S(1)}, f32[1,4,32,512]{3,2,1,0:T(8,128)S(1)}, u32[]{:S(2)}, u32[]{:S(2)}) collective-permute-start(f32[1,4,32,512]{3,2,1,0:T(8,128)S(1)} %get-tuple-element.23), channel_id=1, source_target_pairs={{0,448},{64,128},{128,64},{192,256},{256,192},{320,384},{384,320},... | collective-permute-start | bytes 786440 | tf_op jit(solution)/shard_map/ppermute | solution.py:293
  25.0 16.3 %copy-start = (f32[16,32,512]{2,1,0:T(8,128)S(1)}, f32[16,32,512]{2,1,0:T(8,128)}, u32[]{:S(2)}) copy-start(f32[16,32,512]{2,1,0:T(8,128)} %shard_map.47.refs_4_.refs_8_.refs_12_.refs_16_.refs_3_.refs_7_.refs_11_.refs_15_) | copy-start | bytes 3145732
  25.0 9.8 %collective-permute-start = (f32[1,4,32,512]{3,2,1,0:T(8,128)S(1)}, f32[1,4,32,512]{3,2,1,0:T(8,128)S(1)}, u32[]{:S(2)}, u32[]{:S(2)}) collective-permute-start(f32[1,4,32,512]{3,2,1,0:T(8,128)S(1)} %get-tuple-element.24), channel_id=1, source_target_pairs={{0,64},{64,0},{128,192},{192,128},{256,320},{320,256},{384,448},{4... | collective-permute-start | bytes 786440 | tf_op jit(solution)/shard_map/ppermute | solution.py:293
  34.8 0.7 copy-start.3
  35.5 15.7 %collective-permute-start.2 = (f32[2,4,32,512]{3,2,1,0:T(8,128)S(1)}, f32[2,4,32,512]{3,2,1,0:T(8,128)}, u32[]{:S(2)}, u32[]{:S(2)}) collective-permute-start(f32[2,4,32,512]{3,2,1,0:T(8,128)S(1)} %pad_maximum_fusion), channel_id=1, source_target_pairs={{0,448},{64,128},{128,64},{192,256},{256,192},{320,384},{384,320},... | collective-permute-start | bytes 1572872 | tf_op jit(solution)/shard_map/ppermute | solution.py:293
  38.2 14.6 %collective-permute-start.3 = (f32[2,4,32,512]{3,2,1,0:T(8,128)S(1)}, f32[2,4,32,512]{3,2,1,0:T(8,128)}, u32[]{:S(2)}, u32[]{:S(2)}) collective-permute-start(f32[2,4,32,512]{3,2,1,0:T(8,128)S(1)} %pad_maximum_fusion.1), channel_id=1, source_target_pairs={{0,64},{64,0},{128,192},{192,128},{256,320},{320,256},{384,448},{4... | collective-permute-start | bytes 1572872 | tf_op jit(solution)/shard_map/ppermute | solution.py:293
  41.3 21.1 %collective-permute-start.7 = (f32[16,32,512]{2,1,0:T(8,128)S(1)}, f32[16,32,512]{2,1,0:T(8,128)S(1)}, u32[]{:S(2)}, u32[]{:S(2)}) collective-permute-start(f32[16,32,512]{2,1,0:T(8,128)S(1)} %copy-done), channel_id=1, source_target_pairs={{0,1},{1,0},{2,3},{3,2},{4,5},{5,4},{6,7},{7,6},{8,9},{9,8},{10,11... | collective-permute-start | bytes 3145736 | tf_op jit(solution)/shard_map/ppermute | solution.py:302
  52.7 9.7 %collective-permute-start.8 = (f32[16,32,512]{2,1,0:T(8,128)S(1)}, f32[16,32,512]{2,1,0:T(8,128)}, u32[]{:S(2)}, u32[]{:S(2)}) collective-permute-start(f32[16,32,512]{2,1,0:T(8,128)S(1)} %collective-permute-done.4.refs_5_.refs_9_.refs_13_.refs_17_.refs_4_.refs_8_.refs_12_.refs_16_), channel_id=1, source_target_pairs={{0,1},{1,0},{2,3},{3,2},{4,5},{5,4},{6,7},{7,6},{8,9},{9,8},{10,11... | collective-permute-start | bytes 3145736 | tf_op jit(solution)/shard_map/ppermute | solution.py:306
  54.7 16.5 %collective-permute-start.5 = (f32[2,4,32,512]{3,2,1,0:T(8,128)}, f32[2,4,32,512]{3,2,1,0:T(8,128)}, u32[]{:S(2)}, u32[]{:S(2)}) collective-permute-start(f32[2,4,32,512]{3,2,1,0:T(8,128)} %collective-permute-done.2.refs_1_), channel_id=1, source_target_pairs={{0,64},{64,0},{128,192},{192,128},{256,320},{320,256},{384,448},{4... | collective-permute-start | bytes 1572872 | tf_op jit(solution)/shard_map/ppermute | solution.py:293
  57.8 17.5 %collective-permute-start.6 = (f32[2,4,32,512]{3,2,1,0:T(8,128)}, f32[2,4,32,512]{3,2,1,0:T(8,128)}, u32[]{:S(2)}, u32[]{:S(2)}) collective-permute-start(f32[2,4,32,512]{3,2,1,0:T(8,128)} %collective-permute-done.3.refs_2_), channel_id=1, source_target_pairs={{0,448},{64,128},{128,64},{192,256},{256,192},{320,384},{384,320},... | collective-permute-start | bytes 1572872 | tf_op jit(solution)/shard_map/ppermute | solution.py:293
  62.4 1.0 copy-start.2
  63.5 0.9 copy-start.4
  75.3 16.5 %collective-permute-start.9 = (f32[2,4,32,512]{3,2,1,0:T(8,128)}, f32[2,4,32,512]{3,2,1,0:T(8,128)S(1)}, u32[]{:S(2)}, u32[]{:S(2)}) collective-permute-start(f32[2,4,32,512]{3,2,1,0:T(8,128)} %collective-permute-done.5.refs_1_), channel_id=1, source_target_pairs={{0,448},{64,128},{128,64},{192,256},{256,192},{320,384},{384,320},... | collective-permute-start | bytes 1572872 | tf_op jit(solution)/shard_map/ppermute | solution.py:293
  78.4 15.0 %collective-permute-start.10 = (f32[2,4,32,512]{3,2,1,0:T(8,128)}, f32[2,4,32,512]{3,2,1,0:T(8,128)S(1)}, u32[]{:S(2)}, u32[]{:S(2)}) collective-permute-start(f32[2,4,32,512]{3,2,1,0:T(8,128)} %collective-permute-done.6.refs_2_), channel_id=1, source_target_pairs={{0,64},{64,0},{128,192},{192,128},{256,320},{320,256},{384,448},{4... | collective-permute-start | bytes 1572872 | tf_op jit(solution)/shard_map/ppermute | solution.py:293
